TPU v7x, 256 devices: a whole 4x4x8 slice. The times are simulated.
256 devices in a mesh: dp: 16 (over z_lo, y), expert: 16 (over z_hi, x, core).
Axes of the slice: x: 4, y: 4, z: 8 (z_hi: 2, z_lo: 4; z = z_hi * 4 + z_lo), core: 2. Of those that a mesh axis runs over, the one named last changes fastest.
Arguments:
- tokens: float32 [256, 256, 1280], P(('dp', 'expert')), may hold values from -8 to 8
- router: float32 [1280, 16], replicated, may hold values from -1 to 1
- w_in: float32 [16, 1280, 5120], P('expert', None, 'dp'), may hold values from -0.15625 to 0.15625
- w_out: float32 [16, 5120, 1280], P('expert', 'dp'), may hold values from -0.078125 to 0.078125
- cotangent: float32 [256, 256, 1280], P(('dp', 'expert')), may hold values from -6 to 6
Outputs:
- grad_tokens: float32 [256, 256, 1280], P(('dp', 'expert'))
- grad_router: float32 [1280, 16], replicated
- grad_w_in: float32 [16, 1280, 5120], P('expert', None, 'dp')
- grad_w_out: float32 [16, 5120, 1280], P('expert', 'dp')
All inputs are finite; a program needn't handle non-finite values.
Results may differ from a plain program's by a relative error of at most 0.00021.
Values sent between devices are 32-bit elements; how exact they have to be, the bound alone decides.
No kernel may reach another device: no remote copies, remote signals or barrier semaphores. Data moves between devices by JAX's collectives and lax.ppermute only.
A program may use at most 64 MiB of HBM per device.

v0:
```python
import jax
import jax.numpy as jnp
from jax import lax
from jax.sharding import PartitionSpec as P

highest = lax.Precision.HIGHEST


def routing(tokens, router):
    logits = jnp.einsum("ipd,de->ipe", tokens, router, precision=highest)
    return (jax.nn.softmax(logits, axis=1), jax.nn.softmax(logits, axis=2))


def on_device(tokens, router, w_in, w_out, cotangent):
    n_img = tokens.shape[0]
    width = tokens.shape[2]
    n_exp = lax.axis_size("expert")
    e_dev = w_in.shape[0]
    dispatch, combine = routing(tokens, router)
    slot_in = jnp.einsum("ipe,ipd->ied", dispatch, tokens, precision=highest)
    arrived = lax.all_to_all(
        slot_in.reshape(n_img, n_exp, e_dev, width),
        "expert",
        split_axis=1,
        concat_axis=0,
        tiled=True,
    )
    arrived = arrived.reshape(n_exp * n_img, e_dev, width)
    gathered = lax.all_gather(arrived, "dp", axis=0, tiled=True)
    pre_act = jnp.einsum("red,edh->reh", gathered, w_in, precision=highest)
    hidden, gelu_pull = jax.vjp(jax.nn.gelu, pre_act)
    row_block = hidden
    partial_out = lax.psum_scatter(
        jnp.einsum("reh,ehd->red", row_block, w_out, precision=highest),
        "dp",
        scatter_dimension=0,
        tiled=True,
    )
    slot_out = lax.all_to_all(partial_out, "expert", split_axis=0, concat_axis=1, tiled=True)
    d_comb = jnp.einsum("ipd,ied->ipe", cotangent, slot_out, precision=highest)
    d_slot_out = jnp.einsum("ipe,ipd->ied", combine, cotangent, precision=highest)
    d_arrived = lax.all_to_all(
        d_slot_out.reshape(n_img, n_exp, e_dev, width),
        "expert",
        split_axis=1,
        concat_axis=0,
        tiled=True,
    )
    d_arrived = d_arrived.reshape(n_exp * n_img, e_dev, width)
    d_gathered = lax.all_gather(d_arrived, "dp", axis=0, tiled=True)
    d_hidden = jnp.einsum("red,ehd->reh", d_gathered, w_out, precision=highest)
    grad_w_out = jnp.einsum("reh,red->ehd", hidden, d_gathered, precision=highest)
    d_pre = gelu_pull(d_hidden)[0]
    grad_w_in = jnp.einsum("red,reh->edh", gathered, d_pre, precision=highest)
    row_block = d_pre
    partial_grad = lax.psum_scatter(
        jnp.einsum("reh,edh->red", row_block, w_in, precision=highest),
        "dp",
        scatter_dimension=0,
        tiled=True,
    )
    d_slot_in = lax.all_to_all(partial_grad, "expert", split_axis=0, concat_axis=1, tiled=True)
    d_disp = jnp.einsum("ipd,ied->ipe", tokens, d_slot_in, precision=highest)
    d_logits = dispatch * (d_disp - jnp.sum(dispatch * d_disp, axis=1, keepdims=True))
    d_logits = d_logits + combine * (d_comb - jnp.sum(combine * d_comb, axis=2, keepdims=True))
    grad_tokens = jnp.einsum("ipe,ied->ipd", dispatch, d_slot_in, precision=highest)
    grad_tokens = grad_tokens + jnp.einsum("ipe,de->ipd", d_logits, router, precision=highest)
    local_router = jnp.einsum("ipd,ipe->de", tokens, d_logits, precision=highest)
    grad_router = lax.psum(local_router, ("dp", "expert"))
    return (grad_tokens, grad_router, grad_w_in, grad_w_out)


def solution(mesh):
    return jax.shard_map(
        on_device,
        mesh=mesh,
        in_specs=(
            P(("dp", "expert"), None, None),
            P(),
            P("expert", None, "dp"),
            P("expert", "dp", None),
            P(("dp", "expert"), None, None),
        ),
        out_specs=(
            P(("dp", "expert"), None, None),
            P(),
            P("expert", None, "dp"),
            P("expert", "dp", None),
        ),
        check_vma=False,
    )
```

profile of v0, /device:TPU:1, one launch (start us, length us, event | category | flops | bytes accessed | tf_op | source)
XLA Modules:
  0.0 630.1 jit_solution(14719296063107420548)
XLA Ops:
  7.2 0.0 copy-start
  7.2 0.0 copy-start.1
  7.2 0.0 all-gather.7.cloned.1.call-start
  7.2 2.7 fusion.75
  10.0 0.2 fusion.63
  10.1 0.0 copy-done.1
  10.2 0.7 convolution_bitcast_fusion.5
  10.9 0.1 copy.14
  11.0 22.1 %all_to_all.16 = f32[1,16,1,1280]{3,2,0,1:T(1,128)} all-to-all(f32[1,16,1,1280]{3,2,0,1:T(1,128)S(1)} %copy.14), channel_id=1, replica_groups=mesh['dp'=16,'expert'=16] {'expert'}, dimensions={1} | all-to-all | bytes 163840 | tf_op jit(solution)/shard_map/all_to_all | solution.py:21
  33.0 0.0 all-gather.7.cloned.1.call-update
  33.1 0.0 all-gather.5.cloned.1.call-start
  33.1 2.0 convolution_bitcast_fusion.6
  35.1 0.1 copy.13
  35.2 13.4 %all_to_all.17 = f32[1,16,1,1280]{3,2,0,1:T(1,128)} all-to-all(f32[1,16,1,1280]{3,2,0,1:T(1,128)S(1)} %copy.13), channel_id=1, replica_groups=mesh['dp'=16,'expert'=16] {'expert'}, dimensions={1} | all-to-all | bytes 163840 | tf_op jit(solution)/shard_map/all_to_all | solution.py:42
  48.6 0.0 all-gather.5.cloned.1.call-update
  48.6 0.0 reduce-scatter.5.cloned.1.call-start
  48.7 52.6 %all-gather.7.cloned.1.call-done = f32[1,256,1,1280]{3,2,0,1:T(1,128)} async-done(((f32[1,16,1,1280]{3,2,0,1:T(1,128)}), f32[1,256,1,1280]{3,2,0,1:T(1,128)}) %all-gather.7.cloned.1.call-update) | async-done | bytes 1310736 | tf_op jit(solution)/shard_map/all_gather | solution.py:29
  101.3 3.3 fusion.29
  104.6 0.0 copy-done
  104.6 3.4 convolution_bitcast_fusion.2
  108.0 0.0 reduce-scatter.5.cloned.1.call-update
  108.0 0.2 reduce-scatter.3.cloned.1.call-start
  108.2 74.9 %all-gather.5.cloned.1.call-done = f32[1,256,1,1280]{3,2,0,1:T(1,128)} async-done(((f32[1,16,1,1280]{3,2,0,1:T(1,128)}), f32[1,256,1,1280]{3,2,0,1:T(1,128)}) %all-gather.5.cloned.1.call-update) | async-done | bytes 1310736 | tf_op jit(solution)/shard_map/all_gather | solution.py:50
  183.1 0.0 copy-start.2
  183.1 3.0 fusion.46
  186.1 0.0 copy-start.3
  186.2 0.7 copy-done.3
  186.9 0.0 copy-done.2
  186.9 3.4 convolution_bitcast_fusion.3
  190.2 0.0 reduce-scatter.3.cloned.1.call-update
  190.2 4.1 convolution_bitcast_fusion
  194.3 74.9 %reduce-scatter.5.cloned.1.call-done = f32[16,1,1280]{2,0,1:T(8,128)} async-done(((f32[256,1,1280]{2,0,1:T(8,128)}), f32[16,1,1280]{2,0,1:T(8,128)}) %reduce-scatter.5.cloned.1.call-update) | async-done | bytes 81936 | tf_op jit(solution)/shard_map/reduce_scatter | solution.py:33
  269.2 1.6 copy.16
  270.8 18.4 %all-to-all-start.3 = ((f32[16,1,1280]{2,1,0:T(1,128)}), f32[16,1,1280]{2,1,0:T(1,128)S(1)}, u32[]{:S(2)}, u32[]{:S(2)}) async-start(f32[16,1,1280]{2,1,0:T(1,128)} %copy.16), calls=%async_computation.5 | async-start | bytes 163840 | tf_op jit(solution)/shard_map/all_to_all | solution.py:39
  289.2 4.1 convolution_bitcast_fusion.1
  293.3 61.3 %reduce-scatter.3.cloned.1.call-done = f32[16,1,1280]{2,0,1:T(8,128)} async-done(((f32[256,1,1280]{2,0,1:T(8,128)}), f32[16,1,1280]{2,0,1:T(8,128)}) %reduce-scatter.3.cloned.1.call-update) | async-done | bytes 81936 | tf_op jit(solution)/shard_map/reduce_scatter | solution.py:56
  354.5 1.6 copy.15
  356.1 0.0 all-to-all-done.3
  356.1 18.3 %all-to-all-start.2 = ((f32[16,1,1280]{2,1,0:T(1,128)}), f32[16,1,1280]{2,1,0:T(1,128)S(1)}, u32[]{:S(2)}, u32[]{:S(2)}) async-start(f32[16,1,1280]{2,1,0:T(1,128)} %copy.15), calls=%async_computation.3 | async-start | bytes 163840 | tf_op jit(solution)/shard_map/all_to_all | solution.py:62
  374.4 0.3 all-reduce.2.cloned.1.call-start
  374.7 2.4 fusion.37
  377.1 7.0 %all-to-all-done.2 = f32[16,1,1280]{2,1,0:T(1,128)S(1)} async-done(((f32[16,1,1280]{2,1,0:T(1,128)}), f32[16,1,1280]{2,1,0:T(1,128)S(1)}, u32[]{:S(2)}, u32[]{:S(2)}) %all-to-all-start.2) | async-done | bytes 81952 | tf_op jit(solution)/shard_map/all_to_all | solution.py:62
  384.2 1.2 multiply_reduce_fusion.1
  385.4 0.0 copy-start.4
  385.4 1.4 convolution_bitcast_fusion.4
  386.8 0.0 all-reduce.2.cloned.1.call-update
  386.8 1.3 fusion.56
  388.1 0.0 copy-done.4
  388.1 2.4 fusion
  390.5 231.5 %all-reduce.2.cloned.1.call-done = f32[1280,16]{0,1:T(8,128)} async-done(((f32[1280,16]{0,1:T(8,128)}), f32[1280,16]{0,1:T(8,128)}) %all-reduce.2.cloned.1.call-update) | async-done | bytes 81936 | tf_op jit(solution)/shard_map/psum | solution.py:69
  622.0 1.5 copy.58
Async XLA Ops:
  7.2 97.4 %copy-start = (f32[1,320,1280]{2,1,0:T(8,128)S(1)}, f32[1,320,1280]{2,1,0:T(8,128)}, u32[]{:S(2)}) copy-start(f32[1,320,1280]{2,1,0:T(8,128)} %param.8) | copy-start | bytes 4915204
  7.2 3.0 copy-start.1
  7.2 94.1 %all-gather.7.cloned.1.call-start = ((), (), s32[]{:S(2)}) async-start(), calls=%async_computation.10 | async-start | bytes 1392640 | tf_op jit(solution)/shard_map/all_gather | solution.py:29
  33.1 150.0 %all-gather.5.cloned.1.call-start = ((), (), s32[]{:S(2)}) async-start(), calls=%async_computation.9 | async-start | bytes 1392640 | tf_op jit(solution)/shard_map/all_gather | solution.py:50
  48.6 220.5 %reduce-scatter.5.cloned.1.call-start = ((), (), s32[]{:S(2)}) async-start(), calls=%async_computation.7 | async-start | bytes 1392640 | tf_op jit(solution)/shard_map/reduce_scatter | solution.py:33
  108.0 246.5 %reduce-scatter.3.cloned.1.call-start = ((), (), s32[]{:S(2)}) async-start(), calls=%async_computation.6 | async-start | bytes 1392640 | tf_op jit(solution)/shard_map/reduce_scatter | solution.py:56
  183.1 3.8 copy-start.2
  186.1 0.7 copy-start.3
  270.8 85.3 %all-to-all-start.3 = ((f32[16,1,1280]{2,1,0:T(1,128)}), f32[16,1,1280]{2,1,0:T(1,128)S(1)}, u32[]{:S(2)}, u32[]{:S(2)}) async-start(f32[16,1,1280]{2,1,0:T(1,128)} %copy.16), calls=%async_computation.5 | async-start | bytes 163840 | tf_op jit(solution)/shard_map/all_to_all | solution.py:39
  356.1 28.0 %all-to-all-start.2 = ((f32[16,1,1280]{2,1,0:T(1,128)}), f32[16,1,1280]{2,1,0:T(1,128)S(1)}, u32[]{:S(2)}, u32[]{:S(2)}) async-start(f32[16,1,1280]{2,1,0:T(1,128)} %copy.15), calls=%async_computation.3 | async-start | bytes 163840 | tf_op jit(solution)/shard_map/all_to_all | solution.py:62
  374.4 247.6 %all-reduce.2.cloned.1.call-start = ((), (), s32[]{:S(2)}) async-start(), calls=%async_computation.8 | async-start | bytes 163840 | tf_op jit(solution)/shard_map/psum | solution.py:69
  385.4 2.7 copy-start.4
Sparse Core Ops, SparseCore 0:
  33.2 68.0 all-gather.6
  103.0 79.9 all-gather.4
  186.2 82.9 reduce-scatter.4
  272.2 82.3 reduce-scatter.2
  386.9 235.0 all-reduce.1
where the time goes:
time: 631 us; the launch traced here: 630 us
  waiting for transfers between devices  502 us (80%)
  starting transfers between devices  37.3 us (6%)
  blocking collectives  35.5 us (6%)
  matrix products  35.4 us (6%)
  between operations  13.9 us (2%)
    psum x1, waiting for transfers between devices, on_device(): grad_router = lax.psum(local_router, ('dp', 'expert'))  232 us
    reduce_scatter x1, waiting for transfers between devices, on_device(): lax.psum_scatter(jnp.einsum('reh,ehd->red', row_block, w_out, precision=h...  74.9 us
    all_gather x1, waiting for transfers between devices, on_device(): d_gathered = lax.all_gather(d_arrived, 'dp', axis=0, tiled=True)  74.9 us
    reduce_scatter x1, waiting for transfers between devices, on_device(): lax.psum_scatter(jnp.einsum('reh,edh->red', row_block, w_in, precision=hi...  61.3 us
    all_gather x1, waiting for transfers between devices, on_device(): gathered = lax.all_gather(arrived, 'dp', axis=0, tiled=True)  52.6 us
    all_to_all x1, blocking collectives, on_device(): lax.all_to_all(slot_in.reshape(n_img, n_exp, e_dev, width), 'expert', spl...  22.1 us
    all_to_all x1, starting transfers between devices, on_device(): lax.all_to_all(partial_out, 'expert', split_axis=0, concat_axis=1, tiled=...  18.4 us
    all_to_all x1, starting transfers between devices, on_device(): lax.all_to_all(partial_grad, 'expert', split_axis=0, concat_axis=1, tiled...  18.3 us
  transfers between devices with their start and end apart: 7, of which 6 were waited for; matrix products, arithmetic and copies ran while one was open for 5% of the time, Pallas kernels for 0%

commit v1 on v0

v1 whole, which is shorter than its diff:
```python
import jax
import jax.numpy as jnp
from jax import lax
from jax.sharding import Mesh, PartitionSpec as P

highest = lax.Precision.HIGHEST
high = lax.Precision.HIGH

DP = ("zl", "y")
EX = ("zh", "x", "c")
ZEX = ("zl",) + EX
ALL = DP + EX
UP = [(i, (i + 1) % 4) for i in range(4)]
DOWN = [(i, (i - 1) % 4) for i in range(4)]


def gather_y(block):
    half = block.shape[0] // 2
    from_below = lax.ppermute(block, "y", UP)
    from_above = lax.ppermute(block, "y", DOWN)
    far_a = lax.ppermute(from_below[:half], "y", UP)
    far_b = lax.ppermute(from_above[half:], "y", DOWN)
    return jnp.concatenate([block, from_below, from_above, far_a, far_b])


def scatter_y(parts):
    n = parts.shape[0] // 4
    half = n // 2
    own, below, above = parts[:n], parts[n : 2 * n], parts[2 * n : 3 * n]
    far_a, far_b = parts[3 * n : 3 * n + half], parts[3 * n + half :]
    got_a = lax.ppermute(far_a, "y", DOWN)
    got_b = lax.ppermute(far_b, "y", UP)
    to_below = jnp.concatenate([below[:half] + got_a, below[half:]])
    to_above = jnp.concatenate([above[:half], above[half:] + got_b])
    return own + lax.ppermute(to_below, "y", DOWN) + lax.ppermute(to_above, "y", UP)


def sum_all(local):
    e, d = local.shape
    lanes = 128
    n = e * d // lanes
    pieces = jnp.pad(local.reshape(n, 1, lanes), ((0, 256 - n), (0, 0), (0, 0)))
    mine = lax.all_to_all(pieces, ALL, 0, 0, tiled=True)
    total = jnp.sum(mine, axis=0, keepdims=True)
    back = lax.all_to_all(jnp.broadcast_to(total, (256, 1, lanes)), ALL, 0, 0, tiled=True)
    return back[:n].reshape(e, d)


def on_device(tokens, router, w_in, w_out, cotangent):
    tokens, cotangent = tokens[0], cotangent[0]
    w_in, w_out = w_in[0], w_out[0]
    width = tokens.shape[1]
    n_exp = router.shape[1]
    logits = jnp.einsum("pd,de->pe", tokens, router, precision=highest)
    dispatch = jax.nn.softmax(logits, axis=0)
    combine = jax.nn.softmax(logits, axis=1)
    slot_in = jnp.einsum("pe,pd->ed", dispatch, tokens, precision=high)
    d_slot_out = jnp.einsum("pe,pd->ed", combine, cotangent, precision=high)
    both = jnp.concatenate([slot_in, d_slot_out], axis=1)
    sent = jnp.broadcast_to(both[None], (4, n_exp, 2 * width)).reshape(4 * n_exp, 2 * width)
    arrived = lax.all_to_all(sent, ZEX, 0, 0, tiled=True)
    gathered = gather_y(arrived)
    x, dy = gathered[:, :width], gathered[:, width:]
    pre_act = jnp.einsum("rd,dh->rh", x, w_in, precision=high)
    hidden, gelu_pull = jax.vjp(jax.nn.gelu, pre_act)
    d_hidden = jnp.einsum("rd,hd->rh", dy, w_out, precision=high)
    d_pre = gelu_pull(d_hidden)[0]
    part_out = jnp.einsum("rh,hd->rd", hidden, w_out, precision=high)
    part_grad = jnp.einsum("rh,dh->rd", d_pre, w_in, precision=high)
    summed = scatter_y(jnp.concatenate([part_out, part_grad], axis=1))
    grad_w_out = jnp.einsum("rh,rd->hd", hidden, dy, precision=high)
    grad_w_in = jnp.einsum("rd,rh->dh", x, d_pre, precision=high)
    back = lax.all_to_all(summed, ZEX, 0, 0, tiled=True)
    back = jnp.sum(back.reshape(4, n_exp, 2 * width), axis=0)
    slot_out, d_slot_in = back[:, :width], back[:, width:]
    d_comb = jnp.einsum("pd,ed->pe", cotangent, slot_out, precision=high)
    d_disp = jnp.einsum("pd,ed->pe", tokens, d_slot_in, precision=high)
    d_logits = dispatch * (d_disp - jnp.sum(dispatch * d_disp, axis=0, keepdims=True))
    d_logits = d_logits + combine * (d_comb - jnp.sum(combine * d_comb, axis=1, keepdims=True))
    local_router = jnp.einsum("pe,pd->ed", d_logits, tokens, precision=high)
    grad_router = sum_all(local_router).T
    grad_tokens = jnp.einsum("pe,ed->pd", dispatch, d_slot_in, precision=high)
    grad_tokens = grad_tokens + jnp.einsum("pe,de->pd", d_logits, router, precision=high)
    return (grad_tokens[None], grad_router, grad_w_in[None], grad_w_out[None])


def solution(mesh):
    split = Mesh(mesh.devices.reshape(4, 4, 2, 4, 2), ALL)
    return jax.shard_map(
        on_device,
        mesh=split,
        in_specs=(
            P(ALL, None, None),
            P(),
            P(EX, None, DP),
            P(EX, DP, None),
            P(ALL, None, None),
        ),
        out_specs=(
            P(ALL, None, None),
            P(),
            P(EX, None, DP),
            P(EX, DP, None),
        ),
        check_vma=False,
    )
```

time: 631 us -> 184 us (0.29)
  waiting for transfers between devices: 502 us -> 63.6 us
  blocking collectives: 35.5 us -> 65.2 us
  starting transfers between devices: 37.3 us -> 22 us
  matrix products: 35.4 us -> 20.3 us
  between operations: 13.9 us -> 1.08 us
    psum x1 -> x0, waiting for transfers between devices: 232 us -> none  [on_device(): grad_router = lax.psum(local_router, ('dp', 'expert'))]
    reduce_scatter x2 -> x0, waiting for transfers between devices: 136 us -> none  [the longest x1 74.9 us: on_device(): lax.psum_scatter(jnp.einsum('reh,ehd->red', row_block, w_out, precision=h...]
    all_gather x2 -> x0, waiting for transfers between devices: 127 us -> none  [the longest x1 74.9 us: on_device(): d_gathered = lax.all_gather(d_arrived, 'dp', axis=0, tiled=True)]
    ppermute x0 -> x8, waiting for transfers between devices: none -> 46.4 us  [the longest x1 13.7 us: gather_y(): from_above = lax.ppermute(block, 'y', DOWN)]
    all_to_all x2, blocking collectives: 35.5 us -> 65.2 us  [the longest x1 33.3 us: on_device(): arrived = lax.all_to_all(sent, ZEX, 0, 0, tiled=True)]
    all_to_all x2, starting transfers between devices: 36.7 us -> 12.4 us  [the longest x1 6.59 us: sum_all(): lax.all_to_all(jnp.broadcast_to(total, (256, 1, lanes)), ALL, 0, 0, tiled...]
    dot_general x14, matrix products: 35.4 us -> 20.3 us  [the longest x1 3.51 us: on_device(): grad_w_in = jnp.einsum('rd,rh->dh', x, d_pre, precision=high)]
    all_to_all x2, waiting for transfers between devices: 7.04 us -> 17.3 us  [the longest x1 10.1 us: sum_all(): lax.all_to_all(jnp.broadcast_to(total, (256, 1, lanes)), ALL, 0, 0, tiled...]
  transfers between devices with their start and end apart: 7 -> 10, of which waited for: 6 -> 8; matrix products, arithmetic and copies ran while one was open for 5% -> 5% of each run, Pallas kernels for 0% -> 0%
where the time goes in v1:
time: 184 us; the launch traced here: 183 us
  blocking collectives  65.2 us (35%)
  waiting for transfers between devices  63.6 us (35%)
  starting transfers between devices  22 us (12%)
  matrix products  20.3 us (11%)
  local copies, waits for them, and re-layouts  9.04 us (5%)
  other arithmetic  2.04 us (1%)
    all_to_all x1, blocking collectives, on_device(): arrived = lax.all_to_all(sent, ZEX, 0, 0, tiled=True)  33.3 us
    all_to_all x1, blocking collectives, on_device(): back = lax.all_to_all(summed, ZEX, 0, 0, tiled=True)  31.9 us
    ppermute x1, waiting for transfers between devices, gather_y(): from_above = lax.ppermute(block, 'y', DOWN)  13.7 us
    all_to_all x1, waiting for transfers between devices, sum_all(): lax.all_to_all(jnp.broadcast_to(total, (256, 1, lanes)), ALL, 0, 0, tiled...  10.1 us
    ppermute x1, waiting for transfers between devices, gather_y(): far_a = lax.ppermute(from_below[:half], 'y', UP)  8.79 us
    all_to_all x1, waiting for transfers between devices, sum_all(): mine = lax.all_to_all(pieces, ALL, 0, 0, tiled=True)  7.14 us
    ppermute x1, waiting for transfers between devices, scatter_y(): lax.ppermute(to_above, 'y', UP)  7.07 us
    ppermute x1, waiting for transfers between devices, scatter_y(): got_a = lax.ppermute(far_a, 'y', DOWN)  6.66 us
  transfers between devices with their start and end apart: 10, of which 8 were waited for; matrix products, arithmetic and copies ran while one was open for 5% of the time, Pallas kernels for 0%

profile of v1, /device:TPU:1, one launch (start us, length us, event | category | flops | bytes accessed | tf_op | source)
XLA Modules:
  0.0 183.4 jit_solution(4869063969977192463)
XLA Ops:
  0.6 0.0 copy-start
  0.6 0.0 copy-start.1
  0.7 0.0 copy-start.5
  0.7 2.7 %fusion.71 = (f32[16]{0:T(128)S(1)}, f32[256]{0:T(256)S(1)}, f32[256,16]{0,1:T(8,128)S(1)}) fusion(f32[1280,16]{0,1:T(8,128)} %param.6, f32[1,256,1280]{2,1,0:T(8,128)} %param.5), kind=kOutput, calls=%fused_computation.94 | convolution fusion | flops 62922480 | bytes 1410112 | tf_op jit(solution)/shard_map/pd,de->pe/dot_general | solution.py:54
  3.4 0.0 copy-start.14
  3.4 0.2 fusion.57
  3.6 0.5 fusion.17
  4.1 0.4 fusion.11
  4.5 0.9 broadcast_in_dim.10
  5.4 2.7 %all_to_all.20 = f32[64,1,2560]{2,1,0:T(1,128)} reshape(f32[4,16,2560]{2,1,0:T(8,128)} %broadcast_in_dim.10) | data formatting | bytes 1310720 | tf_op jit(solution)/shard_map/all_to_all | solution.py:61
  8.1 33.3 %all_to_all.31 = f32[64,1,2560]{2,1,0:T(1,128)S(1)} all-to-all(f32[64,1,2560]{2,1,0:T(1,128)} %all_to_all.20), channel_id=1, replica_groups=mesh['zl'=4,'y'=4,'zh'=2,'x'=4,'c'=2] {'zl','zh','x','c'}, dimensions={0} | all-to-all | bytes 1310720 | tf_op jit(solution)/shard_map/all_to_all | solution.py:61
  41.5 2.8 %collective-permute-start.1 = (f32[64,2560]{1,0:T(8,128)S(1)}, f32[64,2560]{1,0:T(8,128)S(1)}, u32[]{:S(2)}, u32[]{:S(2)}) collective-permute-start(f32[64,2560]{1,0:T(8,128)S(1)} %bitcast.59), channel_id=1, source_target_pairs={{0,48},{16,0},{32,16},{48,32},{1,49},{17,1},{33,17},{49,33},{2,50}... | collective-permute-start | bytes 1966088 | tf_op jit(solution)/shard_map/ppermute | solution.py:20
  44.3 0.0 collective-permute-start
  44.4 13.7 %collective-permute-done.1 = f32[64,2560]{1,0:T(8,128)S(1)} collective-permute-done((f32[64,2560]{1,0:T(8,128)S(1)}, f32[64,2560]{1,0:T(8,128)S(1)}, u32[]{:S(2)}, u32[]{:S(2)}) %collective-permute-start.1) | collective-permute-done | bytes 655392 | tf_op jit(solution)/shard_map/ppermute | solution.py:20
  58.1 3.5 %collective-permute-start.3 = (f32[32,2560]{1,0:T(8,128)S(1)}, f32[32,2560]{1,0:T(8,128)S(1)}, u32[]{:S(2)}, u32[]{:S(2)}) collective-permute-start(f32[32,2560]{1,0:T(8,128)S(1)} %slice.63), channel_id=1, source_target_pairs={{0,48},{16,0},{32,16},{48,32},{1,49},{17,1},{33,17},{49,33},{2,50}... | collective-permute-start | bytes 983048 | tf_op jit(solution)/shard_map/ppermute | solution.py:22
  61.5 0.0 collective-permute-done
  61.6 0.0 copy-start.4
  61.6 0.1 collective-permute-start.2
  61.8 8.8 %collective-permute-done.2 = f32[32,2560]{1,0:T(8,128)S(1)} collective-permute-done((f32[32,2560]{1,0:T(8,128)S(1)}, f32[32,2560]{1,0:T(8,128)S(1)}, u32[]{:S(2)}, u32[]{:S(2)}) %collective-permute-start.2) | collective-permute-done | bytes 327712 | tf_op jit(solution)/shard_map/ppermute | solution.py:21
  70.6 0.0 collective-permute-done.3
  70.7 0.9 fusion.7
  71.6 0.6 copy-done.2
  72.2 0.0 copy-done
  72.2 1.0 fusion.40
  73.2 0.0 copy-start.6
  73.2 1.3 fusion.3
  74.6 1.4 fusion.5
  76.0 0.4 collective-permute-start.4
  76.3 6.7 %collective-permute-done.4 = f32[32,2560]{1,0:T(8,128)S(1)} collective-permute-done((f32[32,2560]{1,0:T(8,128)S(1)}, f32[32,2560]{1,0:T(8,128)S(1)}, u32[]{:S(2)}, u32[]{:S(2)}) %collective-permute-start.4) | collective-permute-done | bytes 327712 | tf_op jit(solution)/shard_map/ppermute | solution.py:31
  83.0 0.1 fusion.44
  83.1 0.1 collective-permute-start.6
  83.3 2.7 %collective-permute-start.5 = (f32[64,2560]{1,0:T(8,128)S(1)}, f32[64,2560]{1,0:T(8,128)S(1)}, u32[]{:S(2)}, u32[]{:S(2)}) collective-permute-start(f32[64,2560]{1,0:T(8,128)S(1)} %pad_maximum_fusion), channel_id=1, source_target_pairs={{0,48},{16,0},{32,16},{48,32},{1,49},{17,1},{33,17},{49,33},{2,50}... | collective-permute-start | bytes 1966088 | tf_op jit(solution)/shard_map/ppermute | solution.py:35
  86.0 4.3 %collective-permute-done.6 = f32[32,2560]{1,0:T(8,128)S(1)} collective-permute-done((f32[32,2560]{1,0:T(8,128)S(1)}, f32[32,2560]{1,0:T(8,128)S(1)}, u32[]{:S(2)}, u32[]{:S(2)}) %collective-permute-start.6) | collective-permute-done | bytes 327712 | tf_op jit(solution)/shard_map/ppermute | solution.py:32
  90.4 0.1 pad_maximum_fusion.1
  90.5 0.1 collective-permute-start.7
  90.5 5.9 %collective-permute-done.5 = f32[64,2560]{1,0:T(8,128)S(1)} collective-permute-done((f32[64,2560]{1,0:T(8,128)S(1)}, f32[64,2560]{1,0:T(8,128)S(1)}, u32[]{:S(2)}, u32[]{:S(2)}) %collective-permute-start.5) | collective-permute-done | bytes 655392 | tf_op jit(solution)/shard_map/ppermute | solution.py:35
  96.4 7.1 %collective-permute-done.7 = f32[64,2560]{1,0:T(8,128)S(1)} collective-permute-done((f32[64,2560]{1,0:T(8,128)S(1)}, f32[64,2560]{1,0:T(8,128)S(1)}, u32[]{:S(2)}, u32[]{:S(2)}) %collective-permute-start.7) | collective-permute-done | bytes 655392 | tf_op jit(solution)/shard_map/ppermute | solution.py:35
  103.5 0.1 fusion.34
  103.6 0.7 copy.9
  104.3 31.9 %all_to_all.32 = f32[64,1,2560]{2,1,0:T(1,128)S(1)} all-to-all(f32[64,1,2560]{2,1,0:T(1,128)S(1)} %copy.9), channel_id=1, replica_groups=mesh['zl'=4,'y'=4,'zh'=2,'x'=4,'c'=2] {'zl','zh','x','c'}, dimensions={0} | all-to-all | bytes 1310720 | tf_op jit(solution)/shard_map/all_to_all | solution.py:73
  136.2 0.9 copy.12
  137.0 1.1 reduce_sum.56
  138.2 1.9 %fusion.28 = f32[256,16]{0,1:T(8,128)S(1)} fusion(f32[1,256,1280]{2,1,0:T(8,128)} %param.9, f32[16,2560]{1,0:T(8,128)S(1)} %reduce_sum.56), kind=kOutput, calls=%fused_computation.41 | convolution fusion | flops 31457280 | bytes 1409024 | tf_op jit(solution)/shard_map/pd,ed->pe/dot_general | solution.py:76
  140.1 0.1 copy-done.10
  140.2 0.8 multiply_reduce_fusion.1
  141.0 0.0 copy-start.8
  141.0 0.6 copy-done.8
  141.6 1.1 fusion.13
  142.7 0.7 pad.4
  143.5 5.8 %all-to-all-start.2 = ((f32[256,1,128]{2,1,0:T(1,128)}), f32[256,1,128]{2,1,0:T(1,128)S(1)}, u32[]{:S(2)}, u32[]{:S(2)}) async-start(f32[256,1,128]{2,1,0:T(1,128)} %pad.4), calls=%async_computation.2 | async-start | bytes 262144 | tf_op jit(solution)/shard_map/all_to_all | solution.py:43
  149.3 0.0 copy-start.3
  149.3 3.5 %convolution_bitcast_fusion.1 = f32[1,1280,320]{1,2,0:T(8,128)} fusion(f32[256,320]{0,1:T(8,128)} %copy-done.6, f32[256,2560]{1,0:T(8,128)} %copy-done.2), kind=kOutput, calls=%fused_computation.13 | convolution fusion | flops 629145600 | bytes 3276800 | tf_op jit(solution)/shard_map/rd,rh->dh/dot_general | solution.py:72
  152.8 2.1 %convolution_bitcast_fusion = f32[1,320,1280]{2,1,0:T(8,128)} fusion(f32[256,2560]{1,0:T(8,128)S(1)} %copy-done.3, f32[256,320]{0,1:T(8,128)S(1)} %fusion.7), kind=kOutput, calls=%fused_computation.12 | convolution fusion | flops 629800960 | bytes 3276800 | tf_op jit(solution)/shard_map/rh,rd->hd/dot_general | solution.py:71
  154.9 0.0 copy-start.19
  154.9 0.0 copy-start.21
  154.9 7.1 %all-to-all-done.2 = f32[256,1,128]{2,1,0:T(1,128)S(1)} async-done(((f32[256,1,128]{2,1,0:T(1,128)}), f32[256,1,128]{2,1,0:T(1,128)S(1)}, u32[]{:S(2)}, u32[]{:S(2)}) %all-to-all-start.2) | async-done | bytes 131104 | tf_op jit(solution)/shard_map/all_to_all | solution.py:43
  162.1 0.3 reduce_sum.59
  162.3 0.7 broadcast_in_dim.12
  163.0 6.6 %all-to-all-start.3 = ((f32[256,1,128]{2,1,0:T(1,128)}), f32[256,1,128]{2,1,0:T(1,128)S(1)}, u32[]{:S(2)}, u32[]{:S(2)}) async-start(f32[256,1,128]{2,1,0:T(1,128)} %broadcast_in_dim.12), calls=%async_computation.3 | async-start | bytes 262144 | tf_op jit(solution)/shard_map/all_to_all | solution.py:45
  169.7 0.8 fusion.54
  170.5 1.9 %fusion = f32[1,256,1280]{2,1,0:T(8,128)} fusion(f32[256,1280]{1,0:T(8,128)S(1)} %fusion.54, f32[1280,16]{0,1:T(8,128)S(1)} %copy-done.7, f32[256,16]{0,1:T(8,128)S(1)} %fusion.28, f32[256,16]{0,1:T(8,128)S(1)} %copy-done.9, f32[256]{0:T(256)S(1)} %copy-done.19, f32[16]{0:T(128)S(1)} %copy-done.21, f32[256]{0:T(256)S(1)} %copy-done.13, ...), kind=kOutput, calls=%fused_computation.15 | convolution fusion | flops 31821824 | bytes 2755776 | tf_op jit(solution)/shard_map/pe,de->pd/dot_general | solution.py:83
  172.4 10.1 %all-to-all-done.3 = f32[256,1,128]{2,1,0:T(1,128)S(1)} async-done(((f32[256,1,128]{2,1,0:T(1,128)}), f32[256,1,128]{2,1,0:T(1,128)S(1)}, u32[]{:S(2)}, u32[]{:S(2)}) %all-to-all-start.3) | async-done | bytes 131104 | tf_op jit(solution)/shard_map/all_to_all | solution.py:45
  182.5 0.2 slice_reduce_fusion
  182.7 0.7 reshape.38
  (43 shorter events, 0.5 us)
Async XLA Ops:
  0.6 71.5 %copy-start = (f32[1,320,1280]{2,1,0:T(8,128)S(1)}, f32[1,320,1280]{2,1,0:T(8,128)}, u32[]{:S(2)}) copy-start(f32[1,320,1280]{2,1,0:T(8,128)} %param.8) | copy-start | bytes 4915204
  0.6 3.0 %copy-start.1 = (f32[1,256,1280]{2,1,0:T(8,128)S(1)}, f32[1,256,1280]{2,1,0:T(8,128)}, u32[]{:S(2)}) copy-start(f32[1,256,1280]{2,1,0:T(8,128)} %param.5) | copy-start | bytes 3932164
  0.7 3.4 %copy-start.5 = (f32[1,256,1280]{2,1,0:T(8,128)S(1)}, f32[1,256,1280]{2,1,0:T(8,128)}, u32[]{:S(2)}) copy-start(f32[1,256,1280]{2,1,0:T(8,128)} %param.9) | copy-start | bytes 3932164
  3.4 136.8 %copy-start.10 = (f32[256]{0:T(256)}, f32[256]{0:T(256)S(1)}, u32[]{:S(2)}) copy-start(f32[256]{0:T(256)S(1)} %get-tuple-element.9) | copy-start | bytes 3076
  3.4 136.8 %copy-start.14 = (f32[16]{0:T(128)}, f32[16]{0:T(128)S(1)}, u32[]{:S(2)}) copy-start(f32[16]{0:T(128)S(1)} %get-tuple-element.8) | copy-start | bytes 196
  3.6 136.6 %copy-start.12 = (f32[256]{0:T(256)}, f32[256]{0:T(256)S(1)}, u32[]{:S(2)}) copy-start(f32[256]{0:T(256)S(1)} %get-tuple-element.7) | copy-start | bytes 3076
  3.6 136.6 %copy-start.16 = (f32[16]{0:T(128)}, f32[16]{0:T(128)S(1)}, u32[]{:S(2)}) copy-start(f32[16]{0:T(128)S(1)} %get-tuple-element.6) | copy-start | bytes 196
  41.5 16.5 %collective-permute-start.1 = (f32[64,2560]{1,0:T(8,128)S(1)}, f32[64,2560]{1,0:T(8,128)S(1)}, u32[]{:S(2)}, u32[]{:S(2)}) collective-permute-start(f32[64,2560]{1,0:T(8,128)S(1)} %bitcast.59), channel_id=1, source_target_pairs={{0,48},{16,0},{32,16},{48,32},{1,49},{17,1},{33,17},{49,33},{2,50}... | collective-permute-start | bytes 1966088 | tf_op jit(solution)/shard_map/ppermute | solution.py:20
  44.3 17.2 %collective-permute-start = (f32[64,2560]{1,0:T(8,128)S(1)}, f32[64,2560]{1,0:T(8,128)S(1)}, u32[]{:S(2)}, u32[]{:S(2)}) collective-permute-start(f32[64,2560]{1,0:T(8,128)S(1)} %bitcast.60), channel_id=1, source_target_pairs={{0,16},{16,32},{32,48},{48,0},{1,17},{17,33},{33,49},{49,1},{2,18}... | collective-permute-start | bytes 1966088 | tf_op jit(solution)/shard_map/ppermute | solution.py:19
  58.1 12.5 %collective-permute-start.3 = (f32[32,2560]{1,0:T(8,128)S(1)}, f32[32,2560]{1,0:T(8,128)S(1)}, u32[]{:S(2)}, u32[]{:S(2)}) collective-permute-start(f32[32,2560]{1,0:T(8,128)S(1)} %slice.63), channel_id=1, source_target_pairs={{0,48},{16,0},{32,16},{48,32},{1,49},{17,1},{33,17},{49,33},{2,50}... | collective-permute-start | bytes 983048 | tf_op jit(solution)/shard_map/ppermute | solution.py:22
  61.6 9.1 %copy-start.4 = (f32[1,1280,320]{1,2,0:T(8,128)S(1)}, f32[1,1280,320]{1,2,0:T(8,128)}, u32[]{:S(2)}) copy-start(f32[1,1280,320]{1,2,0:T(8,128)} %param.7) | copy-start | bytes 4915204
  61.6 9.0 %collective-permute-start.2 = (f32[32,2560]{1,0:T(8,128)S(1)}, f32[32,2560]{1,0:T(8,128)S(1)}, u32[]{:S(2)}, u32[]{:S(2)}) collective-permute-start(f32[32,2560]{1,0:T(8,128)S(1)} %slice.62), channel_id=1, source_target_pairs={{0,16},{16,32},{32,48},{48,0},{1,17},{17,33},{33,49},{49,1},{2,18}... | collective-permute-start | bytes 983048 | tf_op jit(solution)/shard_map/ppermute | solution.py:21
  70.6 1.5 copy-start.2
  73.2 1.4 copy-start.6
  76.0 7.0 %collective-permute-start.4 = (f32[32,2560]{1,0:T(8,128)S(1)}, f32[32,2560]{1,0:T(8,128)S(1)}, u32[]{:S(2)}, u32[]{:S(2)}) collective-permute-start(f32[32,2560]{1,0:T(8,128)S(1)} %fusion.45), channel_id=1, source_target_pairs={{0,48},{16,0},{32,16},{48,32},{1,49},{17,1},{33,17},{49,33},{2,50}... | collective-permute-start | bytes 983048 | tf_op jit(solution)/shard_map/ppermute | solution.py:31
  83.1 7.2 %collective-permute-start.6 = (f32[32,2560]{1,0:T(8,128)S(1)}, f32[32,2560]{1,0:T(8,128)S(1)}, u32[]{:S(2)}, u32[]{:S(2)}) collective-permute-start(f32[32,2560]{1,0:T(8,128)S(1)} %get-tuple-element.13), channel_id=1, source_target_pairs={{0,16},{16,32},{32,48},{48,0},{1,17},{17,33},{33,49},{49,1},{2,18}... | collective-permute-start | bytes 983048 | tf_op jit(solution)/shard_map/ppermute | solution.py:32
  83.3 13.1 %collective-permute-start.5 = (f32[64,2560]{1,0:T(8,128)S(1)}, f32[64,2560]{1,0:T(8,128)S(1)}, u32[]{:S(2)}, u32[]{:S(2)}) collective-permute-start(f32[64,2560]{1,0:T(8,128)S(1)} %pad_maximum_fusion), channel_id=1, source_target_pairs={{0,48},{16,0},{32,16},{48,32},{1,49},{17,1},{33,17},{49,33},{2,50}... | collective-permute-start | bytes 1966088 | tf_op jit(solution)/shard_map/ppermute | solution.py:35
  90.5 13.0 %collective-permute-start.7 = (f32[64,2560]{1,0:T(8,128)S(1)}, f32[64,2560]{1,0:T(8,128)S(1)}, u32[]{:S(2)}, u32[]{:S(2)}) collective-permute-start(f32[64,2560]{1,0:T(8,128)S(1)} %pad_maximum_fusion.1), channel_id=1, source_target_pairs={{0,16},{16,32},{32,48},{48,0},{1,17},{17,33},{33,49},{49,1},{2,18}... | collective-permute-start | bytes 1966088 | tf_op jit(solution)/shard_map/ppermute | solution.py:35
  141.0 0.6 copy-start.8
  141.0 0.6 copy-start.18
  141.0 0.6 copy-start.20
  143.5 18.6 %all-to-all-start.2 = ((f32[256,1,128]{2,1,0:T(1,128)}), f32[256,1,128]{2,1,0:T(1,128)S(1)}, u32[]{:S(2)}, u32[]{:S(2)}) async-start(f32[256,1,128]{2,1,0:T(1,128)} %pad.4), calls=%async_computation.2 | async-start | bytes 262144 | tf_op jit(solution)/shard_map/all_to_all | solution.py:43
  149.3 3.5 %copy-start.3 = (f32[256,2560]{1,0:T(8,128)S(1)}, f32[256,2560]{1,0:T(8,128)}, u32[]{:S(2)}) copy-start(f32[256,2560]{1,0:T(8,128)} %copy-done.2) | copy-start | bytes 7864324
  152.8 16.9 %copy-start.15 = (f32[16]{0:T(128)S(1)}, f32[16]{0:T(128)}, u32[]{:S(2)}) copy-start(f32[16]{0:T(128)} %copy-done.14) | copy-start | bytes 196
  152.8 16.9 %copy-start.17 = (f32[16]{0:T(128)S(1)}, f32[16]{0:T(128)}, u32[]{:S(2)}) copy-start(f32[16]{0:T(128)} %copy-done.16) | copy-start | bytes 196
  154.9 15.6 %copy-start.7 = (f32[1280,16]{0,1:T(8,128)S(1)}, f32[1280,16]{0,1:T(8,128)}, u32[]{:S(2)}) copy-start(f32[1280,16]{0,1:T(8,128)} %param.6) | copy-start | bytes 245764
  154.9 15.6 %copy-start.9 = (f32[256,16]{0,1:T(8,128)S(1)}, f32[256,16]{0,1:T(8,128)}, u32[]{:S(2)}) copy-start(f32[256,16]{0,1:T(8,128)} %copy-done.8) | copy-start | bytes 49156
  154.9 15.6 %copy-start.11 = (f32[256]{0:T(256)S(1)}, f32[256]{0:T(256)}, u32[]{:S(2)}) copy-start(f32[256]{0:T(256)} %copy-done.10) | copy-start | bytes 3076
  154.9 15.6 %copy-start.13 = (f32[256]{0:T(256)S(1)}, f32[256]{0:T(256)}, u32[]{:S(2)}) copy-start(f32[256]{0:T(256)} %copy-done.12) | copy-start | bytes 3076
  154.9 15.6 %copy-start.19 = (f32[256]{0:T(256)S(1)}, f32[256]{0:T(256)}, u32[]{:S(2)}) copy-start(f32[256]{0:T(256)} %copy-done.18) | copy-start | bytes 3076
  154.9 15.6 %copy-start.21 = (f32[16]{0:T(128)S(1)}, f32[16]{0:T(128)}, u32[]{:S(2)}) copy-start(f32[16]{0:T(128)} %copy-done.20) | copy-start | bytes 196
  163.0 19.5 %all-to-all-start.3 = ((f32[256,1,128]{2,1,0:T(1,128)}), f32[256,1,128]{2,1,0:T(1,128)S(1)}, u32[]{:S(2)}, u32[]{:S(2)}) async-start(f32[256,1,128]{2,1,0:T(1,128)} %broadcast_in_dim.12), calls=%async_computation.3 | async-start | bytes 262144 | tf_op jit(solution)/shard_map/all_to_all | solution.py:45

commit v2 on v1

--- a/solution.py
+++ b/solution.py
@@ -35,15 +35,24 @@
     return own + lax.ppermute(to_below, "y", DOWN) + lax.ppermute(to_above, "y", UP)
 
 
+def sum_axis(block, axis):
+    total = block
+    for k in range(1, 4):
+        total = total + lax.ppermute(block, axis, [(i, (i + k) % 4) for i in range(4)])
+    return total
+
+
 def sum_all(local):
-    e, d = local.shape
-    lanes = 128
-    n = e * d // lanes
-    pieces = jnp.pad(local.reshape(n, 1, lanes), ((0, 256 - n), (0, 0), (0, 0)))
-    mine = lax.all_to_all(pieces, ALL, 0, 0, tiled=True)
-    total = jnp.sum(mine, axis=0, keepdims=True)
-    back = lax.all_to_all(jnp.broadcast_to(total, (256, 1, lanes)), ALL, 0, 0, tiled=True)
-    return back[:n].reshape(e, d)
+    swap = [(0, 1), (1, 0)]
+    first = lax.axis_index("c") == 0
+    half = local.shape[0] // 2
+    low, top = local[:half], local[half:]
+    mine = jnp.where(first, low, top) + lax.ppermute(jnp.where(first, top, low), "c", swap)
+    mine = sum_axis(sum_axis(mine, "x"), "y")
+    pieces = jnp.broadcast_to(mine[None], (8,) + mine.shape)
+    mine = jnp.sum(lax.all_to_all(pieces, ("zl", "zh"), 0, 0, tiled=True), axis=0)
+    other = lax.ppermute(mine, "c", swap)
+    return jnp.where(first, jnp.concatenate([mine, other]), jnp.concatenate([other, mine]))
 
 
 def on_device(tokens, router, w_in, w_out, cotangent):
@@ -59,15 +68,15 @@
     both = jnp.concatenate([slot_in, d_slot_out], axis=1)
     sent = jnp.broadcast_to(both[None], (4, n_exp, 2 * width)).reshape(4 * n_exp, 2 * width)
     arrived = lax.all_to_all(sent, ZEX, 0, 0, tiled=True)
-    gathered = gather_y(arrived)
-    x, dy = gathered[:, :width], gathered[:, width:]
+    x = gather_y(arrived[:, :width])
+    dy = gather_y(arrived[:, width:])
     pre_act = jnp.einsum("rd,dh->rh", x, w_in, precision=high)
     hidden, gelu_pull = jax.vjp(jax.nn.gelu, pre_act)
     d_hidden = jnp.einsum("rd,hd->rh", dy, w_out, precision=high)
     d_pre = gelu_pull(d_hidden)[0]
     part_out = jnp.einsum("rh,hd->rd", hidden, w_out, precision=high)
     part_grad = jnp.einsum("rh,dh->rd", d_pre, w_in, precision=high)
-    summed = scatter_y(jnp.concatenate([part_out, part_grad], axis=1))
+    summed = jnp.concatenate([scatter_y(part_out), scatter_y(part_grad)], axis=1)
     grad_w_out = jnp.einsum("rh,rd->hd", hidden, dy, precision=high)
     grad_w_in = jnp.einsum("rd,rh->dh", x, d_pre, precision=high)
     back = lax.all_to_all(summed, ZEX, 0, 0, tiled=True)

time: 184 us -> 168 us (0.913)
  blocking collectives: 65.2 us -> 33.3 us
  starting transfers between devices: 22 us -> 43.3 us
  waiting for transfers between devices: 63.6 us -> 57.7 us
    all_to_all x1 -> x0, blocking collectives: 31.9 us -> none  [on_device(): back = lax.all_to_all(summed, ZEX, 0, 0, tiled=True)]
    ppermute x1 -> x2, waiting for transfers between devices: 13.7 us -> 0.01 us  [gather_y(): from_above = lax.ppermute(block, 'y', DOWN)]
    ppermute x0 -> x8, starting transfers between devices: none -> 11.3 us  [the longest x6 5.75 us: sum_axis(): lax.ppermute(block, axis, [(i, (i + k) % 4) for i in range(4)])]
    ppermute x1 -> x2, waiting for transfers between devices: 0.01 us -> 8.89 us  [gather_y(): from_below = lax.ppermute(block, 'y', UP)]
    ppermute x1 -> x2, waiting for transfers between devices: 8.79 us -> 0.33 us  [gather_y(): far_a = lax.ppermute(from_below[:half], 'y', UP)]
    ppermute x0 -> x8, waiting for transfers between devices: none -> 5.72 us  [the longest x6 4.85 us: sum_axis(): lax.ppermute(block, axis, [(i, (i + k) % 4) for i in range(4)])]
    ppermute x1 -> x2, waiting for transfers between devices: 5.87 us -> 0.35 us  [scatter_y(): lax.ppermute(to_below, 'y', DOWN)]
    ppermute x1 -> x2, waiting for transfers between devices: 7.07 us -> 11.8 us  [scatter_y(): lax.ppermute(to_above, 'y', UP)]
  transfers between devices with their start and end apart: 10 -> 26, of which waited for: 8 -> 18; matrix products, arithmetic and copies ran while one was open for 5% -> 8% of each run, Pallas kernels for 0% -> 0%
where the time goes in v2:
time: 168 us; the launch traced here: 167 us
  waiting for transfers between devices  57.7 us (34%)
  starting transfers between devices  43.3 us (26%)
  blocking collectives  33.3 us (20%)
  matrix products  19.3 us (11%)
  local copies, waits for them, and re-layouts  9.32 us (6%)
  other arithmetic  3.47 us (2%)
    all_to_all x1, blocking collectives, on_device(): arrived = lax.all_to_all(sent, ZEX, 0, 0, tiled=True)  33.3 us
    all_to_all x1, waiting for transfers between devices, on_device(): back = lax.all_to_all(summed, ZEX, 0, 0, tiled=True)  20.3 us
    ppermute x2, waiting for transfers between devices, scatter_y(): lax.ppermute(to_above, 'y', UP)  11.8 us
    all_to_all x1, starting transfers between devices, on_device(): back = lax.all_to_all(summed, ZEX, 0, 0, tiled=True)  10.3 us
    ppermute x2, waiting for transfers between devices, gather_y(): from_below = lax.ppermute(block, 'y', UP)  8.89 us
    ppermute x2, waiting for transfers between devices, scatter_y(): got_b = lax.ppermute(far_b, 'y', UP)  6.47 us
    ppermute x6, starting transfers between devices, sum_axis(): lax.ppermute(block, axis, [(i, (i + k) % 4) for i in range(4)])  5.75 us
    ppermute x2, starting transfers between devices, gather_y(): far_b = lax.ppermute(from_above[half:], 'y', DOWN)  5.64 us
  transfers between devices with their start and end apart: 26, of which 18 were waited for; matrix products, arithmetic and copies ran while one was open for 8% of the time, Pallas kernels for 0%

profile of v2, /device:TPU:1, one launch (start us, length us, event | category | flops | bytes accessed | tf_op | source)
XLA Modules:
  0.0 167.5 jit_solution(5446211535619940214)
XLA Ops:
  0.7 2.7 %fusion.57 = (f32[16]{0:T(128)S(1)}, f32[256]{0:T(256)S(1)}, f32[256,16]{0,1:T(8,128)S(1)}) fusion(f32[1280,16]{0,1:T(8,128)} %param.6, f32[1,256,1280]{2,1,0:T(8,128)} %param.5), kind=kOutput, calls=%fused_computation.87 | convolution fusion | flops 62922480 | bytes 1410112 | tf_op jit(solution)/shard_map/pd,de->pe/dot_general | solution.py:63
  3.4 0.2 fusion.43
  3.6 0.5 fusion.17
  4.1 0.4 fusion.11
  4.5 0.9 broadcast_in_dim.10
  5.4 2.7 %all_to_all.17 = f32[64,1,2560]{2,1,0:T(1,128)} reshape(f32[4,16,2560]{2,1,0:T(8,128)} %broadcast_in_dim.10) | data formatting | bytes 1310720 | tf_op jit(solution)/shard_map/all_to_all | solution.py:70
  8.1 33.3 %all_to_all.26 = f32[64,1,2560]{2,1,0:T(1,128)S(1)} all-to-all(f32[64,1,2560]{2,1,0:T(1,128)} %all_to_all.17), channel_id=1, replica_groups=mesh['zl'=4,'y'=4,'zh'=2,'x'=4,'c'=2] {'zl','zh','x','c'}, dimensions={0} | all-to-all | bytes 1310720 | tf_op jit(solution)/shard_map/all_to_all | solution.py:70
  41.5 0.1 fusion.58
  41.6 1.4 collective-permute-start
  42.9 1.5 collective-permute-start.1
  44.5 2.7 %collective-permute-start.9 = (f32[64,1280]{1,0:T(8,128)S(1)}, f32[64,1280]{1,0:T(8,128)S(1)}, u32[]{:S(2)}, u32[]{:S(2)}) collective-permute-start(f32[64,1280]{1,0:T(8,128)S(1)} %get-tuple-element.18), channel_id=1, source_target_pairs={{0,48},{16,0},{32,16},{48,32},{1,49},{17,1},{33,17},{49,33},{2,50}... | collective-permute-start | bytes 983048 | tf_op jit(solution)/shard_map/ppermute | solution.py:20
  47.1 4.7 %collective-permute-done = f32[64,1280]{1,0:T(8,128)S(1)} collective-permute-done((f32[64,1280]{1,0:T(8,128)S(1)}, f32[64,1280]{1,0:T(8,128)S(1)}, u32[]{:S(2)}, u32[]{:S(2)}) %collective-permute-start) | collective-permute-done | bytes 327712 | tf_op jit(solution)/shard_map/ppermute | solution.py:19
  52.0 2.7 %collective-permute-start.3 = (f32[32,1280]{1,0:T(8,128)S(1)}, f32[32,1280]{1,0:T(8,128)S(1)}, u32[]{:S(2)}, u32[]{:S(2)}) collective-permute-start(f32[32,1280]{1,0:T(8,128)S(1)} %slice.110), channel_id=1, source_target_pairs={{0,48},{16,0},{32,16},{48,32},{1,49},{17,1},{33,17},{49,33},{2,50}... | collective-permute-start | bytes 491528 | tf_op jit(solution)/shard_map/ppermute | solution.py:22
  54.8 4.2 %collective-permute-done.8 = f32[64,1280]{1,0:T(8,128)S(1)} collective-permute-done((f32[64,1280]{1,0:T(8,128)S(1)}, f32[64,1280]{1,0:T(8,128)S(1)}, u32[]{:S(2)}, u32[]{:S(2)}) %collective-permute-start.8) | collective-permute-done | bytes 327712 | tf_op jit(solution)/shard_map/ppermute | solution.py:19
  59.0 2.9 %collective-permute-start.11 = (f32[32,1280]{1,0:T(8,128)S(1)}, f32[32,1280]{1,0:T(8,128)S(1)}, u32[]{:S(2)}, u32[]{:S(2)}) collective-permute-start(f32[32,1280]{1,0:T(8,128)S(1)} %slice.120), channel_id=1, source_target_pairs={{0,48},{16,0},{32,16},{48,32},{1,49},{17,1},{33,17},{49,33},{2,50}... | collective-permute-start | bytes 491528 | tf_op jit(solution)/shard_map/ppermute | solution.py:22
  62.1 0.3 collective-permute-done.2
  62.5 0.9 copy-done.6
  63.4 0.9 fusion.7
  64.3 0.1 copy-done.4
  64.5 1.3 fusion.3
  65.8 1.7 collective-permute-start.4
  67.6 1.0 fusion.32
  68.6 1.4 fusion.5
  70.0 0.1 collective-permute-start.12
  70.2 2.8 %collective-permute-start.5 = (f32[64,1280]{1,0:T(8,128)S(1)}, f32[64,1280]{1,0:T(8,128)S(1)}, u32[]{:S(2)}, u32[]{:S(2)}) collective-permute-start(f32[64,1280]{1,0:T(8,128)S(1)} %pad_maximum_fusion), channel_id=1, source_target_pairs={{0,48},{16,0},{32,16},{48,32},{1,49},{17,1},{33,17},{49,33},{2,50}... | collective-permute-start | bytes 983048 | tf_op jit(solution)/shard_map/ppermute | solution.py:35
  73.0 2.1 %collective-permute-done.12 = f32[32,1280]{1,0:T(8,128)S(1)} collective-permute-done((f32[32,1280]{1,0:T(8,128)S(1)}, f32[32,1280]{1,0:T(8,128)S(1)}, u32[]{:S(2)}, u32[]{:S(2)}) %collective-permute-start.12) | collective-permute-done | bytes 163872 | tf_op jit(solution)/shard_map/ppermute | solution.py:31
  75.3 1.4 collective-permute-start.13
  76.6 0.2 collective-permute-start.14
  76.8 1.6 collective-permute-done.6
  78.6 4.9 %collective-permute-done.14 = f32[32,1280]{1,0:T(8,128)S(1)} collective-permute-done((f32[32,1280]{1,0:T(8,128)S(1)}, f32[32,1280]{1,0:T(8,128)S(1)}, u32[]{:S(2)}, u32[]{:S(2)}) %collective-permute-start.14) | collective-permute-done | bytes 163872 | tf_op jit(solution)/shard_map/ppermute | solution.py:32
  83.6 5.2 %collective-permute-done.7 = f32[64,1280]{1,0:T(8,128)S(1)} collective-permute-done((f32[64,1280]{1,0:T(8,128)S(1)}, f32[64,1280]{1,0:T(8,128)S(1)}, u32[]{:S(2)}, u32[]{:S(2)}) %collective-permute-start.7) | collective-permute-done | bytes 327712 | tf_op jit(solution)/shard_map/ppermute | solution.py:35
  88.9 0.3 collective-permute-done.13
  89.2 6.6 %collective-permute-done.15 = f32[64,1280]{1,0:T(8,128)S(1)} collective-permute-done((f32[64,1280]{1,0:T(8,128)S(1)}, f32[64,1280]{1,0:T(8,128)S(1)}, u32[]{:S(2)}, u32[]{:S(2)}) %collective-permute-start.15) | collective-permute-done | bytes 327712 | tf_op jit(solution)/shard_map/ppermute | solution.py:35
  95.9 1.5 copy.10
  97.5 10.3 %all-to-all-start.1 = ((f32[64,1,2560]{2,1,0:T(1,128)}), f32[64,1,2560]{2,1,0:T(1,128)}, u32[]{:S(2)}, u32[]{:S(2)}) async-start(f32[64,1,2560]{2,1,0:T(1,128)} %copy.10), calls=%async_computation.1 | async-start | bytes 1310720 | tf_op jit(solution)/shard_map/all_to_all | solution.py:82
  107.8 20.3 %all-to-all-done.1 = f32[64,1,2560]{2,1,0:T(1,128)} async-done(((f32[64,1,2560]{2,1,0:T(1,128)}), f32[64,1,2560]{2,1,0:T(1,128)}, u32[]{:S(2)}, u32[]{:S(2)}) %all-to-all-start.1) | async-done | bytes 655392 | tf_op jit(solution)/shard_map/all_to_all | solution.py:82
  128.1 2.0 %copy.12 = f32[64,1,2560]{2,0,1:T(8,128)} copy(f32[64,1,2560]{2,1,0:T(1,128)} %all-to-all-done.1) | data formatting | bytes 1310720
  130.0 1.1 reduce_sum.56
  131.2 1.9 %fusion.24 = f32[256,16]{0,1:T(8,128)S(1)} fusion(f32[1,256,1280]{2,1,0:T(8,128)} %param.9, f32[16,2560]{1,0:T(8,128)S(1)} %reduce_sum.56), kind=kOutput, calls=%fused_computation.25 | convolution fusion | flops 31457280 | bytes 1409024 | tf_op jit(solution)/shard_map/pd,ed->pe/dot_general | solution.py:85
  133.1 0.8 multiply_reduce_fusion.1
  133.9 0.5 fusion.13
  134.4 0.5 collective-permute-start.16
  134.9 0.9 collective-permute-done.16
  135.8 0.5 collective-permute-start.17
  136.3 1.7 %collective-permute-start.18 = (f32[8,1280]{1,0:T(8,128)S(1)}, f32[8,1280]{1,0:T(8,128)S(1)}, u32[]{:S(2)}, u32[]{:S(2)}) collective-permute-start(f32[8,1280]{1,0:T(8,128)S(1)} %select_add_fusion), channel_id=1, source_target_pairs={{0,4},{2,6},{4,0},{6,2},{1,5},{3,7},{5,1},{7,3},{8,12},{10,14},{12... | collective-permute-start | bytes 122888 | tf_op jit(solution)/shard_map/ppermute | solution.py:41
  138.0 0.8 collective-permute-start.19
  138.8 1.1 collective-permute-done.17
  139.9 0.7 collective-permute-done.18
  140.6 0.6 collective-permute-done.19
  141.3 0.4 collective-permute-start.21
  141.8 2.2 %collective-permute-start.22 = (f32[8,1280]{1,0:T(8,128)S(1)}, f32[8,1280]{1,0:T(8,128)S(1)}, u32[]{:S(2)}, u32[]{:S(2)}) collective-permute-start(f32[8,1280]{1,0:T(8,128)S(1)} %add_add_fusion.1), channel_id=1, source_target_pairs={{0,48},{16,0},{32,16},{48,32},{1,49},{17,1},{33,17},{49,33},{2,50}... | collective-permute-start | bytes 122888 | tf_op jit(solution)/shard_map/ppermute | solution.py:41
  144.0 1.4 collective-permute-done.20
  145.4 0.4 collective-permute-done.21
  145.8 0.6 collective-permute-done.22
  146.4 0.7 broadcast_in_dim.12
  147.2 4.1 %all-to-all-start.2 = ((f32[8,8,1280]{2,1,0:T(8,128)}), f32[8,8,1280]{2,1,0:T(8,128)}, u32[]{:S(2)}, u32[]{:S(2)}) async-start(f32[8,8,1280]{2,1,0:T(8,128)} %broadcast_in_dim.12), calls=%async_computation.2 | async-start | bytes 655360 | tf_op jit(solution)/shard_map/all_to_all | solution.py:53
  151.3 3.1 %convolution_bitcast_fusion.1 = f32[1,1280,320]{1,2,0:T(8,128)} fusion(f32[256,1280]{1,0:T(8,128)S(1)} %copy-done.5, f32[256,320]{0,1:T(8,128)} %copy-done.8), kind=kOutput, calls=%fused_computation.1 | convolution fusion | flops 629145600 | bytes 3276800 | tf_op jit(solution)/shard_map/rd,rh->dh/dot_general | solution.py:81
  154.3 2.1 %convolution_bitcast_fusion = f32[1,320,1280]{2,1,0:T(8,128)} fusion(f32[256,1280]{1,0:T(8,128)S(1)} %copy-done.3, f32[256,320]{0,1:T(8,128)S(1)} %fusion.7), kind=kOutput, calls=%fused_computation | convolution fusion | flops 629800960 | bytes 3276800 | tf_op jit(solution)/shard_map/rh,rd->hd/dot_general | solution.py:80
  156.4 0.8 fusion.40
  157.2 1.7 %all-to-all-done.2 = f32[8,8,1280]{2,1,0:T(8,128)} async-done(((f32[8,8,1280]{2,1,0:T(8,128)}), f32[8,8,1280]{2,1,0:T(8,128)}, u32[]{:S(2)}, u32[]{:S(2)}) %all-to-all-start.2) | async-done | bytes 327712 | tf_op jit(solution)/shard_map/all_to_all | solution.py:53
  158.9 1.0 reduce_sum.59
  159.9 5.0 %collective-permute-start.23 = (f32[8,1280]{1,0:T(8,128)S(1)}, f32[8,1280]{1,0:T(8,128)S(1)}, u32[]{:S(2)}, u32[]{:S(2)}) collective-permute-start(f32[8,1280]{1,0:T(8,128)S(1)} %reduce_sum.59), channel_id=1, source_target_pairs={{0,1},{1,0},{2,3},{3,2},{4,5},{5,4},{6,7},{7,6},{8,9},{9,8},{10,11... | collective-permute-start | bytes 122888 | tf_op jit(solution)/shard_map/ppermute | solution.py:54
  165.0 1.9 %fusion = f32[1,256,1280]{2,1,0:T(8,128)} fusion(f32[256,1280]{1,0:T(8,128)S(1)} %fusion.40, f32[1280,16]{0,1:T(8,128)S(1)} %copy-done.9, f32[256,16]{0,1:T(8,128)S(1)} %fusion.24, f32[256,16]{0,1:T(8,128)S(1)} %get-tuple-element.23, f32[256]{0:T(256)S(1)} %get-tuple-element.5, f32[16]{0:T(128)S(1)} %get-tuple-element.4, f32[256]{0:T(256)S(1)} %get-tuple-element.7, ...), kind=kOutput, calls=%fused_computation.3 | convolution fusion | flops 31821824 | bytes 2755776 | tf_op jit(solution)/shard_map/pe,de->pd/dot_general | solution.py:92
  166.8 0.6 fusion.38
  (64 shorter events, 1.3 us)
Async XLA Ops:
  0.6 63.8 %copy-start = (f32[1,320,1280]{2,1,0:T(8,128)S(1)}, f32[1,320,1280]{2,1,0:T(8,128)}, u32[]{:S(2)}) copy-start(f32[1,320,1280]{2,1,0:T(8,128)} %param.8) | copy-start | bytes 4915204
  0.6 2.9 %copy-start.1 = (f32[1,256,1280]{2,1,0:T(8,128)S(1)}, f32[1,256,1280]{2,1,0:T(8,128)}, u32[]{:S(2)}) copy-start(f32[1,256,1280]{2,1,0:T(8,128)} %param.5) | copy-start | bytes 3932164
  0.7 3.4 %copy-start.7 = (f32[1,256,1280]{2,1,0:T(8,128)S(1)}, f32[1,256,1280]{2,1,0:T(8,128)}, u32[]{:S(2)}) copy-start(f32[1,256,1280]{2,1,0:T(8,128)} %param.9) | copy-start | bytes 3932164
  41.6 10.3 %collective-permute-start = (f32[64,1280]{1,0:T(8,128)S(1)}, f32[64,1280]{1,0:T(8,128)S(1)}, u32[]{:S(2)}, u32[]{:S(2)}) collective-permute-start(f32[64,1280]{1,0:T(8,128)S(1)} %get-tuple-element.21), channel_id=1, source_target_pairs={{0,16},{16,32},{32,48},{48,0},{1,17},{17,33},{33,49},{49,1},{2,18}... | collective-permute-start | bytes 983048 | tf_op jit(solution)/shard_map/ppermute | solution.py:19
  42.9 9.1 %collective-permute-start.1 = (f32[64,1280]{1,0:T(8,128)S(1)}, f32[64,1280]{1,0:T(8,128)S(1)}, u32[]{:S(2)}, u32[]{:S(2)}) collective-permute-start(f32[64,1280]{1,0:T(8,128)S(1)} %get-tuple-element.21), channel_id=1, source_target_pairs={{0,48},{16,0},{32,16},{48,32},{1,49},{17,1},{33,17},{49,33},{2,50}... | collective-permute-start | bytes 983048 | tf_op jit(solution)/shard_map/ppermute | solution.py:20
  44.5 14.4 %collective-permute-start.8 = (f32[64,1280]{1,0:T(8,128)S(1)}, f32[64,1280]{1,0:T(8,128)S(1)}, u32[]{:S(2)}, u32[]{:S(2)}) collective-permute-start(f32[64,1280]{1,0:T(8,128)S(1)} %get-tuple-element.18), channel_id=1, source_target_pairs={{0,16},{16,32},{32,48},{48,0},{1,17},{17,33},{33,49},{49,1},{2,18}... | collective-permute-start | bytes 983048 | tf_op jit(solution)/shard_map/ppermute | solution.py:19
  44.5 14.5 %collective-permute-start.9 = (f32[64,1280]{1,0:T(8,128)S(1)}, f32[64,1280]{1,0:T(8,128)S(1)}, u32[]{:S(2)}, u32[]{:S(2)}) collective-permute-start(f32[64,1280]{1,0:T(8,128)S(1)} %get-tuple-element.18), channel_id=1, source_target_pairs={{0,48},{16,0},{32,16},{48,32},{1,49},{17,1},{33,17},{49,33},{2,50}... | collective-permute-start | bytes 983048 | tf_op jit(solution)/shard_map/ppermute | solution.py:20
  51.9 10.5 %collective-permute-start.2 = (f32[32,1280]{1,0:T(8,128)S(1)}, f32[32,1280]{1,0:T(8,128)S(1)}, u32[]{:S(2)}, u32[]{:S(2)}) collective-permute-start(f32[32,1280]{1,0:T(8,128)S(1)} %slice.109), channel_id=1, source_target_pairs={{0,16},{16,32},{32,48},{48,0},{1,17},{17,33},{33,49},{49,1},{2,18}... | collective-permute-start | bytes 491528 | tf_op jit(solution)/shard_map/ppermute | solution.py:21
  52.0 10.4 %collective-permute-start.3 = (f32[32,1280]{1,0:T(8,128)S(1)}, f32[32,1280]{1,0:T(8,128)S(1)}, u32[]{:S(2)}, u32[]{:S(2)}) collective-permute-start(f32[32,1280]{1,0:T(8,128)S(1)} %slice.110), channel_id=1, source_target_pairs={{0,48},{16,0},{32,16},{48,32},{1,49},{17,1},{33,17},{49,33},{2,50}... | collective-permute-start | bytes 491528 | tf_op jit(solution)/shard_map/ppermute | solution.py:22
  58.9 8.6 %collective-permute-start.10 = (f32[32,1280]{1,0:T(8,128)S(1)}, f32[32,1280]{1,0:T(8,128)S(1)}, u32[]{:S(2)}, u32[]{:S(2)}) collective-permute-start(f32[32,1280]{1,0:T(8,128)S(1)} %slice.119), channel_id=1, source_target_pairs={{0,16},{16,32},{32,48},{48,0},{1,17},{17,33},{33,49},{49,1},{2,18}... | collective-permute-start | bytes 491528 | tf_op jit(solution)/shard_map/ppermute | solution.py:21
  59.0 8.5 %collective-permute-start.11 = (f32[32,1280]{1,0:T(8,128)S(1)}, f32[32,1280]{1,0:T(8,128)S(1)}, u32[]{:S(2)}, u32[]{:S(2)}) collective-permute-start(f32[32,1280]{1,0:T(8,128)S(1)} %slice.120), channel_id=1, source_target_pairs={{0,48},{16,0},{32,16},{48,32},{1,49},{17,1},{33,17},{49,33},{2,50}... | collective-permute-start | bytes 491528 | tf_op jit(solution)/shard_map/ppermute | solution.py:22
  62.0 1.4 copy-start.6
  63.4 1.1 copy-start.4
  65.8 4.3 %collective-permute-start.4 = (f32[32,1280]{1,0:T(8,128)S(1)}, f32[32,1280]{1,0:T(8,128)S(1)}, u32[]{:S(2)}, u32[]{:S(2)}) collective-permute-start(f32[32,1280]{1,0:T(8,128)S(1)} %slice.113), channel_id=1, source_target_pairs={{0,48},{16,0},{32,16},{48,32},{1,49},{17,1},{33,17},{49,33},{2,50}... | collective-permute-start | bytes 491528 | tf_op jit(solution)/shard_map/ppermute | solution.py:31
  67.5 1.1 copy-start.2
  68.6 1.4 copy-start.8
  70.0 5.2 %collective-permute-start.12 = (f32[32,1280]{1,0:T(8,128)S(1)}, f32[32,1280]{1,0:T(8,128)S(1)}, u32[]{:S(2)}, u32[]{:S(2)}) collective-permute-start(f32[32,1280]{1,0:T(8,128)S(1)} %slice.123), channel_id=1, source_target_pairs={{0,48},{16,0},{32,16},{48,32},{1,49},{17,1},{33,17},{49,33},{2,50}... | collective-permute-start | bytes 491528 | tf_op jit(solution)/shard_map/ppermute | solution.py:31
  70.2 13.4 %collective-permute-start.5 = (f32[64,1280]{1,0:T(8,128)S(1)}, f32[64,1280]{1,0:T(8,128)S(1)}, u32[]{:S(2)}, u32[]{:S(2)}) collective-permute-start(f32[64,1280]{1,0:T(8,128)S(1)} %pad_maximum_fusion), channel_id=1, source_target_pairs={{0,48},{16,0},{32,16},{48,32},{1,49},{17,1},{33,17},{49,33},{2,50}... | collective-permute-start | bytes 983048 | tf_op jit(solution)/shard_map/ppermute | solution.py:35
  73.0 5.4 %collective-permute-start.6 = (f32[32,1280]{1,0:T(8,128)S(1)}, f32[32,1280]{1,0:T(8,128)S(1)}, u32[]{:S(2)}, u32[]{:S(2)}) collective-permute-start(f32[32,1280]{1,0:T(8,128)S(1)} %get-tuple-element.11), channel_id=1, source_target_pairs={{0,16},{16,32},{32,48},{48,0},{1,17},{17,33},{33,49},{49,1},{2,18}... | collective-permute-start | bytes 491528 | tf_op jit(solution)/shard_map/ppermute | solution.py:32
  75.3 14.0 %collective-permute-start.13 = (f32[64,1280]{1,0:T(8,128)S(1)}, f32[64,1280]{1,0:T(8,128)S(1)}, u32[]{:S(2)}, u32[]{:S(2)}) collective-permute-start(f32[64,1280]{1,0:T(8,128)S(1)} %pad_maximum_fusion.2), channel_id=1, source_target_pairs={{0,48},{16,0},{32,16},{48,32},{1,49},{17,1},{33,17},{49,33},{2,50}... | collective-permute-start | bytes 983048 | tf_op jit(solution)/shard_map/ppermute | solution.py:35
  76.6 6.8 %collective-permute-start.14 = (f32[32,1280]{1,0:T(8,128)S(1)}, f32[32,1280]{1,0:T(8,128)S(1)}, u32[]{:S(2)}, u32[]{:S(2)}) collective-permute-start(f32[32,1280]{1,0:T(8,128)S(1)} %get-tuple-element.15), channel_id=1, source_target_pairs={{0,16},{16,32},{32,48},{48,0},{1,17},{17,33},{33,49},{49,1},{2,18}... | collective-permute-start | bytes 491528 | tf_op jit(solution)/shard_map/ppermute | solution.py:32
  78.5 10.3 %collective-permute-start.7 = (f32[64,1280]{1,0:T(8,128)S(1)}, f32[64,1280]{1,0:T(8,128)S(1)}, u32[]{:S(2)}, u32[]{:S(2)}) collective-permute-start(f32[64,1280]{1,0:T(8,128)S(1)} %pad_maximum_fusion.1), channel_id=1, source_target_pairs={{0,16},{16,32},{32,48},{48,0},{1,17},{17,33},{33,49},{49,1},{2,18}... | collective-permute-start | bytes 983048 | tf_op jit(solution)/shard_map/ppermute | solution.py:35
  83.5 12.3 %collective-permute-start.15 = (f32[64,1280]{1,0:T(8,128)S(1)}, f32[64,1280]{1,0:T(8,128)S(1)}, u32[]{:S(2)}, u32[]{:S(2)}) collective-permute-start(f32[64,1280]{1,0:T(8,128)S(1)} %pad_maximum_fusion.3), channel_id=1, source_target_pairs={{0,16},{16,32},{32,48},{48,0},{1,17},{17,33},{33,49},{49,1},{2,18}... | collective-permute-start | bytes 983048 | tf_op jit(solution)/shard_map/ppermute | solution.py:35
  97.5 30.6 %all-to-all-start.1 = ((f32[64,1,2560]{2,1,0:T(1,128)}), f32[64,1,2560]{2,1,0:T(1,128)}, u32[]{:S(2)}, u32[]{:S(2)}) async-start(f32[64,1,2560]{2,1,0:T(1,128)} %copy.10), calls=%async_computation.1 | async-start | bytes 1310720 | tf_op jit(solution)/shard_map/all_to_all | solution.py:82
  134.4 16.8 %copy-start.5 = (f32[256,1280]{1,0:T(8,128)S(1)}, f32[256,1280]{1,0:T(8,128)}, u32[]{:S(2)}) copy-start(f32[256,1280]{1,0:T(8,128)} %copy-done.4) | copy-start | bytes 3932164
  134.4 1.4 collective-permute-start.16
  135.8 4.1 %collective-permute-start.17 = (f32[8,1280]{1,0:T(8,128)S(1)}, f32[8,1280]{1,0:T(8,128)S(1)}, u32[]{:S(2)}, u32[]{:S(2)}) collective-permute-start(f32[8,1280]{1,0:T(8,128)S(1)} %select_add_fusion), channel_id=1, source_target_pairs={{0,2},{2,4},{4,6},{6,0},{1,3},{3,5},{5,7},{7,1},{8,10},{10,12},{12... | collective-permute-start | bytes 122888 | tf_op jit(solution)/shard_map/ppermute | solution.py:41
  136.3 4.4 %collective-permute-start.18 = (f32[8,1280]{1,0:T(8,128)S(1)}, f32[8,1280]{1,0:T(8,128)S(1)}, u32[]{:S(2)}, u32[]{:S(2)}) collective-permute-start(f32[8,1280]{1,0:T(8,128)S(1)} %select_add_fusion), channel_id=1, source_target_pairs={{0,4},{2,6},{4,0},{6,2},{1,5},{3,7},{5,1},{7,3},{8,12},{10,14},{12... | collective-permute-start | bytes 122888 | tf_op jit(solution)/shard_map/ppermute | solution.py:41
  138.0 3.3 %collective-permute-start.19 = (f32[8,1280]{1,0:T(8,128)S(1)}, f32[8,1280]{1,0:T(8,128)S(1)}, u32[]{:S(2)}, u32[]{:S(2)}) collective-permute-start(f32[8,1280]{1,0:T(8,128)S(1)} %select_add_fusion), channel_id=1, source_target_pairs={{0,6},{2,0},{4,2},{6,4},{1,7},{3,1},{5,3},{7,5},{8,14},{10,8},{12,... | collective-permute-start | bytes 122888 | tf_op jit(solution)/shard_map/ppermute | solution.py:41
  141.3 4.2 %collective-permute-start.20 = (f32[8,1280]{1,0:T(8,128)S(1)}, f32[8,1280]{1,0:T(8,128)S(1)}, u32[]{:S(2)}, u32[]{:S(2)}) collective-permute-start(f32[8,1280]{1,0:T(8,128)S(1)} %add_add_fusion.1), channel_id=1, source_target_pairs={{0,16},{16,32},{32,48},{48,0},{1,17},{17,33},{33,49},{49,1},{2,18}... | collective-permute-start | bytes 122888 | tf_op jit(solution)/shard_map/ppermute | solution.py:41
  141.3 4.5 %collective-permute-start.21 = (f32[8,1280]{1,0:T(8,128)S(1)}, f32[8,1280]{1,0:T(8,128)S(1)}, u32[]{:S(2)}, u32[]{:S(2)}) collective-permute-start(f32[8,1280]{1,0:T(8,128)S(1)} %add_add_fusion.1), channel_id=1, source_target_pairs={{0,32},{16,48},{32,0},{48,16},{1,33},{17,49},{33,1},{49,17},{2,34}... | collective-permute-start | bytes 122888 | tf_op jit(solution)/shard_map/ppermute | solution.py:41
  141.8 4.6 %collective-permute-start.22 = (f32[8,1280]{1,0:T(8,128)S(1)}, f32[8,1280]{1,0:T(8,128)S(1)}, u32[]{:S(2)}, u32[]{:S(2)}) collective-permute-start(f32[8,1280]{1,0:T(8,128)S(1)} %add_add_fusion.1), channel_id=1, source_target_pairs={{0,48},{16,0},{32,16},{48,32},{1,49},{17,1},{33,17},{49,33},{2,50}... | collective-permute-start | bytes 122888 | tf_op jit(solution)/shard_map/ppermute | solution.py:41
  147.2 11.7 %all-to-all-start.2 = ((f32[8,8,1280]{2,1,0:T(8,128)}), f32[8,8,1280]{2,1,0:T(8,128)}, u32[]{:S(2)}, u32[]{:S(2)}) async-start(f32[8,8,1280]{2,1,0:T(8,128)} %broadcast_in_dim.12), calls=%async_computation.2 | async-start | bytes 655360 | tf_op jit(solution)/shard_map/all_to_all | solution.py:53
  151.3 3.1 %copy-start.3 = (f32[256,1280]{1,0:T(8,128)S(1)}, f32[256,1280]{1,0:T(8,128)}, u32[]{:S(2)}) copy-start(f32[256,1280]{1,0:T(8,128)} %copy-done.2) | copy-start | bytes 3932164
  156.4 8.5 %copy-start.9 = (f32[1280,16]{0,1:T(8,128)S(1)}, f32[1280,16]{0,1:T(8,128)}, u32[]{:S(2)}) copy-start(f32[1280,16]{0,1:T(8,128)} %param.6) | copy-start | bytes 245764
  159.9 6.9 %collective-permute-start.23 = (f32[8,1280]{1,0:T(8,128)S(1)}, f32[8,1280]{1,0:T(8,128)S(1)}, u32[]{:S(2)}, u32[]{:S(2)}) collective-permute-start(f32[8,1280]{1,0:T(8,128)S(1)} %reduce_sum.59), channel_id=1, source_target_pairs={{0,1},{1,0},{2,3},{3,2},{4,5},{5,4},{6,7},{7,6},{8,9},{9,8},{10,11... | collective-permute-start | bytes 122888 | tf_op jit(solution)/shard_map/ppermute | solution.py:54

commit v3 on v2

v3 whole, which is shorter than its diff:
```python
import jax
import jax.numpy as jnp
from jax import lax
from jax.experimental import pallas as pl
from jax.experimental.pallas import tpu as pltpu
from jax.sharding import Mesh, PartitionSpec as P

highest = lax.Precision.HIGHEST
high = lax.Precision.HIGH

DP = ("zl", "y")
EX = ("zh", "x", "c")
ZEX = ("zl",) + EX
ALL = DP + EX
UP = [(i, (i + 1) % 4) for i in range(4)]
DOWN = [(i, (i - 1) % 4) for i in range(4)]


def gather_y(block):
    half = block.shape[0] // 2
    from_below = lax.ppermute(block, "y", UP)
    from_above = lax.ppermute(block, "y", DOWN)
    far_a = lax.ppermute(from_below[:half], "y", UP)
    far_b = lax.ppermute(from_above[half:], "y", DOWN)
    return jnp.concatenate([block, from_below, from_above, far_a, far_b])


def scatter_y(parts):
    n = parts.shape[0] // 4
    half = n // 2
    own, below, above, far = parts[:n], parts[n : 2 * n], parts[2 * n : 3 * n], parts[3 * n :]
    down = lax.ppermute(jnp.concatenate([below[half:], far[:half]]), "y", DOWN)
    up = lax.ppermute(jnp.concatenate([above[:half], far[half:]]), "y", UP)
    down, up = lax.optimization_barrier((down, up))
    low, top = lax.optimization_barrier((below[:half] + down[half:], above[half:] + up[half:]))
    low, top = lax.ppermute(low, "y", DOWN), lax.ppermute(top, "y", UP)
    low, top = lax.optimization_barrier((low, top))
    return jnp.concatenate([own[:half] + up[:half] + low, own[half:] + down[:half] + top])


def sum_axis(block, axis):
    total = block
    for k in range(1, 4):
        total = total + lax.ppermute(block, axis, [(i, (i + k) % 4) for i in range(4)])
    return total


def sum_all(local, beside):
    swap = [(0, 1), (1, 0)]
    first = lax.axis_index("c") == 0
    half = local.shape[0] // 2
    low, top = local[:half], local[half:]
    mine = jnp.where(first, low, top) + lax.ppermute(jnp.where(first, top, low), "c", swap)
    mine = sum_axis(sum_axis(mine, "x"), "y")
    pieces = jnp.broadcast_to(mine[None], (8,) + mine.shape)
    mine = jnp.sum(lax.all_to_all(pieces, ("zl", "zh"), 0, 0, tiled=True), axis=0)
    mine, beside = lax.optimization_barrier((mine, beside))
    other = lax.ppermute(mine, "c", swap)
    return jnp.where(first, jnp.concatenate([mine, other]), jnp.concatenate([other, mine])), beside


def split(a):
    top = a.astype(jnp.bfloat16)
    return top, (a - top.astype(jnp.float32)).astype(jnp.bfloat16)


def dot3(a, b, dims):
    (a_top, a_low), (b_top, b_low) = a, b
    dot = lambda u, v: lax.dot_general(u, v, (dims, ((), ())), preferred_element_type=jnp.float32)
    return dot(a_low, b_top) + dot(a_top, b_low) + dot(a_top, b_top)


PIECES = 4


def fetch(source, target, sems):
    rows = target.shape[0] // PIECES
    return [
        pltpu.make_async_copy(
            source.at[pl.ds(k * rows, rows)], target.at[pl.ds(k * rows, rows)], sems.at[k]
        )
        for k in range(PIECES)
    ]


def route_kernel(
    tokens_hbm, cotangent_hbm, router_ref, sent_ref, dispatch_ref, combine_ref, tokens_ref, cotangent_ref, sems
):
    e, d = router_ref.shape
    first = fetch(tokens_hbm, tokens_ref, sems.at[0])
    second = fetch(cotangent_hbm, cotangent_ref, sems.at[1])
    for copy in first + second:
        copy.start()
    half = tokens_ref.shape[0] // 2
    parts = []
    for k in range(2):
        for copy in first[k * PIECES // 2 : (k + 1) * PIECES // 2]:
            copy.wait()
        parts.append(
            lax.dot_general(
                router_ref[...],
                tokens_ref[k * half : (k + 1) * half, :],
                (((1,), (1,)), ((), ())),
                precision=highest,
                preferred_element_type=jnp.float32,
            )
        )
    logits = jnp.concatenate(parts, axis=1)
    tokens = tokens_ref[...]
    by_token = jnp.exp(logits - jnp.max(logits, axis=1, keepdims=True))
    dispatch = by_token / jnp.sum(by_token, axis=1, keepdims=True)
    by_expert = jnp.exp(logits - jnp.max(logits, axis=0, keepdims=True))
    combine = by_expert / jnp.sum(by_expert, axis=0, keepdims=True)
    dispatch_ref[...] = dispatch
    combine_ref[...] = combine
    slot_in = dot3(split(dispatch), split(tokens), ((1,), (0,)))
    for copy in second:
        copy.wait()
    d_slot_out = dot3(split(combine), split(cotangent_ref[...]), ((1,), (0,)))
    for k in range(4):
        sent_ref[k * e : (k + 1) * e, 0, :d] = slot_in
        sent_ref[k * e : (k + 1) * e, 0, d:] = d_slot_out


def route(tokens, cotangent, router_t):
    e, d = router_t.shape
    p = tokens.shape[0]
    f32 = jnp.float32
    return pl.pallas_call(
        route_kernel,
        out_shape=(
            jax.ShapeDtypeStruct((4 * e, 1, 2 * d), f32),
            jax.ShapeDtypeStruct((e, p), f32),
            jax.ShapeDtypeStruct((e, p), f32),
        ),
        in_specs=[
            pl.BlockSpec(memory_space=pltpu.HBM),
            pl.BlockSpec(memory_space=pltpu.HBM),
            pl.BlockSpec(memory_space=pltpu.VMEM),
        ],
        scratch_shapes=[
            pltpu.VMEM((p, d), f32),
            pltpu.VMEM((p, d), f32),
            pltpu.SemaphoreType.DMA((2, PIECES)),
        ],
        compiler_params=pltpu.CompilerParams(vmem_limit_bytes=56 * 2**20),
        name="route",
    )(tokens, cotangent, router_t)


def finish_kernel(
    back_hbm, tokens_ref, cotangent_ref, dispatch_ref, combine_ref, local_ref, weights_ref, slots_ref,
    back_ref, sems
):
    e, p = dispatch_ref.shape
    d = tokens_ref.shape[1]
    copies = fetch(back_hbm, back_ref, sems)
    for copy in copies:
        copy.start()
    total = None
    for k in range(4):
        copies[k].wait()
        rows = back_ref[k * e : (k + 1) * e, 0, :]
        total = rows if total is None else total + rows
    slot_out, d_slot_in = total[:, :d], total[:, d:]
    slots_ref[...] = d_slot_in
    dispatch, combine = dispatch_ref[...], combine_ref[...]
    tokens = split(tokens_ref[...])
    d_disp = dot3(split(d_slot_in), tokens, ((1,), (1,)))
    d_comb = dot3(split(slot_out), split(cotangent_ref[...]), ((1,), (1,)))
    d_logits = dispatch * (d_disp - jnp.sum(dispatch * d_disp, axis=1, keepdims=True))
    d_logits = d_logits + combine * (d_comb - jnp.sum(combine * d_comb, axis=0, keepdims=True))
    weights_ref[:e, :] = dispatch
    weights_ref[e:, :] = d_logits
    local_ref[...] = dot3(split(d_logits), tokens, ((1,), (0,)))


def finish(back, halves, dispatch, combine):
    e, p = dispatch.shape
    d = back.shape[2] // 2
    f32 = jnp.float32
    return pl.pallas_call(
        finish_kernel,
        out_shape=(
            jax.ShapeDtypeStruct((e, d), f32),
            jax.ShapeDtypeStruct((2 * e, p), f32),
            jax.ShapeDtypeStruct((e, d), f32),
        ),
        in_specs=[pl.BlockSpec(memory_space=pltpu.HBM)] + [pl.BlockSpec(memory_space=pltpu.VMEM)] * 4,
        scratch_shapes=[pltpu.VMEM(back.shape, f32), pltpu.SemaphoreType.DMA((PIECES,))],
        compiler_params=pltpu.CompilerParams(vmem_limit_bytes=24 * 2**20),
        name="finish",
    )(back, *halves, dispatch, combine)


def on_device(tokens, router, w_in, w_out, cotangent):
    tokens, cotangent = tokens[0], cotangent[0]
    w_in, w_out = w_in[0], w_out[0]
    width = tokens.shape[1]
    n_exp = router.shape[1]
    router_t = router.T
    sent, dispatch, combine = route(tokens, cotangent, router_t)
    arrived = lax.all_to_all(sent, ZEX, 0, 0, tiled=True).reshape(4 * n_exp, 2 * width)
    x = gather_y(arrived[:, :width])
    dy = gather_y(arrived[:, width:])
    pre_act = jnp.einsum("rd,dh->rh", x, w_in, precision=high)
    hidden, gelu_pull = jax.vjp(jax.nn.gelu, pre_act)
    d_hidden = jnp.einsum("rd,hd->rh", dy, w_out, precision=high)
    d_pre = gelu_pull(d_hidden)[0]
    part_out = jnp.einsum("rh,hd->rd", hidden, w_out, precision=high)
    part_grad = jnp.einsum("rh,dh->rd", d_pre, w_in, precision=high)
    summed = jnp.concatenate([scatter_y(part_out), scatter_y(part_grad)], axis=1)
    grad_w_out = jnp.einsum("rh,rd->hd", hidden, dy, precision=high)
    grad_w_in = jnp.einsum("rd,rh->dh", x, d_pre, precision=high)
    back = lax.all_to_all(summed.reshape(4 * n_exp, 1, 2 * width), ZEX, 0, 0, tiled=True)
    halves = tokens, cotangent
    back, grad_w_in, grad_w_out = lax.optimization_barrier((back, grad_w_in, grad_w_out))
    local_router, weights, d_slot_in = finish(back, halves, dispatch, combine)
    slots = jnp.concatenate([d_slot_in, router_t])
    grad_tokens = jnp.einsum("kp,kd->pd", weights, slots, precision=high)
    grad_router, grad_tokens = sum_all(local_router, grad_tokens)
    grad_router = grad_router.T
    return (grad_tokens[None], grad_router, grad_w_in[None], grad_w_out[None])


def solution(mesh):
    split = Mesh(mesh.devices.reshape(4, 4, 2, 4, 2), ALL)
    return jax.shard_map(
        on_device,
        mesh=split,
        in_specs=(
            P(ALL, None, None),
            P(),
            P(EX, None, DP),
            P(EX, DP, None),
            P(ALL, None, None),
        ),
        out_specs=(
            P(ALL, None, None),
            P(),
            P(EX, None, DP),
            P(EX, DP, None),
        ),
        check_vma=False,
    )
```

time: 168 us -> 158 us (0.940)
  waiting for transfers between devices: 57.7 us -> 47.4 us
  Pallas kernels: 0 us -> 9.27 us
  matrix products: 19.3 us -> 11.6 us
  starting transfers between devices: 43.3 us -> 49.4 us
  local copies, waits for them, and re-layouts: 9.32 us -> 4.66 us
  other arithmetic: 3.47 us -> 1.04 us
    ppermute x8, waiting for transfers between devices: 20.8 us -> 10.8 us  [the longest x2 5.45 us: scatter_y(): up = lax.ppermute(jnp.concatenate([above[:half], far[half:]]), 'y', UP)]
    pallas_call x0 -> x2, Pallas kernels: none -> 9.27 us  [the longest x1 6.26 us: route(): pl.pallas_call(route_kernel, out_shape=(jax.ShapeDtypeStruct((4 * e, 1, 2...]
    dot_general x8 -> x1, matrix products: 9.48 us -> 1.78 us  [on_device(): grad_tokens = jnp.einsum('kp,kd->pd', weights, slots, precision=high)]
    all_to_all x1, waiting for transfers between devices: 20.3 us -> 15.1 us  [on_device(): lax.all_to_all(summed.reshape(4 * n_exp, 1, 2 * width), ZEX, 0, 0, tiled=...]
    ppermute x8, starting transfers between devices: 6.31 us -> 10.7 us  [the longest x2 5.35 us: scatter_y(): down = lax.ppermute(jnp.concatenate([below[half:], far[:half]]), 'y', DOWN)]
    all_to_all x2 -> x0, local copies, waits for them, and re-layouts: 4.21 us -> none  [the longest x1 2.7 us: on_device(): arrived = lax.all_to_all(sent, ZEX, 0, 0, tiled=True)]
    all_to_all x1, waiting for transfers between devices: 1.68 us -> 5.44 us  [sum_all(): lax.all_to_all(pieces, ('zl', 'zh'), 0, 0, tiled=True)]
  transfers between devices with their start and end apart: 26 -> 26, of which waited for: 18 -> 17; matrix products, arithmetic and copies ran while one was open for 8% -> 8% of each run, Pallas kernels for 0% -> 0%
where the time goes in v3:
time: 158 us
  starting transfers between devices  49.4 us (31%)
  waiting for transfers between devices  47.4 us (30%)
  blocking collectives  33.4 us (21%)
  matrix products  11.6 us (7%)
  Pallas kernels  9.27 us (6%)
  local copies, waits for them, and re-layouts  4.66 us (3%)
    all_to_all x1, blocking collectives, on_device(): lax.all_to_all(sent, ZEX, 0, 0, tiled=True).reshape(4 * n_exp, 2 * width)  33.4 us
    all_to_all x1, waiting for transfers between devices, on_device(): lax.all_to_all(summed.reshape(4 * n_exp, 1, 2 * width), ZEX, 0, 0, tiled=...  15.1 us
    all_to_all x1, starting transfers between devices, on_device(): lax.all_to_all(summed.reshape(4 * n_exp, 1, 2 * width), ZEX, 0, 0, tiled=...  11.9 us
    ppermute x2, waiting for transfers between devices, gather_y(): from_below = lax.ppermute(block, 'y', UP)  8.89 us
    pallas_call x1, Pallas kernels, route(): pl.pallas_call(route_kernel, out_shape=(jax.ShapeDtypeStruct((4 * e, 1, 2...  6.26 us
    ppermute x6, starting transfers between devices, sum_axis(): lax.ppermute(block, axis, [(i, (i + k) % 4) for i in range(4)])  5.75 us
    ppermute x2, starting transfers between devices, gather_y(): far_b = lax.ppermute(from_above[half:], 'y', DOWN)  5.46 us
    ppermute x2, waiting for transfers between devices, scatter_y(): up = lax.ppermute(jnp.concatenate([above[:half], far[half:]]), 'y', UP)  5.45 us
  transfers between devices with their start and end apart: 26, of which 17 were waited for; matrix products, arithmetic and copies ran while one was open for 8% of the time, Pallas kernels for 0%

profile of v3, /device:TPU:1, one launch (start us, length us, event | category | flops | bytes accessed | tf_op | source)
XLA Modules:
  0.0 157.7 jit_solution(5051569024304856260)
XLA Ops:
  0.6 0.0 copy-start
  0.6 6.3 %route.1 = (f32[64,1,2560]{2,1,0:T(1,128)}, f32[16,256]{1,0:T(8,128)}, f32[16,256]{1,0:T(8,128)}) custom-call(f32[256,1280]{1,0:T(8,128)} %bitcast.30, f32[256,1280]{1,0:T(8,128)} %bitcast.32, f32[16,1280]{1,0:T(8,128)} %bitcast.38), custom_call_target="tpu_custom_call" | custom-call | tf_op jit(solution)/shard_map/route/pallas_call | solution.py:129
  6.9 33.4 %all_to_all.15 = f32[64,1,2560]{2,1,0:T(1,128)S(1)} all-to-all(f32[64,1,2560]{2,1,0:T(1,128)} %get-tuple-element.27), channel_id=1, replica_groups=mesh['zl'=4,'y'=4,'zh'=2,'x'=4,'c'=2] {'zl','zh','x','c'}, dimensions={0} | all-to-all | bytes 1310720 | tf_op jit(solution)/shard_map/all_to_all | solution.py:203
  40.3 0.1 fusion.37
  40.4 1.4 collective-permute-start
  41.8 1.5 collective-permute-start.1
  43.3 2.7 %collective-permute-start.9 = (f32[64,1280]{1,0:T(8,128)S(1)}, f32[64,1280]{1,0:T(8,128)S(1)}, u32[]{:S(2)}, u32[]{:S(2)}) collective-permute-start(f32[64,1280]{1,0:T(8,128)S(1)} %get-tuple-element.66), channel_id=1, source_target_pairs={{0,48},{16,0},{32,16},{48,32},{1,49},{17,1},{33,17},{49,33},{2,50}... | collective-permute-start | bytes 983048 | tf_op jit(solution)/shard_map/ppermute | solution.py:22
  46.0 4.7 %collective-permute-done = f32[64,1280]{1,0:T(8,128)S(1)} collective-permute-done((f32[64,1280]{1,0:T(8,128)S(1)}, f32[64,1280]{1,0:T(8,128)S(1)}, u32[]{:S(2)}, u32[]{:S(2)}) %collective-permute-start) | collective-permute-done | bytes 327712 | tf_op jit(solution)/shard_map/ppermute | solution.py:21
  50.7 0.1 collective-permute-start.2
  50.9 2.7 %collective-permute-start.3 = (f32[32,1280]{1,0:T(8,128)S(1)}, f32[32,1280]{1,0:T(8,128)S(1)}, u32[]{:S(2)}, u32[]{:S(2)}) collective-permute-start(f32[32,1280]{1,0:T(8,128)S(1)} %slice.154), channel_id=1, source_target_pairs={{0,48},{16,0},{32,16},{48,32},{1,49},{17,1},{33,17},{49,33},{2,50}... | collective-permute-start | bytes 491528 | tf_op jit(solution)/shard_map/ppermute | solution.py:24
  53.6 4.2 %collective-permute-done.8 = f32[64,1280]{1,0:T(8,128)S(1)} collective-permute-done((f32[64,1280]{1,0:T(8,128)S(1)}, f32[64,1280]{1,0:T(8,128)S(1)}, u32[]{:S(2)}, u32[]{:S(2)}) %collective-permute-start.8) | collective-permute-done | bytes 327712 | tf_op jit(solution)/shard_map/ppermute | solution.py:21
  57.8 0.1 collective-permute-start.10
  57.9 2.7 %collective-permute-start.11 = (f32[32,1280]{1,0:T(8,128)S(1)}, f32[32,1280]{1,0:T(8,128)S(1)}, u32[]{:S(2)}, u32[]{:S(2)}) collective-permute-start(f32[32,1280]{1,0:T(8,128)S(1)} %slice.165), channel_id=1, source_target_pairs={{0,48},{16,0},{32,16},{48,32},{1,49},{17,1},{33,17},{49,33},{2,50}... | collective-permute-start | bytes 491528 | tf_op jit(solution)/shard_map/ppermute | solution.py:24
  60.6 0.0 copy-start.7
  60.8 0.5 collective-permute-done.2
  61.3 0.8 copy-done.7
  62.1 0.9 fusion.6
  63.0 1.3 fusion.2
  64.4 0.4 collective-permute-start.5
  64.9 2.6 %collective-permute-start.4 = (f32[64,1280]{1,0:T(8,128)S(1)}, f32[64,1280]{1,0:T(8,128)S(1)}, u32[]{:S(2)}, u32[]{:S(2)}) collective-permute-start(f32[64,1280]{1,0:T(8,128)S(1)} %pad_maximum_fusion), channel_id=1, source_target_pairs={{0,48},{16,0},{32,16},{48,32},{1,49},{17,1},{33,17},{49,33},{2,50}... | collective-permute-start | bytes 983048 | tf_op jit(solution)/shard_map/ppermute | solution.py:32
  67.5 0.0 copy-start.5
  67.5 1.0 fusion.13
  68.6 0.0 copy-done.5
  68.6 1.4 fusion.4
  70.0 0.1 collective-permute-start.13
  70.2 2.7 %collective-permute-start.12 = (f32[64,1280]{1,0:T(8,128)S(1)}, f32[64,1280]{1,0:T(8,128)S(1)}, u32[]{:S(2)}, u32[]{:S(2)}) collective-permute-start(f32[64,1280]{1,0:T(8,128)S(1)} %pad_maximum_fusion.2), channel_id=1, source_target_pairs={{0,48},{16,0},{32,16},{48,32},{1,49},{17,1},{33,17},{49,33},{2,50}... | collective-permute-start | bytes 983048 | tf_op jit(solution)/shard_map/ppermute | solution.py:32
  72.9 2.3 %collective-permute-start.6 = (f32[32,1280]{1,0:T(8,128)S(1)}, f32[32,1280]{1,0:T(8,128)S(1)}, u32[]{:S(2)}, u32[]{:S(2)}) collective-permute-start(f32[32,1280]{1,0:T(8,128)S(1)} %get-tuple-element.30), channel_id=1, source_target_pairs={{0,48},{16,0},{32,16},{48,32},{1,49},{17,1},{33,17},{49,33},{2,50}... | collective-permute-start | bytes 491528 | tf_op jit(solution)/shard_map/ppermute | solution.py:36
  75.3 5.4 %collective-permute-done.13 = f32[64,1280]{1,0:T(8,128)S(1)} collective-permute-done((f32[64,1280]{1,0:T(8,128)S(1)}, f32[64,1280]{1,0:T(8,128)S(1)}, u32[]{:S(2)}, u32[]{:S(2)}) %collective-permute-start.13) | collective-permute-done | bytes 327712 | tf_op jit(solution)/shard_map/ppermute | solution.py:33
  80.8 2.6 %collective-permute-start.14 = (f32[32,1280]{1,0:T(8,128)S(1)}, f32[32,1280]{1,0:T(8,128)S(1)}, u32[]{:S(2)}, u32[]{:S(2)}) collective-permute-start(f32[32,1280]{1,0:T(8,128)S(1)} %get-tuple-element.36), channel_id=1, source_target_pairs={{0,48},{16,0},{32,16},{48,32},{1,49},{17,1},{33,17},{49,33},{2,50}... | collective-permute-start | bytes 491528 | tf_op jit(solution)/shard_map/ppermute | solution.py:36
  83.3 0.0 collective-permute-done.6
  83.4 0.8 collective-permute-done.7
  84.2 3.2 %collective-permute-done.14 = f32[32,1280]{1,0:T(8,128)S(1)} collective-permute-done((f32[32,1280]{1,0:T(8,128)S(1)}, f32[32,1280]{1,0:T(8,128)S(1)}, u32[]{:S(2)}, u32[]{:S(2)}) %collective-permute-start.14) | collective-permute-done | bytes 163872 | tf_op jit(solution)/shard_map/ppermute | solution.py:36
  87.4 1.3 collective-permute-done.15
  88.7 0.1 fusion.17
  88.9 1.3 reshape.16
  90.2 11.9 %all-to-all-start.1 = ((f32[64,1,2560]{2,1,0:T(1,128)}), f32[64,1,2560]{2,1,0:T(1,128)}, u32[]{:S(2)}, u32[]{:S(2)}) async-start(f32[64,1,2560]{2,1,0:T(1,128)} %reshape.16), calls=%async_computation.1 | async-start | bytes 1310720 | tf_op jit(solution)/shard_map/all_to_all | solution.py:215
  102.1 0.0 copy-start.6
  102.1 3.1 %fusion.38 = f32[1280,320]{0,1:T(8,128)} fusion(f32[256,1280]{1,0:T(8,128)S(1)} %constant_dynamic-update-slice_fusion, f32[256,320]{0,1:T(8,128)} %copy-done.8), kind=kOutput, calls=%fused_computation.68 | convolution fusion | flops 629145600 | bytes 3276800 | tf_op jit(solution)/shard_map/rd,rh->dh/dot_general | solution.py:214
  105.2 2.1 %fusion.24 = f32[320,1280]{1,0:T(8,128)} fusion(f32[256,1280]{1,0:T(8,128)S(1)} %copy-done.6, f32[256,320]{0,1:T(8,128)S(1)} %fusion.6), kind=kOutput, calls=%fused_computation.39 | convolution fusion | flops 629800960 | bytes 3276800 | tf_op jit(solution)/shard_map/rh,rd->hd/dot_general | solution.py:213
  107.3 15.1 %all-to-all-done.1.back_hbm = f32[64,1,2560]{2,1,0:T(1,128)} async-done(((f32[64,1,2560]{2,1,0:T(1,128)}), f32[64,1,2560]{2,1,0:T(1,128)}, u32[]{:S(2)}, u32[]{:S(2)}) %all-to-all-start.1) | async-done | bytes 655392 | tf_op jit(solution)/shard_map/all_to_all | solution.py:215
  122.4 1.3 copy-done.2
  123.7 3.0 %finish.1 = (f32[16,1280]{1,0:T(8,128)S(1)}, f32[32,256]{1,0:T(8,128)S(1)}, f32[16,1280]{1,0:T(8,128)S(1)}) custom-call(f32[64,1,2560]{2,1,0:T(1,128)} %all-to-all-done.1.back_hbm, f32[256,1280]{1,0:T(8,128)S(1)} %bitcast.31, f32[256,1280]{1,0:T(8,128)S(1)} %bitcast.33, f32[16,256]{1,0:T(8,128)S(1)} %copy-done.3, f32[16,256]{1,0:T(8,128)S(1)} %copy-done.4), custom_call_target="tpu_custom_call" | custom-call | tf_op jit(solution)/shard_map/finish/pallas_call | solution.py:182
  126.7 0.0 copy-start.9
  126.8 0.5 collective-permute-start.16
  127.3 0.9 collective-permute-done.16
  128.1 0.5 collective-permute-start.17
  128.6 1.7 %collective-permute-start.18 = (f32[8,1280]{1,0:T(8,128)S(1)}, f32[8,1280]{1,0:T(8,128)S(1)}, u32[]{:S(2)}, u32[]{:S(2)}) collective-permute-start(f32[8,1280]{1,0:T(8,128)S(1)} %select_add_fusion), channel_id=1, source_target_pairs={{0,4},{2,6},{4,0},{6,2},{1,5},{3,7},{5,1},{7,3},{8,12},{10,14},{12... | collective-permute-start | bytes 122888 | tf_op jit(solution)/shard_map/ppermute | solution.py:44
  130.3 0.8 collective-permute-start.19
  131.1 1.1 collective-permute-done.17
  132.3 0.7 collective-permute-done.18
  133.0 0.6 collective-permute-done.19
  133.6 0.1 collective-permute-start.20
  133.7 0.9 collective-permute-start.21
  134.6 1.8 %collective-permute-start.22 = (f32[8,1280]{1,0:T(8,128)S(1)}, f32[8,1280]{1,0:T(8,128)S(1)}, u32[]{:S(2)}, u32[]{:S(2)}) collective-permute-start(f32[8,1280]{1,0:T(8,128)S(1)} %add_add_fusion.1), channel_id=1, source_target_pairs={{0,48},{16,0},{32,16},{48,32},{1,49},{17,1},{33,17},{49,33},{2,50}... | collective-permute-start | bytes 122888 | tf_op jit(solution)/shard_map/ppermute | solution.py:44
  136.4 1.4 collective-permute-done.20
  137.8 0.7 collective-permute-done.21
  138.5 0.2 collective-permute-done.22
  138.8 0.8 broadcast_in_dim.15
  139.5 4.0 %all-to-all-start.2 = ((f32[8,8,1280]{2,1,0:T(8,128)}), f32[8,8,1280]{2,1,0:T(8,128)S(1)}, u32[]{:S(2)}, u32[]{:S(2)}) async-start(f32[8,8,1280]{2,1,0:T(8,128)} %broadcast_in_dim.15), calls=%async_computation.2 | async-start | bytes 655360 | tf_op jit(solution)/shard_map/all_to_all | solution.py:56
  143.5 1.8 %fusion.20 = f32[256,1280]{1,0:T(8,128)} fusion(f32[32,256]{1,0:T(8,128)S(1)} %get-tuple-element.44, f32[16,1280]{1,0:T(8,128)S(1)} %bitcast.39, f32[16,1280]{1,0:T(8,128)S(1)} %get-tuple-element.45), kind=kOutput, calls=%fused_computation.35 | convolution fusion | flops 62955520 | bytes 1507328 | tf_op jit(solution)/shard_map/kp,kd->pd/dot_general | solution.py:220
  145.3 5.4 %all-to-all-done.2 = f32[8,8,1280]{2,1,0:T(8,128)S(1)} async-done(((f32[8,8,1280]{2,1,0:T(8,128)}), f32[8,8,1280]{2,1,0:T(8,128)S(1)}, u32[]{:S(2)}, u32[]{:S(2)}) %all-to-all-start.2) | async-done | bytes 327712 | tf_op jit(solution)/shard_map/all_to_all | solution.py:56
  150.8 5.4 %collective-permute-start.23 = (f32[8,1280]{1,0:T(8,128)S(1)}, f32[8,1280]{1,0:T(8,128)S(1)}, u32[]{:S(2)}, u32[]{:S(2)}) collective-permute-start(f32[8,1280]{1,0:T(8,128)S(1)} %reduce_sum.9), channel_id=1, source_target_pairs={{0,1},{1,0},{2,3},{3,2},{4,5},{5,4},{6,7},{7,6},{8,9},{9,8},{10,11... | collective-permute-start | bytes 122888 | tf_op jit(solution)/shard_map/ppermute | solution.py:58
  156.1 0.9 collective-permute-done.23
  157.0 0.6 fusion.25
  (50 shorter events, 0.7 us)
Async XLA Ops:
  0.6 62.4 %copy-start = (f32[1,320,1280]{2,1,0:T(8,128)S(1)}, f32[1,320,1280]{2,1,0:T(8,128)}, u32[]{:S(2)}) copy-start(f32[1,320,1280]{2,1,0:T(8,128)} %param.8) | copy-start | bytes 4915204
  40.4 10.3 %collective-permute-start = (f32[64,1280]{1,0:T(8,128)S(1)}, f32[64,1280]{1,0:T(8,128)S(1)}, u32[]{:S(2)}, u32[]{:S(2)}) collective-permute-start(f32[64,1280]{1,0:T(8,128)S(1)} %get-tuple-element.69), channel_id=1, source_target_pairs={{0,16},{16,32},{32,48},{48,0},{1,17},{17,33},{33,49},{49,1},{2,18}... | collective-permute-start | bytes 983048 | tf_op jit(solution)/shard_map/ppermute | solution.py:21
  41.8 9.1 %collective-permute-start.1 = (f32[64,1280]{1,0:T(8,128)S(1)}, f32[64,1280]{1,0:T(8,128)S(1)}, u32[]{:S(2)}, u32[]{:S(2)}) collective-permute-start(f32[64,1280]{1,0:T(8,128)S(1)} %get-tuple-element.69), channel_id=1, source_target_pairs={{0,48},{16,0},{32,16},{48,32},{1,49},{17,1},{33,17},{49,33},{2,50}... | collective-permute-start | bytes 983048 | tf_op jit(solution)/shard_map/ppermute | solution.py:22
  43.3 14.4 %collective-permute-start.8 = (f32[64,1280]{1,0:T(8,128)S(1)}, f32[64,1280]{1,0:T(8,128)S(1)}, u32[]{:S(2)}, u32[]{:S(2)}) collective-permute-start(f32[64,1280]{1,0:T(8,128)S(1)} %get-tuple-element.66), channel_id=1, source_target_pairs={{0,16},{16,32},{32,48},{48,0},{1,17},{17,33},{33,49},{49,1},{2,18}... | collective-permute-start | bytes 983048 | tf_op jit(solution)/shard_map/ppermute | solution.py:21
  43.3 14.5 %collective-permute-start.9 = (f32[64,1280]{1,0:T(8,128)S(1)}, f32[64,1280]{1,0:T(8,128)S(1)}, u32[]{:S(2)}, u32[]{:S(2)}) collective-permute-start(f32[64,1280]{1,0:T(8,128)S(1)} %get-tuple-element.66), channel_id=1, source_target_pairs={{0,48},{16,0},{32,16},{48,32},{1,49},{17,1},{33,17},{49,33},{2,50}... | collective-permute-start | bytes 983048 | tf_op jit(solution)/shard_map/ppermute | solution.py:22
  50.7 10.5 %collective-permute-start.2 = (f32[32,1280]{1,0:T(8,128)S(1)}, f32[32,1280]{1,0:T(8,128)S(1)}, u32[]{:S(2)}, u32[]{:S(2)}) collective-permute-start(f32[32,1280]{1,0:T(8,128)S(1)} %slice.153), channel_id=1, source_target_pairs={{0,16},{16,32},{32,48},{48,0},{1,17},{17,33},{33,49},{49,1},{2,18}... | collective-permute-start | bytes 491528 | tf_op jit(solution)/shard_map/ppermute | solution.py:23
  50.9 10.4 %collective-permute-start.3 = (f32[32,1280]{1,0:T(8,128)S(1)}, f32[32,1280]{1,0:T(8,128)S(1)}, u32[]{:S(2)}, u32[]{:S(2)}) collective-permute-start(f32[32,1280]{1,0:T(8,128)S(1)} %slice.154), channel_id=1, source_target_pairs={{0,48},{16,0},{32,16},{48,32},{1,49},{17,1},{33,17},{49,33},{2,50}... | collective-permute-start | bytes 491528 | tf_op jit(solution)/shard_map/ppermute | solution.py:24
  57.8 9.7 %collective-permute-start.10 = (f32[32,1280]{1,0:T(8,128)S(1)}, f32[32,1280]{1,0:T(8,128)S(1)}, u32[]{:S(2)}, u32[]{:S(2)}) collective-permute-start(f32[32,1280]{1,0:T(8,128)S(1)} %slice.164), channel_id=1, source_target_pairs={{0,16},{16,32},{32,48},{48,0},{1,17},{17,33},{33,49},{49,1},{2,18}... | collective-permute-start | bytes 491528 | tf_op jit(solution)/shard_map/ppermute | solution.py:23
  57.9 9.6 %collective-permute-start.11 = (f32[32,1280]{1,0:T(8,128)S(1)}, f32[32,1280]{1,0:T(8,128)S(1)}, u32[]{:S(2)}, u32[]{:S(2)}) collective-permute-start(f32[32,1280]{1,0:T(8,128)S(1)} %slice.165), channel_id=1, source_target_pairs={{0,48},{16,0},{32,16},{48,32},{1,49},{17,1},{33,17},{49,33},{2,50}... | collective-permute-start | bytes 491528 | tf_op jit(solution)/shard_map/ppermute | solution.py:24
  60.6 1.4 copy-start.7
  64.4 8.5 %collective-permute-start.5 = (f32[64,1280]{1,0:T(8,128)S(1)}, f32[64,1280]{1,0:T(8,128)S(1)}, u32[]{:S(2)}, u32[]{:S(2)}) collective-permute-start(f32[64,1280]{1,0:T(8,128)S(1)} %pad_maximum_fusion.1), channel_id=1, source_target_pairs={{0,16},{16,32},{32,48},{48,0},{1,17},{17,33},{33,49},{49,1},{2,18}... | collective-permute-start | bytes 983048 | tf_op jit(solution)/shard_map/ppermute | solution.py:33
  64.9 8.0 %collective-permute-start.4 = (f32[64,1280]{1,0:T(8,128)S(1)}, f32[64,1280]{1,0:T(8,128)S(1)}, u32[]{:S(2)}, u32[]{:S(2)}) collective-permute-start(f32[64,1280]{1,0:T(8,128)S(1)} %pad_maximum_fusion), channel_id=1, source_target_pairs={{0,48},{16,0},{32,16},{48,32},{1,49},{17,1},{33,17},{49,33},{2,50}... | collective-permute-start | bytes 983048 | tf_op jit(solution)/shard_map/ppermute | solution.py:32
  67.5 1.1 copy-start.5
  68.6 12.2 %copy-start.8 = (f32[256,320]{0,1:T(8,128)}, f32[256,320]{0,1:T(8,128)S(1)}, u32[]{:S(2)}) copy-start(f32[256,320]{0,1:T(8,128)S(1)} %fusion.13) | copy-start | bytes 983044
  70.0 10.7 %collective-permute-start.13 = (f32[64,1280]{1,0:T(8,128)S(1)}, f32[64,1280]{1,0:T(8,128)S(1)}, u32[]{:S(2)}, u32[]{:S(2)}) collective-permute-start(f32[64,1280]{1,0:T(8,128)S(1)} %pad_maximum_fusion.3), channel_id=1, source_target_pairs={{0,16},{16,32},{32,48},{48,0},{1,17},{17,33},{33,49},{49,1},{2,18}... | collective-permute-start | bytes 983048 | tf_op jit(solution)/shard_map/ppermute | solution.py:33
  70.2 10.5 %collective-permute-start.12 = (f32[64,1280]{1,0:T(8,128)S(1)}, f32[64,1280]{1,0:T(8,128)S(1)}, u32[]{:S(2)}, u32[]{:S(2)}) collective-permute-start(f32[64,1280]{1,0:T(8,128)S(1)} %pad_maximum_fusion.2), channel_id=1, source_target_pairs={{0,48},{16,0},{32,16},{48,32},{1,49},{17,1},{33,17},{49,33},{2,50}... | collective-permute-start | bytes 983048 | tf_op jit(solution)/shard_map/ppermute | solution.py:32
  72.9 10.4 %collective-permute-start.6 = (f32[32,1280]{1,0:T(8,128)S(1)}, f32[32,1280]{1,0:T(8,128)S(1)}, u32[]{:S(2)}, u32[]{:S(2)}) collective-permute-start(f32[32,1280]{1,0:T(8,128)S(1)} %get-tuple-element.30), channel_id=1, source_target_pairs={{0,48},{16,0},{32,16},{48,32},{1,49},{17,1},{33,17},{49,33},{2,50}... | collective-permute-start | bytes 491528 | tf_op jit(solution)/shard_map/ppermute | solution.py:36
  75.3 9.0 %collective-permute-start.7 = (f32[32,1280]{1,0:T(8,128)S(1)}, f32[32,1280]{1,0:T(8,128)S(1)}, u32[]{:S(2)}, u32[]{:S(2)}) collective-permute-start(f32[32,1280]{1,0:T(8,128)S(1)} %get-tuple-element.31), channel_id=1, source_target_pairs={{0,16},{16,32},{32,48},{48,0},{1,17},{17,33},{33,49},{49,1},{2,18}... | collective-permute-start | bytes 491528 | tf_op jit(solution)/shard_map/ppermute | solution.py:36
  80.8 6.6 %collective-permute-start.14 = (f32[32,1280]{1,0:T(8,128)S(1)}, f32[32,1280]{1,0:T(8,128)S(1)}, u32[]{:S(2)}, u32[]{:S(2)}) collective-permute-start(f32[32,1280]{1,0:T(8,128)S(1)} %get-tuple-element.36), channel_id=1, source_target_pairs={{0,48},{16,0},{32,16},{48,32},{1,49},{17,1},{33,17},{49,33},{2,50}... | collective-permute-start | bytes 491528 | tf_op jit(solution)/shard_map/ppermute | solution.py:36
  83.3 5.4 %collective-permute-start.15 = (f32[32,1280]{1,0:T(8,128)S(1)}, f32[32,1280]{1,0:T(8,128)S(1)}, u32[]{:S(2)}, u32[]{:S(2)}) collective-permute-start(f32[32,1280]{1,0:T(8,128)S(1)} %get-tuple-element.37), channel_id=1, source_target_pairs={{0,16},{16,32},{32,48},{48,0},{1,17},{17,33},{33,49},{49,1},{2,18}... | collective-permute-start | bytes 491528 | tf_op jit(solution)/shard_map/ppermute | solution.py:36
  90.2 32.2 %all-to-all-start.1 = ((f32[64,1,2560]{2,1,0:T(1,128)}), f32[64,1,2560]{2,1,0:T(1,128)}, u32[]{:S(2)}, u32[]{:S(2)}) async-start(f32[64,1,2560]{2,1,0:T(1,128)} %reshape.16), calls=%async_computation.1 | async-start | bytes 1310720 | tf_op jit(solution)/shard_map/all_to_all | solution.py:215
  102.1 3.1 %copy-start.6 = (f32[256,1280]{1,0:T(8,128)S(1)}, f32[256,1280]{1,0:T(8,128)}, u32[]{:S(2)}) copy-start(f32[256,1280]{1,0:T(8,128)} %copy-done.5) | copy-start | bytes 3932164
  105.2 17.2 %copy-start.1 = (f32[1,256,1280]{2,1,0:T(8,128)S(1)}, f32[1,256,1280]{2,1,0:T(8,128)}, u32[]{:S(2)}) copy-start(f32[1,256,1280]{2,1,0:T(8,128)} %param.5) | copy-start | bytes 3932164
  105.2 17.2 %copy-start.3 = (f32[16,256]{1,0:T(8,128)S(1)}, f32[16,256]{1,0:T(8,128)}, u32[]{:S(2)}) copy-start(f32[16,256]{1,0:T(8,128)} %get-tuple-element.41.dispatch_ref) | copy-start | bytes 49156
  105.2 17.2 %copy-start.4 = (f32[16,256]{1,0:T(8,128)S(1)}, f32[16,256]{1,0:T(8,128)}, u32[]{:S(2)}) copy-start(f32[16,256]{1,0:T(8,128)} %get-tuple-element.42.combine_ref) | copy-start | bytes 49156
  122.4 1.3 copy-start.2
  126.7 16.8 %copy-start.9 = (f32[1280,16]{0,1:T(8,128)S(1)}, f32[1280,16]{0,1:T(8,128)}, u32[]{:S(2)}) copy-start(f32[1280,16]{0,1:T(8,128)} %param.6) | copy-start | bytes 245764
  126.8 1.4 collective-permute-start.16
  128.1 4.1 %collective-permute-start.17 = (f32[8,1280]{1,0:T(8,128)S(1)}, f32[8,1280]{1,0:T(8,128)S(1)}, u32[]{:S(2)}, u32[]{:S(2)}) collective-permute-start(f32[8,1280]{1,0:T(8,128)S(1)} %select_add_fusion), channel_id=1, source_target_pairs={{0,2},{2,4},{4,6},{6,0},{1,3},{3,5},{5,7},{7,1},{8,10},{10,12},{12... | collective-permute-start | bytes 122888 | tf_op jit(solution)/shard_map/ppermute | solution.py:44
  128.6 4.4 %collective-permute-start.18 = (f32[8,1280]{1,0:T(8,128)S(1)}, f32[8,1280]{1,0:T(8,128)S(1)}, u32[]{:S(2)}, u32[]{:S(2)}) collective-permute-start(f32[8,1280]{1,0:T(8,128)S(1)} %select_add_fusion), channel_id=1, source_target_pairs={{0,4},{2,6},{4,0},{6,2},{1,5},{3,7},{5,1},{7,3},{8,12},{10,14},{12... | collective-permute-start | bytes 122888 | tf_op jit(solution)/shard_map/ppermute | solution.py:44
  130.3 3.3 %collective-permute-start.19 = (f32[8,1280]{1,0:T(8,128)S(1)}, f32[8,1280]{1,0:T(8,128)S(1)}, u32[]{:S(2)}, u32[]{:S(2)}) collective-permute-start(f32[8,1280]{1,0:T(8,128)S(1)} %select_add_fusion), channel_id=1, source_target_pairs={{0,6},{2,0},{4,2},{6,4},{1,7},{3,1},{5,3},{7,5},{8,14},{10,8},{12,... | collective-permute-start | bytes 122888 | tf_op jit(solution)/shard_map/ppermute | solution.py:44
  133.6 4.2 %collective-permute-start.20 = (f32[8,1280]{1,0:T(8,128)S(1)}, f32[8,1280]{1,0:T(8,128)S(1)}, u32[]{:S(2)}, u32[]{:S(2)}) collective-permute-start(f32[8,1280]{1,0:T(8,128)S(1)} %add_add_fusion.1), channel_id=1, source_target_pairs={{0,16},{16,32},{32,48},{48,0},{1,17},{17,33},{33,49},{49,1},{2,18}... | collective-permute-start | bytes 122888 | tf_op jit(solution)/shard_map/ppermute | solution.py:44
  133.7 4.8 %collective-permute-start.21 = (f32[8,1280]{1,0:T(8,128)S(1)}, f32[8,1280]{1,0:T(8,128)S(1)}, u32[]{:S(2)}, u32[]{:S(2)}) collective-permute-start(f32[8,1280]{1,0:T(8,128)S(1)} %add_add_fusion.1), channel_id=1, source_target_pairs={{0,32},{16,48},{32,0},{48,16},{1,33},{17,49},{33,1},{49,17},{2,34}... | collective-permute-start | bytes 122888 | tf_op jit(solution)/shard_map/ppermute | solution.py:44
  134.6 4.2 %collective-permute-start.22 = (f32[8,1280]{1,0:T(8,128)S(1)}, f32[8,1280]{1,0:T(8,128)S(1)}, u32[]{:S(2)}, u32[]{:S(2)}) collective-permute-start(f32[8,1280]{1,0:T(8,128)S(1)} %add_add_fusion.1), channel_id=1, source_target_pairs={{0,48},{16,0},{32,16},{48,32},{1,49},{17,1},{33,17},{49,33},{2,50}... | collective-permute-start | bytes 122888 | tf_op jit(solution)/shard_map/ppermute | solution.py:44
  139.5 11.2 %all-to-all-start.2 = ((f32[8,8,1280]{2,1,0:T(8,128)}), f32[8,8,1280]{2,1,0:T(8,128)S(1)}, u32[]{:S(2)}, u32[]{:S(2)}) async-start(f32[8,8,1280]{2,1,0:T(8,128)} %broadcast_in_dim.15), calls=%async_computation.2 | async-start | bytes 655360 | tf_op jit(solution)/shard_map/all_to_all | solution.py:56
  150.8 6.2 %collective-permute-start.23 = (f32[8,1280]{1,0:T(8,128)S(1)}, f32[8,1280]{1,0:T(8,128)S(1)}, u32[]{:S(2)}, u32[]{:S(2)}) collective-permute-start(f32[8,1280]{1,0:T(8,128)S(1)} %reduce_sum.9), channel_id=1, source_target_pairs={{0,1},{1,0},{2,3},{3,2},{4,5},{5,4},{6,7},{7,6},{8,9},{9,8},{10,11... | collective-permute-start | bytes 122888 | tf_op jit(solution)/shard_map/ppermute | solution.py:58

commit v4 on v3

--- a/solution.py
+++ b/solution.py
@@ -25,17 +25,42 @@
     return jnp.concatenate([block, from_below, from_above, far_a, far_b])
 
 
-def scatter_y(parts):
+def send_first(parts):
     n = parts.shape[0] // 4
     half = n // 2
-    own, below, above, far = parts[:n], parts[n : 2 * n], parts[2 * n : 3 * n], parts[3 * n :]
+    below, above, far = parts[n : 2 * n], parts[2 * n : 3 * n], parts[3 * n :]
     down = lax.ppermute(jnp.concatenate([below[half:], far[:half]]), "y", DOWN)
     up = lax.ppermute(jnp.concatenate([above[:half], far[half:]]), "y", UP)
     down, up = lax.optimization_barrier((down, up))
-    low, top = lax.optimization_barrier((below[:half] + down[half:], above[half:] + up[half:]))
+    return down, up, below[:half] + down[half:], above[half:] + up[half:]
+
+
+def scatter_both(out, grad):
+    down_o, up_o, low_o, top_o = send_first(out)
+    down_g, up_g, low_g, top_g = send_first(grad)
+    low, top = jnp.concatenate([low_o, low_g], axis=1), jnp.concatenate([top_o, top_g], axis=1)
+    low, top = lax.optimization_barrier((low, top))
     low, top = lax.ppermute(low, "y", DOWN), lax.ppermute(top, "y", UP)
     low, top = lax.optimization_barrier((low, top))
-    return jnp.concatenate([own[:half] + up[:half] + low, own[half:] + down[:half] + top])
+    return join(out, grad, down_o, up_o, down_g, up_g, low, top)
+
+
+def join_kernel(out, grad, down_o, up_o, down_g, up_g, low, top, joined):
+    half, width = low.shape[0], out.shape[1]
+    for k, (parts, down, up) in enumerate(((out, down_o, up_o), (grad, down_g, up_g))):
+        columns = pl.ds(k * width, width)
+        joined[:half, 0, columns] = parts[:half, :] + up[:half, :] + low[:, columns]
+        joined[half:, 0, columns] = parts[half : 2 * half, :] + down[:half, :] + top[:, columns]
+
+
+def join(*pieces):
+    n, width = pieces[2].shape
+    return pl.pallas_call(
+        join_kernel,
+        out_shape=jax.ShapeDtypeStruct((n, 1, 2 * width), jnp.float32),
+        compiler_params=pltpu.CompilerParams(vmem_limit_bytes=24 * 2**20),
+        name="join",
+    )(*pieces)
 
 
 def sum_axis(block, axis):
@@ -83,30 +108,12 @@
     ]
 
 
-def route_kernel(
-    tokens_hbm, cotangent_hbm, router_ref, sent_ref, dispatch_ref, combine_ref, tokens_ref, cotangent_ref, sems
-):
+def route_kernel(tokens_ref, cotangent_ref, router_ref, sent_ref, dispatch_ref, combine_ref):
     e, d = router_ref.shape
-    first = fetch(tokens_hbm, tokens_ref, sems.at[0])
-    second = fetch(cotangent_hbm, cotangent_ref, sems.at[1])
-    for copy in first + second:
-        copy.start()
-    half = tokens_ref.shape[0] // 2
-    parts = []
-    for k in range(2):
-        for copy in first[k * PIECES // 2 : (k + 1) * PIECES // 2]:
-            copy.wait()
-        parts.append(
-            lax.dot_general(
-                router_ref[...],
-                tokens_ref[k * half : (k + 1) * half, :],
-                (((1,), (1,)), ((), ())),
-                precision=highest,
-                preferred_element_type=jnp.float32,
-            )
-        )
-    logits = jnp.concatenate(parts, axis=1)
     tokens = tokens_ref[...]
+    logits = lax.dot_general(
+        router_ref[...], tokens, (((1,), (1,)), ((), ())), precision=highest, preferred_element_type=jnp.float32
+    )
     by_token = jnp.exp(logits - jnp.max(logits, axis=1, keepdims=True))
     dispatch = by_token / jnp.sum(by_token, axis=1, keepdims=True)
     by_expert = jnp.exp(logits - jnp.max(logits, axis=0, keepdims=True))
@@ -114,8 +121,6 @@
     dispatch_ref[...] = dispatch
     combine_ref[...] = combine
     slot_in = dot3(split(dispatch), split(tokens), ((1,), (0,)))
-    for copy in second:
-        copy.wait()
     d_slot_out = dot3(split(combine), split(cotangent_ref[...]), ((1,), (0,)))
     for k in range(4):
         sent_ref[k * e : (k + 1) * e, 0, :d] = slot_in
@@ -133,17 +138,7 @@
             jax.ShapeDtypeStruct((e, p), f32),
             jax.ShapeDtypeStruct((e, p), f32),
         ),
-        in_specs=[
-            pl.BlockSpec(memory_space=pltpu.HBM),
-            pl.BlockSpec(memory_space=pltpu.HBM),
-            pl.BlockSpec(memory_space=pltpu.VMEM),
-        ],
-        scratch_shapes=[
-            pltpu.VMEM((p, d), f32),
-            pltpu.VMEM((p, d), f32),
-            pltpu.SemaphoreType.DMA((2, PIECES)),
-        ],
-        compiler_params=pltpu.CompilerParams(vmem_limit_bytes=56 * 2**20),
+        compiler_params=pltpu.CompilerParams(vmem_limit_bytes=24 * 2**20),
         name="route",
     )(tokens, cotangent, router_t)
 
@@ -209,10 +204,10 @@
     d_pre = gelu_pull(d_hidden)[0]
     part_out = jnp.einsum("rh,hd->rd", hidden, w_out, precision=high)
     part_grad = jnp.einsum("rh,dh->rd", d_pre, w_in, precision=high)
-    summed = jnp.concatenate([scatter_y(part_out), scatter_y(part_grad)], axis=1)
+    summed = scatter_both(part_out, part_grad)
     grad_w_out = jnp.einsum("rh,rd->hd", hidden, dy, precision=high)
     grad_w_in = jnp.einsum("rd,rh->dh", x, d_pre, precision=high)
-    back = lax.all_to_all(summed.reshape(4 * n_exp, 1, 2 * width), ZEX, 0, 0, tiled=True)
+    back = lax.all_to_all(summed, ZEX, 0, 0, tiled=True)
     halves = tokens, cotangent
     back, grad_w_in, grad_w_out = lax.optimization_barrier((back, grad_w_in, grad_w_out))
     local_router, weights, d_slot_in = finish(back, halves, dispatch, combine)

time: 158 us -> 158 us (level)
  starting transfers between devices: 49.4 us -> 44.6 us
  waiting for transfers between devices: 47.4 us -> 51.9 us
  local copies, waits for them, and re-layouts: 4.66 us -> 7 us
  Pallas kernels: 9.27 us -> 7.03 us
    ppermute x8 -> x6, waiting for transfers between devices: 10.8 us -> 15.6 us  [the longest x2 7.97 us: send_first(): up = lax.ppermute(jnp.concatenate([above[:half], far[half:]]), 'y', UP)]
    unnamed x27 -> x29, local copies, waits for them, and re-layouts: 2.32 us -> 5.97 us
    pallas_call x1, Pallas kernels: 6.26 us -> 2.96 us  [route(): pl.pallas_call(route_kernel, out_shape=(jax.ShapeDtypeStruct((4 * e, 1, 2...]
    all_to_all x1, starting transfers between devices: 11.9 us -> 9.27 us  [on_device(): back = lax.all_to_all(summed, ZEX, 0, 0, tiled=True)]
    ppermute x8 -> x6, starting transfers between devices: 10.7 us -> 8.4 us  [the longest x2 5.35 us: send_first(): down = lax.ppermute(jnp.concatenate([below[half:], far[:half]]), 'y', DOWN)]
  transfers between devices with their start and end apart: 26 -> 24, of which waited for: 17 -> 16; matrix products, arithmetic and copies ran while one was open for 8% -> 7% of each run, Pallas kernels for 0% -> 0%
where the time goes in v4:
time: 158 us; the launch traced here: 157 us
  waiting for transfers between devices  51.9 us (33%)
  starting transfers between devices  44.6 us (28%)
  blocking collectives  33.1 us (21%)
  matrix products  11.4 us (7%)
  Pallas kernels  7.03 us (4%)
  local copies, waits for them, and re-layouts  7 us (4%)
    all_to_all x1, blocking collectives, on_device(): lax.all_to_all(sent, ZEX, 0, 0, tiled=True).reshape(4 * n_exp, 2 * width)  33.1 us
    all_to_all x1, waiting for transfers between devices, on_device(): back = lax.all_to_all(summed, ZEX, 0, 0, tiled=True)  15.1 us
    all_to_all x1, starting transfers between devices, on_device(): back = lax.all_to_all(summed, ZEX, 0, 0, tiled=True)  9.27 us
    ppermute x2, waiting for transfers between devices, gather_y(): from_below = lax.ppermute(block, 'y', UP)  8.89 us
    ppermute x2, waiting for transfers between devices, send_first(): up = lax.ppermute(jnp.concatenate([above[:half], far[half:]]), 'y', UP)  7.97 us
    ppermute x2, waiting for transfers between devices, scatter_both(): low, top = (lax.ppermute(low, 'y', DOWN), lax.ppermute(top, 'y', UP))  7.58 us
    unnamed x29, local copies, waits for them, and re-layouts  5.97 us
    ppermute x6, starting transfers between devices, sum_axis(): lax.ppermute(block, axis, [(i, (i + k) % 4) for i in range(4)])  5.93 us
  transfers between devices with their start and end apart: 24, of which 16 were waited for; matrix products, arithmetic and copies ran while one was open for 7% of the time, Pallas kernels for 0%

profile of v4, /device:TPU:1, one launch (start us, length us, event | category | flops | bytes accessed | tf_op | source)
XLA Modules:
  0.0 157.1 jit_solution(6691744483789801880)
XLA Ops:
  0.6 0.0 copy-start
  0.6 0.0 copy-start.1
  0.7 1.4 copy-done.1
  2.1 1.3 copy-done.3
  3.4 0.9 copy-done.5
  4.3 3.0 %route.1 = (f32[64,1,2560]{2,1,0:T(1,128)S(1)}, f32[16,256]{1,0:T(8,128)S(1)}, f32[16,256]{1,0:T(8,128)S(1)}) custom-call(f32[256,1280]{1,0:T(8,128)S(1)} %bitcast.30, f32[256,1280]{1,0:T(8,128)S(1)} %bitcast.32, f32[16,1280]{1,0:T(8,128)S(1)} %bitcast.34), custom_call_target="tpu_custom_call" | custom-call | tf_op jit(solution)/shard_map/route/pallas_call | solution.py:134
  7.3 33.1 %all_to_all.15 = f32[64,1,2560]{2,1,0:T(1,128)S(1)} all-to-all(f32[64,1,2560]{2,1,0:T(1,128)S(1)} %get-tuple-element.23), channel_id=1, replica_groups=mesh['zl'=4,'y'=4,'zh'=2,'x'=4,'c'=2] {'zl','zh','x','c'}, dimensions={0} | all-to-all | bytes 1310720 | tf_op jit(solution)/shard_map/all_to_all | solution.py:198
  40.5 0.1 fusion.33
  40.6 1.4 collective-permute-start
  41.9 1.5 collective-permute-start.1
  43.5 2.7 %collective-permute-start.5 = (f32[64,1280]{1,0:T(8,128)S(1)}, f32[64,1280]{1,0:T(8,128)S(1)}, u32[]{:S(2)}, u32[]{:S(2)}) collective-permute-start(f32[64,1280]{1,0:T(8,128)S(1)} %get-tuple-element.54), channel_id=1, source_target_pairs={{0,48},{16,0},{32,16},{48,32},{1,49},{17,1},{33,17},{49,33},{2,50}... | collective-permute-start | bytes 983048 | tf_op jit(solution)/shard_map/ppermute | solution.py:22
  46.1 4.7 %collective-permute-done = f32[64,1280]{1,0:T(8,128)S(1)} collective-permute-done((f32[64,1280]{1,0:T(8,128)S(1)}, f32[64,1280]{1,0:T(8,128)S(1)}, u32[]{:S(2)}, u32[]{:S(2)}) %collective-permute-start) | collective-permute-done | bytes 327712 | tf_op jit(solution)/shard_map/ppermute | solution.py:21
  50.9 0.1 collective-permute-start.2
  51.0 2.7 %collective-permute-start.3 = (f32[32,1280]{1,0:T(8,128)S(1)}, f32[32,1280]{1,0:T(8,128)S(1)}, u32[]{:S(2)}, u32[]{:S(2)}) collective-permute-start(f32[32,1280]{1,0:T(8,128)S(1)} %slice.116), channel_id=1, source_target_pairs={{0,48},{16,0},{32,16},{48,32},{1,49},{17,1},{33,17},{49,33},{2,50}... | collective-permute-start | bytes 491528 | tf_op jit(solution)/shard_map/ppermute | solution.py:24
  53.7 4.2 %collective-permute-done.4 = f32[64,1280]{1,0:T(8,128)S(1)} collective-permute-done((f32[64,1280]{1,0:T(8,128)S(1)}, f32[64,1280]{1,0:T(8,128)S(1)}, u32[]{:S(2)}, u32[]{:S(2)}) %collective-permute-start.4) | collective-permute-done | bytes 327712 | tf_op jit(solution)/shard_map/ppermute | solution.py:21
  57.9 0.1 collective-permute-start.6
  58.0 2.7 %collective-permute-start.7 = (f32[32,1280]{1,0:T(8,128)S(1)}, f32[32,1280]{1,0:T(8,128)S(1)}, u32[]{:S(2)}, u32[]{:S(2)}) collective-permute-start(f32[32,1280]{1,0:T(8,128)S(1)} %slice.119), channel_id=1, source_target_pairs={{0,48},{16,0},{32,16},{48,32},{1,49},{17,1},{33,17},{49,33},{2,50}... | collective-permute-start | bytes 491528 | tf_op jit(solution)/shard_map/ppermute | solution.py:24
  60.8 0.0 copy-start.9
  60.9 0.5 collective-permute-done.2
  61.5 0.8 copy-done.9
  62.2 0.9 fusion.6
  63.1 1.3 fusion.2.out
  64.5 0.4 collective-permute-start.9
  65.0 2.6 %collective-permute-start.8 = (f32[64,1280]{1,0:T(8,128)S(1)}, f32[64,1280]{1,0:T(8,128)S(1)}, u32[]{:S(2)}, u32[]{:S(2)}) collective-permute-start(f32[64,1280]{1,0:T(8,128)S(1)} %pad_maximum_fusion), channel_id=1, source_target_pairs={{0,48},{16,0},{32,16},{48,32},{1,49},{17,1},{33,17},{49,33},{2,50}... | collective-permute-start | bytes 983048 | tf_op jit(solution)/shard_map/ppermute | solution.py:32
  67.6 0.0 copy-start.7
  67.6 1.0 fusion.13
  68.6 0.1 copy-done.7
  68.7 1.3 fusion.4.grad
  70.0 0.1 collective-permute-start.11
  70.2 2.7 %collective-permute-start.10 = (f32[64,1280]{1,0:T(8,128)S(1)}, f32[64,1280]{1,0:T(8,128)S(1)}, u32[]{:S(2)}, u32[]{:S(2)}) collective-permute-start(f32[64,1280]{1,0:T(8,128)S(1)} %pad_maximum_fusion.2), channel_id=1, source_target_pairs={{0,48},{16,0},{32,16},{48,32},{1,49},{17,1},{33,17},{49,33},{2,50}... | collective-permute-start | bytes 983048 | tf_op jit(solution)/shard_map/ppermute | solution.py:32
  72.9 8.0 %collective-permute-done.11.up_g = f32[64,1280]{1,0:T(8,128)S(1)} collective-permute-done((f32[64,1280]{1,0:T(8,128)S(1)}, f32[64,1280]{1,0:T(8,128)S(1)}, u32[]{:S(2)}, u32[]{:S(2)}) %collective-permute-start.11) | collective-permute-done | bytes 327712 | tf_op jit(solution)/shard_map/ppermute | solution.py:33
  81.0 2.6 %collective-permute-start.12 = (f32[32,2560]{1,0:T(8,128)S(1)}, f32[32,2560]{1,0:T(8,128)S(1)}, u32[]{:S(2)}, u32[]{:S(2)}) collective-permute-start(f32[32,2560]{1,0:T(8,128)S(1)} %get-tuple-element.28), channel_id=1, source_target_pairs={{0,48},{16,0},{32,16},{48,32},{1,49},{17,1},{33,17},{49,33},{2,50}... | collective-permute-start | bytes 983048 | tf_op jit(solution)/shard_map/ppermute | solution.py:43
  83.6 4.4 %collective-permute-done.12.low = f32[32,2560]{1,0:T(8,128)S(1)} collective-permute-done((f32[32,2560]{1,0:T(8,128)S(1)}, f32[32,2560]{1,0:T(8,128)S(1)}, u32[]{:S(2)}, u32[]{:S(2)}) %collective-permute-start.12) | collective-permute-done | bytes 327712 | tf_op jit(solution)/shard_map/ppermute | solution.py:43
  88.0 3.1 %collective-permute-done.13.top = f32[32,2560]{1,0:T(8,128)S(1)} collective-permute-done((f32[32,2560]{1,0:T(8,128)S(1)}, f32[32,2560]{1,0:T(8,128)S(1)}, u32[]{:S(2)}, u32[]{:S(2)}) %collective-permute-start.13) | collective-permute-done | bytes 327712 | tf_op jit(solution)/shard_map/ppermute | solution.py:43
  91.2 1.1 join.1
  92.2 9.3 %all-to-all-start.1 = ((f32[64,1,2560]{2,1,0:T(1,128)}), f32[64,1,2560]{2,1,0:T(1,128)}, u32[]{:S(2)}, u32[]{:S(2)}) async-start(f32[64,1,2560]{2,1,0:T(1,128)} %join.1), calls=%async_computation.1 | async-start | bytes 1310720 | tf_op jit(solution)/shard_map/all_to_all | solution.py:210
  101.5 0.0 copy-start.8
  101.5 3.1 %fusion.34 = f32[1280,320]{0,1:T(8,128)} fusion(f32[256,1280]{1,0:T(8,128)S(1)} %constant_dynamic-update-slice_fusion, f32[256,320]{0,1:T(8,128)} %copy-done.10), kind=kOutput, calls=%fused_computation.61 | convolution fusion | flops 629145600 | bytes 3276800 | tf_op jit(solution)/shard_map/rd,rh->dh/dot_general | solution.py:209
  104.6 2.1 %fusion.20 = f32[320,1280]{1,0:T(8,128)} fusion(f32[256,1280]{1,0:T(8,128)S(1)} %copy-done.8, f32[256,320]{0,1:T(8,128)S(1)} %fusion.6), kind=kOutput, calls=%fused_computation.32 | convolution fusion | flops 629800960 | bytes 3276800 | tf_op jit(solution)/shard_map/rh,rd->hd/dot_general | solution.py:208
  106.7 15.1 %all-to-all-done.1.back_hbm = f32[64,1,2560]{2,1,0:T(1,128)} async-done(((f32[64,1,2560]{2,1,0:T(1,128)}), f32[64,1,2560]{2,1,0:T(1,128)}, u32[]{:S(2)}, u32[]{:S(2)}) %all-to-all-start.1) | async-done | bytes 655392 | tf_op jit(solution)/shard_map/all_to_all | solution.py:210
  121.8 1.3 copy-done.4
  123.1 3.0 %finish.1 = (f32[16,1280]{1,0:T(8,128)S(1)}, f32[32,256]{1,0:T(8,128)S(1)}, f32[16,1280]{1,0:T(8,128)S(1)}) custom-call(f32[64,1,2560]{2,1,0:T(1,128)} %all-to-all-done.1.back_hbm, f32[256,1280]{1,0:T(8,128)S(1)} %bitcast.31, f32[256,1280]{1,0:T(8,128)S(1)} %bitcast.33, f32[16,256]{1,0:T(8,128)S(1)} %get-tuple-element.33.dispatch_ref, ...), custom_call_target="tpu_custom_call" | custom-call | tf_op jit(solution)/shard_map/finish/pallas_call | solution.py:177
  126.2 0.0 copy-start.6
  126.2 0.5 collective-permute-start.14
  126.7 0.9 collective-permute-done.14
  127.5 0.5 collective-permute-start.15
  128.0 1.7 %collective-permute-start.16 = (f32[8,1280]{1,0:T(8,128)S(1)}, f32[8,1280]{1,0:T(8,128)S(1)}, u32[]{:S(2)}, u32[]{:S(2)}) collective-permute-start(f32[8,1280]{1,0:T(8,128)S(1)} %select_add_fusion), channel_id=1, source_target_pairs={{0,4},{2,6},{4,0},{6,2},{1,5},{3,7},{5,1},{7,3},{8,12},{10,14},{12... | collective-permute-start | bytes 122888 | tf_op jit(solution)/shard_map/ppermute | solution.py:69
  129.7 1.0 collective-permute-start.17
  130.7 1.0 collective-permute-done.15
  131.7 0.7 collective-permute-done.16
  132.4 0.6 collective-permute-done.17
  133.0 0.1 collective-permute-start.18
  133.1 1.2 collective-permute-start.19
  134.3 1.5 collective-permute-start.20
  135.8 1.4 collective-permute-done.18
  137.2 0.6 collective-permute-done.19
  137.8 0.4 collective-permute-done.20
  138.2 0.8 broadcast_in_dim.15
  139.0 4.0 %all-to-all-start.2 = ((f32[8,8,1280]{2,1,0:T(8,128)}), f32[8,8,1280]{2,1,0:T(8,128)S(1)}, u32[]{:S(2)}, u32[]{:S(2)}) async-start(f32[8,8,1280]{2,1,0:T(8,128)} %broadcast_in_dim.15), calls=%async_computation.2 | async-start | bytes 655360 | tf_op jit(solution)/shard_map/all_to_all | solution.py:81
  142.9 1.8 %fusion.16 = f32[256,1280]{1,0:T(8,128)} fusion(f32[32,256]{1,0:T(8,128)S(1)} %get-tuple-element.36, f32[16,1280]{1,0:T(8,128)S(1)} %bitcast.35, f32[16,1280]{1,0:T(8,128)S(1)} %get-tuple-element.37), kind=kOutput, calls=%fused_computation.28 | convolution fusion | flops 62955520 | bytes 1507328 | tf_op jit(solution)/shard_map/kp,kd->pd/dot_general | solution.py:215
  144.7 5.4 %all-to-all-done.2 = f32[8,8,1280]{2,1,0:T(8,128)S(1)} async-done(((f32[8,8,1280]{2,1,0:T(8,128)}), f32[8,8,1280]{2,1,0:T(8,128)S(1)}, u32[]{:S(2)}, u32[]{:S(2)}) %all-to-all-start.2) | async-done | bytes 327712 | tf_op jit(solution)/shard_map/all_to_all | solution.py:81
  150.2 5.4 %collective-permute-start.21 = (f32[8,1280]{1,0:T(8,128)S(1)}, f32[8,1280]{1,0:T(8,128)S(1)}, u32[]{:S(2)}, u32[]{:S(2)}) collective-permute-start(f32[8,1280]{1,0:T(8,128)S(1)} %reduce_sum.9), channel_id=1, source_target_pairs={{0,1},{1,0},{2,3},{3,2},{4,5},{5,4},{6,7},{7,6},{8,9},{9,8},{10,11... | collective-permute-start | bytes 122888 | tf_op jit(solution)/shard_map/ppermute | solution.py:83
  155.6 0.9 collective-permute-done.21
  156.4 0.6 fusion.21
  (47 shorter events, 0.7 us)
Async XLA Ops:
  0.6 62.5 %copy-start = (f32[1,320,1280]{2,1,0:T(8,128)S(1)}, f32[1,320,1280]{2,1,0:T(8,128)}, u32[]{:S(2)}) copy-start(f32[1,320,1280]{2,1,0:T(8,128)} %param.8) | copy-start | bytes 4915204
  0.6 1.4 copy-start.1
  2.1 1.3 copy-start.3
  3.4 0.9 copy-start.5
  40.6 10.3 %collective-permute-start = (f32[64,1280]{1,0:T(8,128)S(1)}, f32[64,1280]{1,0:T(8,128)S(1)}, u32[]{:S(2)}, u32[]{:S(2)}) collective-permute-start(f32[64,1280]{1,0:T(8,128)S(1)} %get-tuple-element.57), channel_id=1, source_target_pairs={{0,16},{16,32},{32,48},{48,0},{1,17},{17,33},{33,49},{49,1},{2,18}... | collective-permute-start | bytes 983048 | tf_op jit(solution)/shard_map/ppermute | solution.py:21
  41.9 9.1 %collective-permute-start.1 = (f32[64,1280]{1,0:T(8,128)S(1)}, f32[64,1280]{1,0:T(8,128)S(1)}, u32[]{:S(2)}, u32[]{:S(2)}) collective-permute-start(f32[64,1280]{1,0:T(8,128)S(1)} %get-tuple-element.57), channel_id=1, source_target_pairs={{0,48},{16,0},{32,16},{48,32},{1,49},{17,1},{33,17},{49,33},{2,50}... | collective-permute-start | bytes 983048 | tf_op jit(solution)/shard_map/ppermute | solution.py:22
  43.5 14.4 %collective-permute-start.4 = (f32[64,1280]{1,0:T(8,128)S(1)}, f32[64,1280]{1,0:T(8,128)S(1)}, u32[]{:S(2)}, u32[]{:S(2)}) collective-permute-start(f32[64,1280]{1,0:T(8,128)S(1)} %get-tuple-element.54), channel_id=1, source_target_pairs={{0,16},{16,32},{32,48},{48,0},{1,17},{17,33},{33,49},{49,1},{2,18}... | collective-permute-start | bytes 983048 | tf_op jit(solution)/shard_map/ppermute | solution.py:21
  43.5 14.5 %collective-permute-start.5 = (f32[64,1280]{1,0:T(8,128)S(1)}, f32[64,1280]{1,0:T(8,128)S(1)}, u32[]{:S(2)}, u32[]{:S(2)}) collective-permute-start(f32[64,1280]{1,0:T(8,128)S(1)} %get-tuple-element.54), channel_id=1, source_target_pairs={{0,48},{16,0},{32,16},{48,32},{1,49},{17,1},{33,17},{49,33},{2,50}... | collective-permute-start | bytes 983048 | tf_op jit(solution)/shard_map/ppermute | solution.py:22
  50.9 10.5 %collective-permute-start.2 = (f32[32,1280]{1,0:T(8,128)S(1)}, f32[32,1280]{1,0:T(8,128)S(1)}, u32[]{:S(2)}, u32[]{:S(2)}) collective-permute-start(f32[32,1280]{1,0:T(8,128)S(1)} %slice.115), channel_id=1, source_target_pairs={{0,16},{16,32},{32,48},{48,0},{1,17},{17,33},{33,49},{49,1},{2,18}... | collective-permute-start | bytes 491528 | tf_op jit(solution)/shard_map/ppermute | solution.py:23
  51.0 10.4 %collective-permute-start.3 = (f32[32,1280]{1,0:T(8,128)S(1)}, f32[32,1280]{1,0:T(8,128)S(1)}, u32[]{:S(2)}, u32[]{:S(2)}) collective-permute-start(f32[32,1280]{1,0:T(8,128)S(1)} %slice.116), channel_id=1, source_target_pairs={{0,48},{16,0},{32,16},{48,32},{1,49},{17,1},{33,17},{49,33},{2,50}... | collective-permute-start | bytes 491528 | tf_op jit(solution)/shard_map/ppermute | solution.py:24
  57.9 9.7 %collective-permute-start.6 = (f32[32,1280]{1,0:T(8,128)S(1)}, f32[32,1280]{1,0:T(8,128)S(1)}, u32[]{:S(2)}, u32[]{:S(2)}) collective-permute-start(f32[32,1280]{1,0:T(8,128)S(1)} %slice.118), channel_id=1, source_target_pairs={{0,16},{16,32},{32,48},{48,0},{1,17},{17,33},{33,49},{49,1},{2,18}... | collective-permute-start | bytes 491528 | tf_op jit(solution)/shard_map/ppermute | solution.py:23
  58.0 9.5 %collective-permute-start.7 = (f32[32,1280]{1,0:T(8,128)S(1)}, f32[32,1280]{1,0:T(8,128)S(1)}, u32[]{:S(2)}, u32[]{:S(2)}) collective-permute-start(f32[32,1280]{1,0:T(8,128)S(1)} %slice.119), channel_id=1, source_target_pairs={{0,48},{16,0},{32,16},{48,32},{1,49},{17,1},{33,17},{49,33},{2,50}... | collective-permute-start | bytes 491528 | tf_op jit(solution)/shard_map/ppermute | solution.py:24
  60.8 1.4 copy-start.9
  64.5 8.4 %collective-permute-start.9 = (f32[64,1280]{1,0:T(8,128)S(1)}, f32[64,1280]{1,0:T(8,128)S(1)}, u32[]{:S(2)}, u32[]{:S(2)}) collective-permute-start(f32[64,1280]{1,0:T(8,128)S(1)} %pad_maximum_fusion.1), channel_id=1, source_target_pairs={{0,16},{16,32},{32,48},{48,0},{1,17},{17,33},{33,49},{49,1},{2,18}... | collective-permute-start | bytes 983048 | tf_op jit(solution)/shard_map/ppermute | solution.py:33
  65.0 8.0 %collective-permute-start.8 = (f32[64,1280]{1,0:T(8,128)S(1)}, f32[64,1280]{1,0:T(8,128)S(1)}, u32[]{:S(2)}, u32[]{:S(2)}) collective-permute-start(f32[64,1280]{1,0:T(8,128)S(1)} %pad_maximum_fusion), channel_id=1, source_target_pairs={{0,48},{16,0},{32,16},{48,32},{1,49},{17,1},{33,17},{49,33},{2,50}... | collective-permute-start | bytes 983048 | tf_op jit(solution)/shard_map/ppermute | solution.py:32
  67.6 1.1 copy-start.7
  68.7 12.3 %copy-start.10 = (f32[256,320]{0,1:T(8,128)}, f32[256,320]{0,1:T(8,128)S(1)}, u32[]{:S(2)}) copy-start(f32[256,320]{0,1:T(8,128)S(1)} %fusion.13) | copy-start | bytes 983044
  70.0 10.8 %collective-permute-start.11 = (f32[64,1280]{1,0:T(8,128)S(1)}, f32[64,1280]{1,0:T(8,128)S(1)}, u32[]{:S(2)}, u32[]{:S(2)}) collective-permute-start(f32[64,1280]{1,0:T(8,128)S(1)} %pad_maximum_fusion.3), channel_id=1, source_target_pairs={{0,16},{16,32},{32,48},{48,0},{1,17},{17,33},{33,49},{49,1},{2,18}... | collective-permute-start | bytes 983048 | tf_op jit(solution)/shard_map/ppermute | solution.py:33
  70.2 10.7 %collective-permute-start.10 = (f32[64,1280]{1,0:T(8,128)S(1)}, f32[64,1280]{1,0:T(8,128)S(1)}, u32[]{:S(2)}, u32[]{:S(2)}) collective-permute-start(f32[64,1280]{1,0:T(8,128)S(1)} %pad_maximum_fusion.2), channel_id=1, source_target_pairs={{0,48},{16,0},{32,16},{48,32},{1,49},{17,1},{33,17},{49,33},{2,50}... | collective-permute-start | bytes 983048 | tf_op jit(solution)/shard_map/ppermute | solution.py:32
  81.0 7.0 %collective-permute-start.12 = (f32[32,2560]{1,0:T(8,128)S(1)}, f32[32,2560]{1,0:T(8,128)S(1)}, u32[]{:S(2)}, u32[]{:S(2)}) collective-permute-start(f32[32,2560]{1,0:T(8,128)S(1)} %get-tuple-element.28), channel_id=1, source_target_pairs={{0,48},{16,0},{32,16},{48,32},{1,49},{17,1},{33,17},{49,33},{2,50}... | collective-permute-start | bytes 983048 | tf_op jit(solution)/shard_map/ppermute | solution.py:43
  83.6 7.6 %collective-permute-start.13 = (f32[32,2560]{1,0:T(8,128)S(1)}, f32[32,2560]{1,0:T(8,128)S(1)}, u32[]{:S(2)}, u32[]{:S(2)}) collective-permute-start(f32[32,2560]{1,0:T(8,128)S(1)} %get-tuple-element.29), channel_id=1, source_target_pairs={{0,16},{16,32},{32,48},{48,0},{1,17},{17,33},{33,49},{49,1},{2,18}... | collective-permute-start | bytes 983048 | tf_op jit(solution)/shard_map/ppermute | solution.py:43
  92.2 29.6 %all-to-all-start.1 = ((f32[64,1,2560]{2,1,0:T(1,128)}), f32[64,1,2560]{2,1,0:T(1,128)}, u32[]{:S(2)}, u32[]{:S(2)}) async-start(f32[64,1,2560]{2,1,0:T(1,128)} %join.1), calls=%async_computation.1 | async-start | bytes 1310720 | tf_op jit(solution)/shard_map/all_to_all | solution.py:210
  101.5 3.1 %copy-start.8 = (f32[256,1280]{1,0:T(8,128)S(1)}, f32[256,1280]{1,0:T(8,128)}, u32[]{:S(2)}) copy-start(f32[256,1280]{1,0:T(8,128)} %copy-done.7) | copy-start | bytes 3932164
  104.6 17.2 %copy-start.2 = (f32[1,256,1280]{2,1,0:T(8,128)S(1)}, f32[1,256,1280]{2,1,0:T(8,128)}, u32[]{:S(2)}) copy-start(f32[1,256,1280]{2,1,0:T(8,128)} %param.5) | copy-start | bytes 3932164
  121.8 1.3 copy-start.4
  126.2 16.8 %copy-start.6 = (f32[1280,16]{0,1:T(8,128)S(1)}, f32[1280,16]{0,1:T(8,128)}, u32[]{:S(2)}) copy-start(f32[1280,16]{0,1:T(8,128)} %param.6) | copy-start | bytes 245764
  126.2 1.4 collective-permute-start.14
  127.5 4.1 %collective-permute-start.15 = (f32[8,1280]{1,0:T(8,128)S(1)}, f32[8,1280]{1,0:T(8,128)S(1)}, u32[]{:S(2)}, u32[]{:S(2)}) collective-permute-start(f32[8,1280]{1,0:T(8,128)S(1)} %select_add_fusion), channel_id=1, source_target_pairs={{0,2},{2,4},{4,6},{6,0},{1,3},{3,5},{5,7},{7,1},{8,10},{10,12},{12... | collective-permute-start | bytes 122888 | tf_op jit(solution)/shard_map/ppermute | solution.py:69
  128.0 4.4 %collective-permute-start.16 = (f32[8,1280]{1,0:T(8,128)S(1)}, f32[8,1280]{1,0:T(8,128)S(1)}, u32[]{:S(2)}, u32[]{:S(2)}) collective-permute-start(f32[8,1280]{1,0:T(8,128)S(1)} %select_add_fusion), channel_id=1, source_target_pairs={{0,4},{2,6},{4,0},{6,2},{1,5},{3,7},{5,1},{7,3},{8,12},{10,14},{12... | collective-permute-start | bytes 122888 | tf_op jit(solution)/shard_map/ppermute | solution.py:69
  129.7 3.3 %collective-permute-start.17 = (f32[8,1280]{1,0:T(8,128)S(1)}, f32[8,1280]{1,0:T(8,128)S(1)}, u32[]{:S(2)}, u32[]{:S(2)}) collective-permute-start(f32[8,1280]{1,0:T(8,128)S(1)} %select_add_fusion), channel_id=1, source_target_pairs={{0,6},{2,0},{4,2},{6,4},{1,7},{3,1},{5,3},{7,5},{8,14},{10,8},{12,... | collective-permute-start | bytes 122888 | tf_op jit(solution)/shard_map/ppermute | solution.py:69
  133.0 4.2 %collective-permute-start.18 = (f32[8,1280]{1,0:T(8,128)S(1)}, f32[8,1280]{1,0:T(8,128)S(1)}, u32[]{:S(2)}, u32[]{:S(2)}) collective-permute-start(f32[8,1280]{1,0:T(8,128)S(1)} %add_add_fusion.1), channel_id=1, source_target_pairs={{0,16},{16,32},{32,48},{48,0},{1,17},{17,33},{33,49},{49,1},{2,18}... | collective-permute-start | bytes 122888 | tf_op jit(solution)/shard_map/ppermute | solution.py:69
  133.1 4.6 %collective-permute-start.19 = (f32[8,1280]{1,0:T(8,128)S(1)}, f32[8,1280]{1,0:T(8,128)S(1)}, u32[]{:S(2)}, u32[]{:S(2)}) collective-permute-start(f32[8,1280]{1,0:T(8,128)S(1)} %add_add_fusion.1), channel_id=1, source_target_pairs={{0,32},{16,48},{32,0},{48,16},{1,33},{17,49},{33,1},{49,17},{2,34}... | collective-permute-start | bytes 122888 | tf_op jit(solution)/shard_map/ppermute | solution.py:69
  134.3 3.9 %collective-permute-start.20 = (f32[8,1280]{1,0:T(8,128)S(1)}, f32[8,1280]{1,0:T(8,128)S(1)}, u32[]{:S(2)}, u32[]{:S(2)}) collective-permute-start(f32[8,1280]{1,0:T(8,128)S(1)} %add_add_fusion.1), channel_id=1, source_target_pairs={{0,48},{16,0},{32,16},{48,32},{1,49},{17,1},{33,17},{49,33},{2,50}... | collective-permute-start | bytes 122888 | tf_op jit(solution)/shard_map/ppermute | solution.py:69
  139.0 11.2 %all-to-all-start.2 = ((f32[8,8,1280]{2,1,0:T(8,128)}), f32[8,8,1280]{2,1,0:T(8,128)S(1)}, u32[]{:S(2)}, u32[]{:S(2)}) async-start(f32[8,8,1280]{2,1,0:T(8,128)} %broadcast_in_dim.15), calls=%async_computation.2 | async-start | bytes 655360 | tf_op jit(solution)/shard_map/all_to_all | solution.py:81
  150.2 6.2 %collective-permute-start.21 = (f32[8,1280]{1,0:T(8,128)S(1)}, f32[8,1280]{1,0:T(8,128)S(1)}, u32[]{:S(2)}, u32[]{:S(2)}) collective-permute-start(f32[8,1280]{1,0:T(8,128)S(1)} %reduce_sum.9), channel_id=1, source_target_pairs={{0,1},{1,0},{2,3},{3,2},{4,5},{5,4},{6,7},{7,6},{8,9},{9,8},{10,11... | collective-permute-start | bytes 122888 | tf_op jit(solution)/shard_map/ppermute | solution.py:83

commit v5 on v4

--- a/solution.py
+++ b/solution.py
@@ -65,7 +65,7 @@
 
 def sum_axis(block, axis):
     total = block
-    for k in range(1, 4):
+    for k in (2, 1, 3):
         total = total + lax.ppermute(block, axis, [(i, (i + k) % 4) for i in range(4)])
     return total
 

time: 158 us -> 157 us (level)
  transfers between devices with their start and end apart: 24 -> 24, of which waited for: 16 -> 14; matrix products, arithmetic and copies ran while one was open for 7% -> 8% of each run, Pallas kernels for 0% -> 0%
where the time goes in v5:
time: 157 us
  waiting for transfers between devices  51.2 us (33%)
  starting transfers between devices  44.9 us (29%)
  blocking collectives  33.1 us (21%)
  matrix products  11.4 us (7%)
  Pallas kernels  7.03 us (4%)
  local copies, waits for them, and re-layouts  7 us (4%)
    all_to_all x1, blocking collectives, on_device(): lax.all_to_all(sent, ZEX, 0, 0, tiled=True).reshape(4 * n_exp, 2 * width)  33.1 us
    all_to_all x1, waiting for transfers between devices, on_device(): back = lax.all_to_all(summed, ZEX, 0, 0, tiled=True)  15.1 us
    all_to_all x1, starting transfers between devices, on_device(): back = lax.all_to_all(summed, ZEX, 0, 0, tiled=True)  9.27 us
    ppermute x2, waiting for transfers between devices, gather_y(): from_below = lax.ppermute(block, 'y', UP)  8.89 us
    ppermute x2, waiting for transfers between devices, send_first(): up = lax.ppermute(jnp.concatenate([above[:half], far[half:]]), 'y', UP)  7.97 us
    ppermute x2, waiting for transfers between devices, scatter_both(): low, top = (lax.ppermute(low, 'y', DOWN), lax.ppermute(top, 'y', UP))  7.58 us
    ppermute x6, starting transfers between devices, sum_axis(): lax.ppermute(block, axis, [(i, (i + k) % 4) for i in range(4)])  6.46 us
    unnamed x29, local copies, waits for them, and re-layouts  5.97 us
  transfers between devices with their start and end apart: 24, of which 14 were waited for; matrix products, arithmetic and copies ran while one was open for 8% of the time, Pallas kernels for 0%

profile of v5, /device:TPU:1, one launch (start us, length us, event | category | flops | bytes accessed | tf_op | source)
XLA Modules:
  0.0 156.6 jit_solution(11001091062002821935)
XLA Ops:
  0.6 0.0 copy-start
  0.6 0.0 copy-start.1
  0.7 1.4 copy-done.1
  2.1 1.3 copy-done.3
  3.4 0.9 copy-done.5
  4.3 3.0 %route.1 = (f32[64,1,2560]{2,1,0:T(1,128)S(1)}, f32[16,256]{1,0:T(8,128)S(1)}, f32[16,256]{1,0:T(8,128)S(1)}) custom-call(f32[256,1280]{1,0:T(8,128)S(1)} %bitcast.30, f32[256,1280]{1,0:T(8,128)S(1)} %bitcast.32, f32[16,1280]{1,0:T(8,128)S(1)} %bitcast.34), custom_call_target="tpu_custom_call" | custom-call | tf_op jit(solution)/shard_map/route/pallas_call | solution.py:134
  7.3 33.1 %all_to_all.15 = f32[64,1,2560]{2,1,0:T(1,128)S(1)} all-to-all(f32[64,1,2560]{2,1,0:T(1,128)S(1)} %get-tuple-element.23), channel_id=1, replica_groups=mesh['zl'=4,'y'=4,'zh'=2,'x'=4,'c'=2] {'zl','zh','x','c'}, dimensions={0} | all-to-all | bytes 1310720 | tf_op jit(solution)/shard_map/all_to_all | solution.py:198
  40.5 0.1 fusion.33
  40.6 1.4 collective-permute-start
  41.9 1.5 collective-permute-start.1
  43.5 2.7 %collective-permute-start.5 = (f32[64,1280]{1,0:T(8,128)S(1)}, f32[64,1280]{1,0:T(8,128)S(1)}, u32[]{:S(2)}, u32[]{:S(2)}) collective-permute-start(f32[64,1280]{1,0:T(8,128)S(1)} %get-tuple-element.54), channel_id=1, source_target_pairs={{0,48},{16,0},{32,16},{48,32},{1,49},{17,1},{33,17},{49,33},{2,50}... | collective-permute-start | bytes 983048 | tf_op jit(solution)/shard_map/ppermute | solution.py:22
  46.1 4.7 %collective-permute-done = f32[64,1280]{1,0:T(8,128)S(1)} collective-permute-done((f32[64,1280]{1,0:T(8,128)S(1)}, f32[64,1280]{1,0:T(8,128)S(1)}, u32[]{:S(2)}, u32[]{:S(2)}) %collective-permute-start) | collective-permute-done | bytes 327712 | tf_op jit(solution)/shard_map/ppermute | solution.py:21
  50.9 0.1 collective-permute-start.2
  51.0 0.0 collective-permute-done.1
  51.0 2.7 %collective-permute-start.3 = (f32[32,1280]{1,0:T(8,128)S(1)}, f32[32,1280]{1,0:T(8,128)S(1)}, u32[]{:S(2)}, u32[]{:S(2)}) collective-permute-start(f32[32,1280]{1,0:T(8,128)S(1)} %slice.116), channel_id=1, source_target_pairs={{0,48},{16,0},{32,16},{48,32},{1,49},{17,1},{33,17},{49,33},{2,50}... | collective-permute-start | bytes 491528 | tf_op jit(solution)/shard_map/ppermute | solution.py:24
  53.7 4.2 %collective-permute-done.4 = f32[64,1280]{1,0:T(8,128)S(1)} collective-permute-done((f32[64,1280]{1,0:T(8,128)S(1)}, f32[64,1280]{1,0:T(8,128)S(1)}, u32[]{:S(2)}, u32[]{:S(2)}) %collective-permute-start.4) | collective-permute-done | bytes 327712 | tf_op jit(solution)/shard_map/ppermute | solution.py:21
  57.9 0.1 collective-permute-start.6
  58.0 0.0 collective-permute-done.5
  58.0 2.7 %collective-permute-start.7 = (f32[32,1280]{1,0:T(8,128)S(1)}, f32[32,1280]{1,0:T(8,128)S(1)}, u32[]{:S(2)}, u32[]{:S(2)}) collective-permute-start(f32[32,1280]{1,0:T(8,128)S(1)} %slice.119), channel_id=1, source_target_pairs={{0,48},{16,0},{32,16},{48,32},{1,49},{17,1},{33,17},{49,33},{2,50}... | collective-permute-start | bytes 491528 | tf_op jit(solution)/shard_map/ppermute | solution.py:24
  60.8 0.0 copy-start.9
  60.9 0.5 collective-permute-done.2
  61.5 0.8 copy-done.9
  62.2 0.9 fusion.6
  63.1 1.3 fusion.2.out
  64.5 0.4 collective-permute-start.9
  65.0 2.6 %collective-permute-start.8 = (f32[64,1280]{1,0:T(8,128)S(1)}, f32[64,1280]{1,0:T(8,128)S(1)}, u32[]{:S(2)}, u32[]{:S(2)}) collective-permute-start(f32[64,1280]{1,0:T(8,128)S(1)} %pad_maximum_fusion), channel_id=1, source_target_pairs={{0,48},{16,0},{32,16},{48,32},{1,49},{17,1},{33,17},{49,33},{2,50}... | collective-permute-start | bytes 983048 | tf_op jit(solution)/shard_map/ppermute | solution.py:32
  67.6 0.0 copy-start.7
  67.6 1.0 fusion.13
  68.6 0.1 copy-done.7
  68.7 1.3 fusion.4.grad
  70.0 0.1 collective-permute-start.11
  70.2 2.7 %collective-permute-start.10 = (f32[64,1280]{1,0:T(8,128)S(1)}, f32[64,1280]{1,0:T(8,128)S(1)}, u32[]{:S(2)}, u32[]{:S(2)}) collective-permute-start(f32[64,1280]{1,0:T(8,128)S(1)} %pad_maximum_fusion.2), channel_id=1, source_target_pairs={{0,48},{16,0},{32,16},{48,32},{1,49},{17,1},{33,17},{49,33},{2,50}... | collective-permute-start | bytes 983048 | tf_op jit(solution)/shard_map/ppermute | solution.py:32
  72.9 8.0 %collective-permute-done.11.up_g = f32[64,1280]{1,0:T(8,128)S(1)} collective-permute-done((f32[64,1280]{1,0:T(8,128)S(1)}, f32[64,1280]{1,0:T(8,128)S(1)}, u32[]{:S(2)}, u32[]{:S(2)}) %collective-permute-start.11) | collective-permute-done | bytes 327712 | tf_op jit(solution)/shard_map/ppermute | solution.py:33
  81.0 2.6 %collective-permute-start.12 = (f32[32,2560]{1,0:T(8,128)S(1)}, f32[32,2560]{1,0:T(8,128)S(1)}, u32[]{:S(2)}, u32[]{:S(2)}) collective-permute-start(f32[32,2560]{1,0:T(8,128)S(1)} %get-tuple-element.28), channel_id=1, source_target_pairs={{0,48},{16,0},{32,16},{48,32},{1,49},{17,1},{33,17},{49,33},{2,50}... | collective-permute-start | bytes 983048 | tf_op jit(solution)/shard_map/ppermute | solution.py:43
  83.6 4.4 %collective-permute-done.12.low = f32[32,2560]{1,0:T(8,128)S(1)} collective-permute-done((f32[32,2560]{1,0:T(8,128)S(1)}, f32[32,2560]{1,0:T(8,128)S(1)}, u32[]{:S(2)}, u32[]{:S(2)}) %collective-permute-start.12) | collective-permute-done | bytes 327712 | tf_op jit(solution)/shard_map/ppermute | solution.py:43
  88.0 3.1 %collective-permute-done.13.top = f32[32,2560]{1,0:T(8,128)S(1)} collective-permute-done((f32[32,2560]{1,0:T(8,128)S(1)}, f32[32,2560]{1,0:T(8,128)S(1)}, u32[]{:S(2)}, u32[]{:S(2)}) %collective-permute-start.13) | collective-permute-done | bytes 327712 | tf_op jit(solution)/shard_map/ppermute | solution.py:43
  91.2 1.1 join.1
  92.2 9.3 %all-to-all-start.1 = ((f32[64,1,2560]{2,1,0:T(1,128)}), f32[64,1,2560]{2,1,0:T(1,128)}, u32[]{:S(2)}, u32[]{:S(2)}) async-start(f32[64,1,2560]{2,1,0:T(1,128)} %join.1), calls=%async_computation.1 | async-start | bytes 1310720 | tf_op jit(solution)/shard_map/all_to_all | solution.py:210
  101.5 0.0 copy-start.8
  101.5 3.1 %fusion.34 = f32[1280,320]{0,1:T(8,128)} fusion(f32[256,1280]{1,0:T(8,128)S(1)} %constant_dynamic-update-slice_fusion, f32[256,320]{0,1:T(8,128)} %copy-done.10), kind=kOutput, calls=%fused_computation.61 | convolution fusion | flops 629145600 | bytes 3276800 | tf_op jit(solution)/shard_map/rd,rh->dh/dot_general | solution.py:209
  104.6 2.1 %fusion.20 = f32[320,1280]{1,0:T(8,128)} fusion(f32[256,1280]{1,0:T(8,128)S(1)} %copy-done.8, f32[256,320]{0,1:T(8,128)S(1)} %fusion.6), kind=kOutput, calls=%fused_computation.32 | convolution fusion | flops 629800960 | bytes 3276800 | tf_op jit(solution)/shard_map/rh,rd->hd/dot_general | solution.py:208
  106.7 15.1 %all-to-all-done.1.back_hbm = f32[64,1,2560]{2,1,0:T(1,128)} async-done(((f32[64,1,2560]{2,1,0:T(1,128)}), f32[64,1,2560]{2,1,0:T(1,128)}, u32[]{:S(2)}, u32[]{:S(2)}) %all-to-all-start.1) | async-done | bytes 655392 | tf_op jit(solution)/shard_map/all_to_all | solution.py:210
  121.8 1.3 copy-done.4
  123.1 3.0 %finish.1 = (f32[16,1280]{1,0:T(8,128)S(1)}, f32[32,256]{1,0:T(8,128)S(1)}, f32[16,1280]{1,0:T(8,128)S(1)}) custom-call(f32[64,1,2560]{2,1,0:T(1,128)} %all-to-all-done.1.back_hbm, f32[256,1280]{1,0:T(8,128)S(1)} %bitcast.31, f32[256,1280]{1,0:T(8,128)S(1)} %bitcast.33, f32[16,256]{1,0:T(8,128)S(1)} %get-tuple-element.33.dispatch_ref, ...), custom_call_target="tpu_custom_call" | custom-call | tf_op jit(solution)/shard_map/finish/pallas_call | solution.py:177
  126.2 0.0 copy-start.6
  126.2 0.5 collective-permute-start.14
  126.7 0.9 collective-permute-done.14
  127.5 0.9 collective-permute-start.15
  128.5 0.7 collective-permute-start.16
  129.2 2.0 %collective-permute-start.17 = (f32[8,1280]{1,0:T(8,128)S(1)}, f32[8,1280]{1,0:T(8,128)S(1)}, u32[]{:S(2)}, u32[]{:S(2)}) collective-permute-start(f32[8,1280]{1,0:T(8,128)S(1)} %select_add_fusion), channel_id=1, source_target_pairs={{0,6},{2,0},{4,2},{6,4},{1,7},{3,1},{5,3},{7,5},{8,14},{10,8},{12,... | collective-permute-start | bytes 122888 | tf_op jit(solution)/shard_map/ppermute | solution.py:69
  131.2 0.8 collective-permute-done.15
  132.0 1.2 collective-permute-done.16
  133.2 0.1 collective-permute-start.18
  133.3 0.6 collective-permute-start.19
  133.9 2.2 %collective-permute-start.20 = (f32[8,1280]{1,0:T(8,128)S(1)}, f32[8,1280]{1,0:T(8,128)S(1)}, u32[]{:S(2)}, u32[]{:S(2)}) collective-permute-start(f32[8,1280]{1,0:T(8,128)S(1)} %add_add_fusion.1), channel_id=1, source_target_pairs={{0,48},{16,0},{32,16},{48,32},{1,49},{17,1},{33,17},{49,33},{2,50}... | collective-permute-start | bytes 122888 | tf_op jit(solution)/shard_map/ppermute | solution.py:69
  136.1 1.7 %collective-permute-done.18 = f32[8,1280]{1,0:T(8,128)S(1)} collective-permute-done((f32[8,1280]{1,0:T(8,128)S(1)}, f32[8,1280]{1,0:T(8,128)S(1)}, u32[]{:S(2)}, u32[]{:S(2)}) %collective-permute-start.18) | collective-permute-done | bytes 40992 | tf_op jit(solution)/shard_map/ppermute | solution.py:69
  137.8 0.1 collective-permute-done.19
  137.9 0.8 broadcast_in_dim.15
  138.7 3.6 %all-to-all-start.2 = ((f32[8,8,1280]{2,1,0:T(8,128)}), f32[8,8,1280]{2,1,0:T(8,128)S(1)}, u32[]{:S(2)}, u32[]{:S(2)}) async-start(f32[8,8,1280]{2,1,0:T(8,128)} %broadcast_in_dim.15), calls=%async_computation.2 | async-start | bytes 655360 | tf_op jit(solution)/shard_map/all_to_all | solution.py:81
  142.3 1.8 %fusion.16 = f32[256,1280]{1,0:T(8,128)} fusion(f32[32,256]{1,0:T(8,128)S(1)} %get-tuple-element.36, f32[16,1280]{1,0:T(8,128)S(1)} %bitcast.35, f32[16,1280]{1,0:T(8,128)S(1)} %get-tuple-element.37), kind=kOutput, calls=%fused_computation.28 | convolution fusion | flops 62955520 | bytes 1507328 | tf_op jit(solution)/shard_map/kp,kd->pd/dot_general | solution.py:215
  144.1 5.5 %all-to-all-done.2 = f32[8,8,1280]{2,1,0:T(8,128)S(1)} async-done(((f32[8,8,1280]{2,1,0:T(8,128)}), f32[8,8,1280]{2,1,0:T(8,128)S(1)}, u32[]{:S(2)}, u32[]{:S(2)}) %all-to-all-start.2) | async-done | bytes 327712 | tf_op jit(solution)/shard_map/all_to_all | solution.py:81
  149.6 5.4 %collective-permute-start.21 = (f32[8,1280]{1,0:T(8,128)S(1)}, f32[8,1280]{1,0:T(8,128)S(1)}, u32[]{:S(2)}, u32[]{:S(2)}) collective-permute-start(f32[8,1280]{1,0:T(8,128)S(1)} %reduce_sum.9), channel_id=1, source_target_pairs={{0,1},{1,0},{2,3},{3,2},{4,5},{5,4},{6,7},{7,6},{8,9},{9,8},{10,11... | collective-permute-start | bytes 122888 | tf_op jit(solution)/shard_map/ppermute | solution.py:83
  155.1 0.9 collective-permute-done.21
  156.0 0.6 fusion.21
  (47 shorter events, 0.6 us)
Async XLA Ops:
  0.6 62.5 %copy-start = (f32[1,320,1280]{2,1,0:T(8,128)S(1)}, f32[1,320,1280]{2,1,0:T(8,128)}, u32[]{:S(2)}) copy-start(f32[1,320,1280]{2,1,0:T(8,128)} %param.8) | copy-start | bytes 4915204
  0.6 1.4 copy-start.1
  2.1 1.3 copy-start.3
  3.4 0.9 copy-start.5
  40.6 10.3 %collective-permute-start = (f32[64,1280]{1,0:T(8,128)S(1)}, f32[64,1280]{1,0:T(8,128)S(1)}, u32[]{:S(2)}, u32[]{:S(2)}) collective-permute-start(f32[64,1280]{1,0:T(8,128)S(1)} %get-tuple-element.57), channel_id=1, source_target_pairs={{0,16},{16,32},{32,48},{48,0},{1,17},{17,33},{33,49},{49,1},{2,18}... | collective-permute-start | bytes 983048 | tf_op jit(solution)/shard_map/ppermute | solution.py:21
  41.9 9.1 %collective-permute-start.1 = (f32[64,1280]{1,0:T(8,128)S(1)}, f32[64,1280]{1,0:T(8,128)S(1)}, u32[]{:S(2)}, u32[]{:S(2)}) collective-permute-start(f32[64,1280]{1,0:T(8,128)S(1)} %get-tuple-element.57), channel_id=1, source_target_pairs={{0,48},{16,0},{32,16},{48,32},{1,49},{17,1},{33,17},{49,33},{2,50}... | collective-permute-start | bytes 983048 | tf_op jit(solution)/shard_map/ppermute | solution.py:22
  43.5 14.4 %collective-permute-start.4 = (f32[64,1280]{1,0:T(8,128)S(1)}, f32[64,1280]{1,0:T(8,128)S(1)}, u32[]{:S(2)}, u32[]{:S(2)}) collective-permute-start(f32[64,1280]{1,0:T(8,128)S(1)} %get-tuple-element.54), channel_id=1, source_target_pairs={{0,16},{16,32},{32,48},{48,0},{1,17},{17,33},{33,49},{49,1},{2,18}... | collective-permute-start | bytes 983048 | tf_op jit(solution)/shard_map/ppermute | solution.py:21
  43.5 14.5 %collective-permute-start.5 = (f32[64,1280]{1,0:T(8,128)S(1)}, f32[64,1280]{1,0:T(8,128)S(1)}, u32[]{:S(2)}, u32[]{:S(2)}) collective-permute-start(f32[64,1280]{1,0:T(8,128)S(1)} %get-tuple-element.54), channel_id=1, source_target_pairs={{0,48},{16,0},{32,16},{48,32},{1,49},{17,1},{33,17},{49,33},{2,50}... | collective-permute-start | bytes 983048 | tf_op jit(solution)/shard_map/ppermute | solution.py:22
  50.9 10.5 %collective-permute-start.2 = (f32[32,1280]{1,0:T(8,128)S(1)}, f32[32,1280]{1,0:T(8,128)S(1)}, u32[]{:S(2)}, u32[]{:S(2)}) collective-permute-start(f32[32,1280]{1,0:T(8,128)S(1)} %slice.115), channel_id=1, source_target_pairs={{0,16},{16,32},{32,48},{48,0},{1,17},{17,33},{33,49},{49,1},{2,18}... | collective-permute-start | bytes 491528 | tf_op jit(solution)/shard_map/ppermute | solution.py:23
  51.0 10.4 %collective-permute-start.3 = (f32[32,1280]{1,0:T(8,128)S(1)}, f32[32,1280]{1,0:T(8,128)S(1)}, u32[]{:S(2)}, u32[]{:S(2)}) collective-permute-start(f32[32,1280]{1,0:T(8,128)S(1)} %slice.116), channel_id=1, source_target_pairs={{0,48},{16,0},{32,16},{48,32},{1,49},{17,1},{33,17},{49,33},{2,50}... | collective-permute-start | bytes 491528 | tf_op jit(solution)/shard_map/ppermute | solution.py:24
  57.9 9.7 %collective-permute-start.6 = (f32[32,1280]{1,0:T(8,128)S(1)}, f32[32,1280]{1,0:T(8,128)S(1)}, u32[]{:S(2)}, u32[]{:S(2)}) collective-permute-start(f32[32,1280]{1,0:T(8,128)S(1)} %slice.118), channel_id=1, source_target_pairs={{0,16},{16,32},{32,48},{48,0},{1,17},{17,33},{33,49},{49,1},{2,18}... | collective-permute-start | bytes 491528 | tf_op jit(solution)/shard_map/ppermute | solution.py:23
  58.0 9.5 %collective-permute-start.7 = (f32[32,1280]{1,0:T(8,128)S(1)}, f32[32,1280]{1,0:T(8,128)S(1)}, u32[]{:S(2)}, u32[]{:S(2)}) collective-permute-start(f32[32,1280]{1,0:T(8,128)S(1)} %slice.119), channel_id=1, source_target_pairs={{0,48},{16,0},{32,16},{48,32},{1,49},{17,1},{33,17},{49,33},{2,50}... | collective-permute-start | bytes 491528 | tf_op jit(solution)/shard_map/ppermute | solution.py:24
  60.8 1.4 copy-start.9
  64.5 8.4 %collective-permute-start.9 = (f32[64,1280]{1,0:T(8,128)S(1)}, f32[64,1280]{1,0:T(8,128)S(1)}, u32[]{:S(2)}, u32[]{:S(2)}) collective-permute-start(f32[64,1280]{1,0:T(8,128)S(1)} %pad_maximum_fusion.1), channel_id=1, source_target_pairs={{0,16},{16,32},{32,48},{48,0},{1,17},{17,33},{33,49},{49,1},{2,18}... | collective-permute-start | bytes 983048 | tf_op jit(solution)/shard_map/ppermute | solution.py:33
  65.0 8.0 %collective-permute-start.8 = (f32[64,1280]{1,0:T(8,128)S(1)}, f32[64,1280]{1,0:T(8,128)S(1)}, u32[]{:S(2)}, u32[]{:S(2)}) collective-permute-start(f32[64,1280]{1,0:T(8,128)S(1)} %pad_maximum_fusion), channel_id=1, source_target_pairs={{0,48},{16,0},{32,16},{48,32},{1,49},{17,1},{33,17},{49,33},{2,50}... | collective-permute-start | bytes 983048 | tf_op jit(solution)/shard_map/ppermute | solution.py:32
  67.6 1.1 copy-start.7
  68.7 12.3 %copy-start.10 = (f32[256,320]{0,1:T(8,128)}, f32[256,320]{0,1:T(8,128)S(1)}, u32[]{:S(2)}) copy-start(f32[256,320]{0,1:T(8,128)S(1)} %fusion.13) | copy-start | bytes 983044
  70.0 10.8 %collective-permute-start.11 = (f32[64,1280]{1,0:T(8,128)S(1)}, f32[64,1280]{1,0:T(8,128)S(1)}, u32[]{:S(2)}, u32[]{:S(2)}) collective-permute-start(f32[64,1280]{1,0:T(8,128)S(1)} %pad_maximum_fusion.3), channel_id=1, source_target_pairs={{0,16},{16,32},{32,48},{48,0},{1,17},{17,33},{33,49},{49,1},{2,18}... | collective-permute-start | bytes 983048 | tf_op jit(solution)/shard_map/ppermute | solution.py:33
  70.2 10.7 %collective-permute-start.10 = (f32[64,1280]{1,0:T(8,128)S(1)}, f32[64,1280]{1,0:T(8,128)S(1)}, u32[]{:S(2)}, u32[]{:S(2)}) collective-permute-start(f32[64,1280]{1,0:T(8,128)S(1)} %pad_maximum_fusion.2), channel_id=1, source_target_pairs={{0,48},{16,0},{32,16},{48,32},{1,49},{17,1},{33,17},{49,33},{2,50}... | collective-permute-start | bytes 983048 | tf_op jit(solution)/shard_map/ppermute | solution.py:32
  81.0 7.0 %collective-permute-start.12 = (f32[32,2560]{1,0:T(8,128)S(1)}, f32[32,2560]{1,0:T(8,128)S(1)}, u32[]{:S(2)}, u32[]{:S(2)}) collective-permute-start(f32[32,2560]{1,0:T(8,128)S(1)} %get-tuple-element.28), channel_id=1, source_target_pairs={{0,48},{16,0},{32,16},{48,32},{1,49},{17,1},{33,17},{49,33},{2,50}... | collective-permute-start | bytes 983048 | tf_op jit(solution)/shard_map/ppermute | solution.py:43
  83.6 7.6 %collective-permute-start.13 = (f32[32,2560]{1,0:T(8,128)S(1)}, f32[32,2560]{1,0:T(8,128)S(1)}, u32[]{:S(2)}, u32[]{:S(2)}) collective-permute-start(f32[32,2560]{1,0:T(8,128)S(1)} %get-tuple-element.29), channel_id=1, source_target_pairs={{0,16},{16,32},{32,48},{48,0},{1,17},{17,33},{33,49},{49,1},{2,18}... | collective-permute-start | bytes 983048 | tf_op jit(solution)/shard_map/ppermute | solution.py:43
  92.2 29.6 %all-to-all-start.1 = ((f32[64,1,2560]{2,1,0:T(1,128)}), f32[64,1,2560]{2,1,0:T(1,128)}, u32[]{:S(2)}, u32[]{:S(2)}) async-start(f32[64,1,2560]{2,1,0:T(1,128)} %join.1), calls=%async_computation.1 | async-start | bytes 1310720 | tf_op jit(solution)/shard_map/all_to_all | solution.py:210
  101.5 3.1 %copy-start.8 = (f32[256,1280]{1,0:T(8,128)S(1)}, f32[256,1280]{1,0:T(8,128)}, u32[]{:S(2)}) copy-start(f32[256,1280]{1,0:T(8,128)} %copy-done.7) | copy-start | bytes 3932164
  104.6 17.2 %copy-start.2 = (f32[1,256,1280]{2,1,0:T(8,128)S(1)}, f32[1,256,1280]{2,1,0:T(8,128)}, u32[]{:S(2)}) copy-start(f32[1,256,1280]{2,1,0:T(8,128)} %param.5) | copy-start | bytes 3932164
  121.8 1.3 copy-start.4
  126.2 16.1 %copy-start.6 = (f32[1280,16]{0,1:T(8,128)S(1)}, f32[1280,16]{0,1:T(8,128)}, u32[]{:S(2)}) copy-start(f32[1280,16]{0,1:T(8,128)} %param.6) | copy-start | bytes 245764
  126.2 1.4 collective-permute-start.14
  127.5 4.4 %collective-permute-start.15 = (f32[8,1280]{1,0:T(8,128)S(1)}, f32[8,1280]{1,0:T(8,128)S(1)}, u32[]{:S(2)}, u32[]{:S(2)}) collective-permute-start(f32[8,1280]{1,0:T(8,128)S(1)} %select_add_fusion), channel_id=1, source_target_pairs={{0,4},{2,6},{4,0},{6,2},{1,5},{3,7},{5,1},{7,3},{8,12},{10,14},{12... | collective-permute-start | bytes 122888 | tf_op jit(solution)/shard_map/ppermute | solution.py:69
  128.5 4.7 %collective-permute-start.16 = (f32[8,1280]{1,0:T(8,128)S(1)}, f32[8,1280]{1,0:T(8,128)S(1)}, u32[]{:S(2)}, u32[]{:S(2)}) collective-permute-start(f32[8,1280]{1,0:T(8,128)S(1)} %select_add_fusion), channel_id=1, source_target_pairs={{0,2},{2,4},{4,6},{6,0},{1,3},{3,5},{5,7},{7,1},{8,10},{10,12},{12... | collective-permute-start | bytes 122888 | tf_op jit(solution)/shard_map/ppermute | solution.py:69
  129.2 4.1 %collective-permute-start.17 = (f32[8,1280]{1,0:T(8,128)S(1)}, f32[8,1280]{1,0:T(8,128)S(1)}, u32[]{:S(2)}, u32[]{:S(2)}) collective-permute-start(f32[8,1280]{1,0:T(8,128)S(1)} %select_add_fusion), channel_id=1, source_target_pairs={{0,6},{2,0},{4,2},{6,4},{1,7},{3,1},{5,3},{7,5},{8,14},{10,8},{12,... | collective-permute-start | bytes 122888 | tf_op jit(solution)/shard_map/ppermute | solution.py:69
  133.2 4.5 %collective-permute-start.18 = (f32[8,1280]{1,0:T(8,128)S(1)}, f32[8,1280]{1,0:T(8,128)S(1)}, u32[]{:S(2)}, u32[]{:S(2)}) collective-permute-start(f32[8,1280]{1,0:T(8,128)S(1)} %add_add_fusion.1), channel_id=1, source_target_pairs={{0,32},{16,48},{32,0},{48,16},{1,33},{17,49},{33,1},{49,17},{2,34}... | collective-permute-start | bytes 122888 | tf_op jit(solution)/shard_map/ppermute | solution.py:69
  133.3 4.6 %collective-permute-start.19 = (f32[8,1280]{1,0:T(8,128)S(1)}, f32[8,1280]{1,0:T(8,128)S(1)}, u32[]{:S(2)}, u32[]{:S(2)}) collective-permute-start(f32[8,1280]{1,0:T(8,128)S(1)} %add_add_fusion.1), channel_id=1, source_target_pairs={{0,16},{16,32},{32,48},{48,0},{1,17},{17,33},{33,49},{49,1},{2,18}... | collective-permute-start | bytes 122888 | tf_op jit(solution)/shard_map/ppermute | solution.py:69
  133.9 4.0 %collective-permute-start.20 = (f32[8,1280]{1,0:T(8,128)S(1)}, f32[8,1280]{1,0:T(8,128)S(1)}, u32[]{:S(2)}, u32[]{:S(2)}) collective-permute-start(f32[8,1280]{1,0:T(8,128)S(1)} %add_add_fusion.1), channel_id=1, source_target_pairs={{0,48},{16,0},{32,16},{48,32},{1,49},{17,1},{33,17},{49,33},{2,50}... | collective-permute-start | bytes 122888 | tf_op jit(solution)/shard_map/ppermute | solution.py:69
  138.7 10.9 %all-to-all-start.2 = ((f32[8,8,1280]{2,1,0:T(8,128)}), f32[8,8,1280]{2,1,0:T(8,128)S(1)}, u32[]{:S(2)}, u32[]{:S(2)}) async-start(f32[8,8,1280]{2,1,0:T(8,128)} %broadcast_in_dim.15), calls=%async_computation.2 | async-start | bytes 655360 | tf_op jit(solution)/shard_map/all_to_all | solution.py:81
  149.6 6.3 %collective-permute-start.21 = (f32[8,1280]{1,0:T(8,128)S(1)}, f32[8,1280]{1,0:T(8,128)S(1)}, u32[]{:S(2)}, u32[]{:S(2)}) collective-permute-start(f32[8,1280]{1,0:T(8,128)S(1)} %reduce_sum.9), channel_id=1, source_target_pairs={{0,1},{1,0},{2,3},{3,2},{4,5},{5,4},{6,7},{7,6},{8,9},{9,8},{10,11... | collective-permute-start | bytes 122888 | tf_op jit(solution)/shard_map/ppermute | solution.py:83

commit v6 on v5

--- a/solution.py
+++ b/solution.py
@@ -76,7 +76,7 @@
     half = local.shape[0] // 2
     low, top = local[:half], local[half:]
     mine = jnp.where(first, low, top) + lax.ppermute(jnp.where(first, top, low), "c", swap)
-    mine = sum_axis(sum_axis(mine, "x"), "y")
+    mine = sum_axis(sum_axis(mine, "y"), "x")
     pieces = jnp.broadcast_to(mine[None], (8,) + mine.shape)
     mine = jnp.sum(lax.all_to_all(pieces, ("zl", "zh"), 0, 0, tiled=True), axis=0)
     mine, beside = lax.optimization_barrier((mine, beside))

time: 157 us -> 157 us (level)
  no operation moved by 1% of the time
where the time goes in v6:
time: 157 us; the launch traced here: 156 us
  waiting for transfers between devices  51.3 us (33%)
  starting transfers between devices  44.6 us (28%)
  blocking collectives  33.1 us (21%)
  matrix products  11.4 us (7%)
  Pallas kernels  7.03 us (4%)
  local copies, waits for them, and re-layouts  7 us (4%)
    all_to_all x1, blocking collectives, on_device(): lax.all_to_all(sent, ZEX, 0, 0, tiled=True).reshape(4 * n_exp, 2 * width)  33.1 us
    all_to_all x1, waiting for transfers between devices, on_device(): back = lax.all_to_all(summed, ZEX, 0, 0, tiled=True)  15.1 us
    all_to_all x1, starting transfers between devices, on_device(): back = lax.all_to_all(summed, ZEX, 0, 0, tiled=True)  9.27 us
    ppermute x2, waiting for transfers between devices, gather_y(): from_below = lax.ppermute(block, 'y', UP)  8.89 us
    ppermute x2, waiting for transfers between devices, send_first(): up = lax.ppermute(jnp.concatenate([above[:half], far[half:]]), 'y', UP)  7.97 us
    ppermute x2, waiting for transfers between devices, scatter_both(): low, top = (lax.ppermute(low, 'y', DOWN), lax.ppermute(top, 'y', UP))  7.58 us
    ppermute x6, starting transfers between devices, sum_axis(): lax.ppermute(block, axis, [(i, (i + k) % 4) for i in range(4)])  6.83 us
    unnamed x29, local copies, waits for them, and re-layouts  5.97 us
  transfers between devices with their start and end apart: 24, of which 14 were waited for; matrix products, arithmetic and copies ran while one was open for 8% of the time, Pallas kernels for 0%

profile of v6, /device:TPU:1, one launch (start us, length us, event | category | flops | bytes accessed | tf_op | source)
XLA Modules:
  0.0 156.4 jit_solution(6990552208490324103)
XLA Ops:
  0.6 0.0 copy-start
  0.6 0.0 copy-start.1
  0.7 1.4 copy-done.1
  2.1 1.3 copy-done.3
  3.4 0.9 copy-done.5
  4.3 3.0 %route.1 = (f32[64,1,2560]{2,1,0:T(1,128)S(1)}, f32[16,256]{1,0:T(8,128)S(1)}, f32[16,256]{1,0:T(8,128)S(1)}) custom-call(f32[256,1280]{1,0:T(8,128)S(1)} %bitcast.30, f32[256,1280]{1,0:T(8,128)S(1)} %bitcast.32, f32[16,1280]{1,0:T(8,128)S(1)} %bitcast.34), custom_call_target="tpu_custom_call" | custom-call | tf_op jit(solution)/shard_map/route/pallas_call | solution.py:134
  7.3 33.1 %all_to_all.15 = f32[64,1,2560]{2,1,0:T(1,128)S(1)} all-to-all(f32[64,1,2560]{2,1,0:T(1,128)S(1)} %get-tuple-element.23), channel_id=1, replica_groups=mesh['zl'=4,'y'=4,'zh'=2,'x'=4,'c'=2] {'zl','zh','x','c'}, dimensions={0} | all-to-all | bytes 1310720 | tf_op jit(solution)/shard_map/all_to_all | solution.py:198
  40.5 0.1 fusion.33
  40.6 1.4 collective-permute-start
  41.9 1.5 collective-permute-start.1
  43.5 0.0 collective-permute-start.4
  43.5 2.7 %collective-permute-start.5 = (f32[64,1280]{1,0:T(8,128)S(1)}, f32[64,1280]{1,0:T(8,128)S(1)}, u32[]{:S(2)}, u32[]{:S(2)}) collective-permute-start(f32[64,1280]{1,0:T(8,128)S(1)} %get-tuple-element.54), channel_id=1, source_target_pairs={{0,48},{16,0},{32,16},{48,32},{1,49},{17,1},{33,17},{49,33},{2,50}... | collective-permute-start | bytes 983048 | tf_op jit(solution)/shard_map/ppermute | solution.py:22
  46.1 4.7 %collective-permute-done = f32[64,1280]{1,0:T(8,128)S(1)} collective-permute-done((f32[64,1280]{1,0:T(8,128)S(1)}, f32[64,1280]{1,0:T(8,128)S(1)}, u32[]{:S(2)}, u32[]{:S(2)}) %collective-permute-start) | collective-permute-done | bytes 327712 | tf_op jit(solution)/shard_map/ppermute | solution.py:21
  50.9 0.1 collective-permute-start.2
  51.0 0.0 collective-permute-done.1
  51.0 2.7 %collective-permute-start.3 = (f32[32,1280]{1,0:T(8,128)S(1)}, f32[32,1280]{1,0:T(8,128)S(1)}, u32[]{:S(2)}, u32[]{:S(2)}) collective-permute-start(f32[32,1280]{1,0:T(8,128)S(1)} %slice.116), channel_id=1, source_target_pairs={{0,48},{16,0},{32,16},{48,32},{1,49},{17,1},{33,17},{49,33},{2,50}... | collective-permute-start | bytes 491528 | tf_op jit(solution)/shard_map/ppermute | solution.py:24
  53.7 4.2 %collective-permute-done.4 = f32[64,1280]{1,0:T(8,128)S(1)} collective-permute-done((f32[64,1280]{1,0:T(8,128)S(1)}, f32[64,1280]{1,0:T(8,128)S(1)}, u32[]{:S(2)}, u32[]{:S(2)}) %collective-permute-start.4) | collective-permute-done | bytes 327712 | tf_op jit(solution)/shard_map/ppermute | solution.py:21
  57.9 0.1 collective-permute-start.6
  58.0 2.7 %collective-permute-start.7 = (f32[32,1280]{1,0:T(8,128)S(1)}, f32[32,1280]{1,0:T(8,128)S(1)}, u32[]{:S(2)}, u32[]{:S(2)}) collective-permute-start(f32[32,1280]{1,0:T(8,128)S(1)} %slice.119), channel_id=1, source_target_pairs={{0,48},{16,0},{32,16},{48,32},{1,49},{17,1},{33,17},{49,33},{2,50}... | collective-permute-start | bytes 491528 | tf_op jit(solution)/shard_map/ppermute | solution.py:24
  60.8 0.0 copy-start.9
  60.9 0.5 collective-permute-done.2
  61.5 0.8 copy-done.9
  62.2 0.9 fusion.6
  63.1 1.3 fusion.2.out
  64.5 0.4 collective-permute-start.9
  65.0 2.6 %collective-permute-start.8 = (f32[64,1280]{1,0:T(8,128)S(1)}, f32[64,1280]{1,0:T(8,128)S(1)}, u32[]{:S(2)}, u32[]{:S(2)}) collective-permute-start(f32[64,1280]{1,0:T(8,128)S(1)} %pad_maximum_fusion), channel_id=1, source_target_pairs={{0,48},{16,0},{32,16},{48,32},{1,49},{17,1},{33,17},{49,33},{2,50}... | collective-permute-start | bytes 983048 | tf_op jit(solution)/shard_map/ppermute | solution.py:32
  67.6 0.0 copy-start.7
  67.6 1.0 fusion.13
  68.6 0.1 copy-done.7
  68.7 1.3 fusion.4.grad
  70.0 0.1 collective-permute-start.11
  70.2 2.7 %collective-permute-start.10 = (f32[64,1280]{1,0:T(8,128)S(1)}, f32[64,1280]{1,0:T(8,128)S(1)}, u32[]{:S(2)}, u32[]{:S(2)}) collective-permute-start(f32[64,1280]{1,0:T(8,128)S(1)} %pad_maximum_fusion.2), channel_id=1, source_target_pairs={{0,48},{16,0},{32,16},{48,32},{1,49},{17,1},{33,17},{49,33},{2,50}... | collective-permute-start | bytes 983048 | tf_op jit(solution)/shard_map/ppermute | solution.py:32
  72.9 8.0 %collective-permute-done.11.up_g = f32[64,1280]{1,0:T(8,128)S(1)} collective-permute-done((f32[64,1280]{1,0:T(8,128)S(1)}, f32[64,1280]{1,0:T(8,128)S(1)}, u32[]{:S(2)}, u32[]{:S(2)}) %collective-permute-start.11) | collective-permute-done | bytes 327712 | tf_op jit(solution)/shard_map/ppermute | solution.py:33
  81.0 2.6 %collective-permute-start.12 = (f32[32,2560]{1,0:T(8,128)S(1)}, f32[32,2560]{1,0:T(8,128)S(1)}, u32[]{:S(2)}, u32[]{:S(2)}) collective-permute-start(f32[32,2560]{1,0:T(8,128)S(1)} %get-tuple-element.28), channel_id=1, source_target_pairs={{0,48},{16,0},{32,16},{48,32},{1,49},{17,1},{33,17},{49,33},{2,50}... | collective-permute-start | bytes 983048 | tf_op jit(solution)/shard_map/ppermute | solution.py:43
  83.6 4.4 %collective-permute-done.12.low = f32[32,2560]{1,0:T(8,128)S(1)} collective-permute-done((f32[32,2560]{1,0:T(8,128)S(1)}, f32[32,2560]{1,0:T(8,128)S(1)}, u32[]{:S(2)}, u32[]{:S(2)}) %collective-permute-start.12) | collective-permute-done | bytes 327712 | tf_op jit(solution)/shard_map/ppermute | solution.py:43
  88.0 3.1 %collective-permute-done.13.top = f32[32,2560]{1,0:T(8,128)S(1)} collective-permute-done((f32[32,2560]{1,0:T(8,128)S(1)}, f32[32,2560]{1,0:T(8,128)S(1)}, u32[]{:S(2)}, u32[]{:S(2)}) %collective-permute-start.13) | collective-permute-done | bytes 327712 | tf_op jit(solution)/shard_map/ppermute | solution.py:43
  91.2 1.1 join.1
  92.2 9.3 %all-to-all-start.1 = ((f32[64,1,2560]{2,1,0:T(1,128)}), f32[64,1,2560]{2,1,0:T(1,128)}, u32[]{:S(2)}, u32[]{:S(2)}) async-start(f32[64,1,2560]{2,1,0:T(1,128)} %join.1), calls=%async_computation.1 | async-start | bytes 1310720 | tf_op jit(solution)/shard_map/all_to_all | solution.py:210
  101.5 0.0 copy-start.8
  101.5 3.1 %fusion.34 = f32[1280,320]{0,1:T(8,128)} fusion(f32[256,1280]{1,0:T(8,128)S(1)} %constant_dynamic-update-slice_fusion, f32[256,320]{0,1:T(8,128)} %copy-done.10), kind=kOutput, calls=%fused_computation.61 | convolution fusion | flops 629145600 | bytes 3276800 | tf_op jit(solution)/shard_map/rd,rh->dh/dot_general | solution.py:209
  104.6 2.1 %fusion.20 = f32[320,1280]{1,0:T(8,128)} fusion(f32[256,1280]{1,0:T(8,128)S(1)} %copy-done.8, f32[256,320]{0,1:T(8,128)S(1)} %fusion.6), kind=kOutput, calls=%fused_computation.32 | convolution fusion | flops 629800960 | bytes 3276800 | tf_op jit(solution)/shard_map/rh,rd->hd/dot_general | solution.py:208
  106.7 15.1 %all-to-all-done.1.back_hbm = f32[64,1,2560]{2,1,0:T(1,128)} async-done(((f32[64,1,2560]{2,1,0:T(1,128)}), f32[64,1,2560]{2,1,0:T(1,128)}, u32[]{:S(2)}, u32[]{:S(2)}) %all-to-all-start.1) | async-done | bytes 655392 | tf_op jit(solution)/shard_map/all_to_all | solution.py:210
  121.8 1.3 copy-done.4
  123.1 3.0 %finish.1 = (f32[16,1280]{1,0:T(8,128)S(1)}, f32[32,256]{1,0:T(8,128)S(1)}, f32[16,1280]{1,0:T(8,128)S(1)}) custom-call(f32[64,1,2560]{2,1,0:T(1,128)} %all-to-all-done.1.back_hbm, f32[256,1280]{1,0:T(8,128)S(1)} %bitcast.31, f32[256,1280]{1,0:T(8,128)S(1)} %bitcast.33, f32[16,256]{1,0:T(8,128)S(1)} %get-tuple-element.33.dispatch_ref, ...), custom_call_target="tpu_custom_call" | custom-call | tf_op jit(solution)/shard_map/finish/pallas_call | solution.py:177
  126.2 0.0 copy-start.6
  126.2 0.5 collective-permute-start.14
  126.7 0.9 collective-permute-done.14
  127.5 0.1 collective-permute-start.15
  127.7 0.6 collective-permute-start.16
  128.2 2.4 %collective-permute-start.17 = (f32[8,1280]{1,0:T(8,128)S(1)}, f32[8,1280]{1,0:T(8,128)S(1)}, u32[]{:S(2)}, u32[]{:S(2)}) collective-permute-start(f32[8,1280]{1,0:T(8,128)S(1)} %select_add_fusion), channel_id=1, source_target_pairs={{0,48},{16,0},{32,16},{48,32},{1,49},{17,1},{33,17},{49,33},{2,50}... | collective-permute-start | bytes 122888 | tf_op jit(solution)/shard_map/ppermute | solution.py:69
  130.6 1.4 collective-permute-done.15
  132.0 1.2 collective-permute-done.16
  133.3 1.1 collective-permute-start.18
  134.4 0.5 collective-permute-start.19
  134.9 2.2 %collective-permute-start.20 = (f32[8,1280]{1,0:T(8,128)S(1)}, f32[8,1280]{1,0:T(8,128)S(1)}, u32[]{:S(2)}, u32[]{:S(2)}) collective-permute-start(f32[8,1280]{1,0:T(8,128)S(1)} %add_add_fusion.1), channel_id=1, source_target_pairs={{0,6},{2,0},{4,2},{6,4},{1,7},{3,1},{5,3},{7,5},{8,14},{10,8},{12,... | collective-permute-start | bytes 122888 | tf_op jit(solution)/shard_map/ppermute | solution.py:69
  137.0 0.7 collective-permute-done.18
  137.7 0.7 collective-permute-done.19
  138.5 0.8 broadcast_in_dim.15
  139.2 4.2 %all-to-all-start.2 = ((f32[8,8,1280]{2,1,0:T(8,128)}), f32[8,8,1280]{2,1,0:T(8,128)S(1)}, u32[]{:S(2)}, u32[]{:S(2)}) async-start(f32[8,8,1280]{2,1,0:T(8,128)} %broadcast_in_dim.15), calls=%async_computation.2 | async-start | bytes 655360 | tf_op jit(solution)/shard_map/all_to_all | solution.py:81
  143.5 1.8 %fusion.16 = f32[256,1280]{1,0:T(8,128)} fusion(f32[32,256]{1,0:T(8,128)S(1)} %get-tuple-element.36, f32[16,1280]{1,0:T(8,128)S(1)} %bitcast.35, f32[16,1280]{1,0:T(8,128)S(1)} %get-tuple-element.37), kind=kOutput, calls=%fused_computation.28 | convolution fusion | flops 62955520 | bytes 1507328 | tf_op jit(solution)/shard_map/kp,kd->pd/dot_general | solution.py:215
  145.2 5.4 %all-to-all-done.2 = f32[8,8,1280]{2,1,0:T(8,128)S(1)} async-done(((f32[8,8,1280]{2,1,0:T(8,128)}), f32[8,8,1280]{2,1,0:T(8,128)S(1)}, u32[]{:S(2)}, u32[]{:S(2)}) %all-to-all-start.2) | async-done | bytes 327712 | tf_op jit(solution)/shard_map/all_to_all | solution.py:81
  150.7 4.2 %collective-permute-start.21 = (f32[8,1280]{1,0:T(8,128)S(1)}, f32[8,1280]{1,0:T(8,128)S(1)}, u32[]{:S(2)}, u32[]{:S(2)}) collective-permute-start(f32[8,1280]{1,0:T(8,128)S(1)} %reduce_sum.9), channel_id=1, source_target_pairs={{0,1},{1,0},{2,3},{3,2},{4,5},{5,4},{6,7},{7,6},{8,9},{9,8},{10,11... | collective-permute-start | bytes 122888 | tf_op jit(solution)/shard_map/ppermute | solution.py:83
  154.9 0.9 collective-permute-done.21
  155.8 0.6 fusion.21
  (47 shorter events, 0.6 us)
Async XLA Ops:
  0.6 62.5 %copy-start = (f32[1,320,1280]{2,1,0:T(8,128)S(1)}, f32[1,320,1280]{2,1,0:T(8,128)}, u32[]{:S(2)}) copy-start(f32[1,320,1280]{2,1,0:T(8,128)} %param.8) | copy-start | bytes 4915204
  0.6 1.4 copy-start.1
  2.1 1.3 copy-start.3
  3.4 0.9 copy-start.5
  40.6 10.3 %collective-permute-start = (f32[64,1280]{1,0:T(8,128)S(1)}, f32[64,1280]{1,0:T(8,128)S(1)}, u32[]{:S(2)}, u32[]{:S(2)}) collective-permute-start(f32[64,1280]{1,0:T(8,128)S(1)} %get-tuple-element.57), channel_id=1, source_target_pairs={{0,16},{16,32},{32,48},{48,0},{1,17},{17,33},{33,49},{49,1},{2,18}... | collective-permute-start | bytes 983048 | tf_op jit(solution)/shard_map/ppermute | solution.py:21
  41.9 9.1 %collective-permute-start.1 = (f32[64,1280]{1,0:T(8,128)S(1)}, f32[64,1280]{1,0:T(8,128)S(1)}, u32[]{:S(2)}, u32[]{:S(2)}) collective-permute-start(f32[64,1280]{1,0:T(8,128)S(1)} %get-tuple-element.57), channel_id=1, source_target_pairs={{0,48},{16,0},{32,16},{48,32},{1,49},{17,1},{33,17},{49,33},{2,50}... | collective-permute-start | bytes 983048 | tf_op jit(solution)/shard_map/ppermute | solution.py:22
  43.5 14.4 %collective-permute-start.4 = (f32[64,1280]{1,0:T(8,128)S(1)}, f32[64,1280]{1,0:T(8,128)S(1)}, u32[]{:S(2)}, u32[]{:S(2)}) collective-permute-start(f32[64,1280]{1,0:T(8,128)S(1)} %get-tuple-element.54), channel_id=1, source_target_pairs={{0,16},{16,32},{32,48},{48,0},{1,17},{17,33},{33,49},{49,1},{2,18}... | collective-permute-start | bytes 983048 | tf_op jit(solution)/shard_map/ppermute | solution.py:21
  43.5 14.5 %collective-permute-start.5 = (f32[64,1280]{1,0:T(8,128)S(1)}, f32[64,1280]{1,0:T(8,128)S(1)}, u32[]{:S(2)}, u32[]{:S(2)}) collective-permute-start(f32[64,1280]{1,0:T(8,128)S(1)} %get-tuple-element.54), channel_id=1, source_target_pairs={{0,48},{16,0},{32,16},{48,32},{1,49},{17,1},{33,17},{49,33},{2,50}... | collective-permute-start | bytes 983048 | tf_op jit(solution)/shard_map/ppermute | solution.py:22
  50.9 10.5 %collective-permute-start.2 = (f32[32,1280]{1,0:T(8,128)S(1)}, f32[32,1280]{1,0:T(8,128)S(1)}, u32[]{:S(2)}, u32[]{:S(2)}) collective-permute-start(f32[32,1280]{1,0:T(8,128)S(1)} %slice.115), channel_id=1, source_target_pairs={{0,16},{16,32},{32,48},{48,0},{1,17},{17,33},{33,49},{49,1},{2,18}... | collective-permute-start | bytes 491528 | tf_op jit(solution)/shard_map/ppermute | solution.py:23
  51.0 10.4 %collective-permute-start.3 = (f32[32,1280]{1,0:T(8,128)S(1)}, f32[32,1280]{1,0:T(8,128)S(1)}, u32[]{:S(2)}, u32[]{:S(2)}) collective-permute-start(f32[32,1280]{1,0:T(8,128)S(1)} %slice.116), channel_id=1, source_target_pairs={{0,48},{16,0},{32,16},{48,32},{1,49},{17,1},{33,17},{49,33},{2,50}... | collective-permute-start | bytes 491528 | tf_op jit(solution)/shard_map/ppermute | solution.py:24
  57.9 9.7 %collective-permute-start.6 = (f32[32,1280]{1,0:T(8,128)S(1)}, f32[32,1280]{1,0:T(8,128)S(1)}, u32[]{:S(2)}, u32[]{:S(2)}) collective-permute-start(f32[32,1280]{1,0:T(8,128)S(1)} %slice.118), channel_id=1, source_target_pairs={{0,16},{16,32},{32,48},{48,0},{1,17},{17,33},{33,49},{49,1},{2,18}... | collective-permute-start | bytes 491528 | tf_op jit(solution)/shard_map/ppermute | solution.py:23
  58.0 9.5 %collective-permute-start.7 = (f32[32,1280]{1,0:T(8,128)S(1)}, f32[32,1280]{1,0:T(8,128)S(1)}, u32[]{:S(2)}, u32[]{:S(2)}) collective-permute-start(f32[32,1280]{1,0:T(8,128)S(1)} %slice.119), channel_id=1, source_target_pairs={{0,48},{16,0},{32,16},{48,32},{1,49},{17,1},{33,17},{49,33},{2,50}... | collective-permute-start | bytes 491528 | tf_op jit(solution)/shard_map/ppermute | solution.py:24
  60.8 1.4 copy-start.9
  64.5 8.4 %collective-permute-start.9 = (f32[64,1280]{1,0:T(8,128)S(1)}, f32[64,1280]{1,0:T(8,128)S(1)}, u32[]{:S(2)}, u32[]{:S(2)}) collective-permute-start(f32[64,1280]{1,0:T(8,128)S(1)} %pad_maximum_fusion.1), channel_id=1, source_target_pairs={{0,16},{16,32},{32,48},{48,0},{1,17},{17,33},{33,49},{49,1},{2,18}... | collective-permute-start | bytes 983048 | tf_op jit(solution)/shard_map/ppermute | solution.py:33
  65.0 8.0 %collective-permute-start.8 = (f32[64,1280]{1,0:T(8,128)S(1)}, f32[64,1280]{1,0:T(8,128)S(1)}, u32[]{:S(2)}, u32[]{:S(2)}) collective-permute-start(f32[64,1280]{1,0:T(8,128)S(1)} %pad_maximum_fusion), channel_id=1, source_target_pairs={{0,48},{16,0},{32,16},{48,32},{1,49},{17,1},{33,17},{49,33},{2,50}... | collective-permute-start | bytes 983048 | tf_op jit(solution)/shard_map/ppermute | solution.py:32
  67.6 1.1 copy-start.7
  68.7 12.3 %copy-start.10 = (f32[256,320]{0,1:T(8,128)}, f32[256,320]{0,1:T(8,128)S(1)}, u32[]{:S(2)}) copy-start(f32[256,320]{0,1:T(8,128)S(1)} %fusion.13) | copy-start | bytes 983044
  70.0 10.8 %collective-permute-start.11 = (f32[64,1280]{1,0:T(8,128)S(1)}, f32[64,1280]{1,0:T(8,128)S(1)}, u32[]{:S(2)}, u32[]{:S(2)}) collective-permute-start(f32[64,1280]{1,0:T(8,128)S(1)} %pad_maximum_fusion.3), channel_id=1, source_target_pairs={{0,16},{16,32},{32,48},{48,0},{1,17},{17,33},{33,49},{49,1},{2,18}... | collective-permute-start | bytes 983048 | tf_op jit(solution)/shard_map/ppermute | solution.py:33
  70.2 10.7 %collective-permute-start.10 = (f32[64,1280]{1,0:T(8,128)S(1)}, f32[64,1280]{1,0:T(8,128)S(1)}, u32[]{:S(2)}, u32[]{:S(2)}) collective-permute-start(f32[64,1280]{1,0:T(8,128)S(1)} %pad_maximum_fusion.2), channel_id=1, source_target_pairs={{0,48},{16,0},{32,16},{48,32},{1,49},{17,1},{33,17},{49,33},{2,50}... | collective-permute-start | bytes 983048 | tf_op jit(solution)/shard_map/ppermute | solution.py:32
  81.0 7.0 %collective-permute-start.12 = (f32[32,2560]{1,0:T(8,128)S(1)}, f32[32,2560]{1,0:T(8,128)S(1)}, u32[]{:S(2)}, u32[]{:S(2)}) collective-permute-start(f32[32,2560]{1,0:T(8,128)S(1)} %get-tuple-element.28), channel_id=1, source_target_pairs={{0,48},{16,0},{32,16},{48,32},{1,49},{17,1},{33,17},{49,33},{2,50}... | collective-permute-start | bytes 983048 | tf_op jit(solution)/shard_map/ppermute | solution.py:43
  83.6 7.6 %collective-permute-start.13 = (f32[32,2560]{1,0:T(8,128)S(1)}, f32[32,2560]{1,0:T(8,128)S(1)}, u32[]{:S(2)}, u32[]{:S(2)}) collective-permute-start(f32[32,2560]{1,0:T(8,128)S(1)} %get-tuple-element.29), channel_id=1, source_target_pairs={{0,16},{16,32},{32,48},{48,0},{1,17},{17,33},{33,49},{49,1},{2,18}... | collective-permute-start | bytes 983048 | tf_op jit(solution)/shard_map/ppermute | solution.py:43
  92.2 29.6 %all-to-all-start.1 = ((f32[64,1,2560]{2,1,0:T(1,128)}), f32[64,1,2560]{2,1,0:T(1,128)}, u32[]{:S(2)}, u32[]{:S(2)}) async-start(f32[64,1,2560]{2,1,0:T(1,128)} %join.1), calls=%async_computation.1 | async-start | bytes 1310720 | tf_op jit(solution)/shard_map/all_to_all | solution.py:210
  101.5 3.1 %copy-start.8 = (f32[256,1280]{1,0:T(8,128)S(1)}, f32[256,1280]{1,0:T(8,128)}, u32[]{:S(2)}) copy-start(f32[256,1280]{1,0:T(8,128)} %copy-done.7) | copy-start | bytes 3932164
  104.6 17.2 %copy-start.2 = (f32[1,256,1280]{2,1,0:T(8,128)S(1)}, f32[1,256,1280]{2,1,0:T(8,128)}, u32[]{:S(2)}) copy-start(f32[1,256,1280]{2,1,0:T(8,128)} %param.5) | copy-start | bytes 3932164
  121.8 1.3 copy-start.4
  126.2 17.3 %copy-start.6 = (f32[1280,16]{0,1:T(8,128)S(1)}, f32[1280,16]{0,1:T(8,128)}, u32[]{:S(2)}) copy-start(f32[1280,16]{0,1:T(8,128)} %param.6) | copy-start | bytes 245764
  126.2 1.4 collective-permute-start.14
  127.5 4.5 %collective-permute-start.15 = (f32[8,1280]{1,0:T(8,128)S(1)}, f32[8,1280]{1,0:T(8,128)S(1)}, u32[]{:S(2)}, u32[]{:S(2)}) collective-permute-start(f32[8,1280]{1,0:T(8,128)S(1)} %select_add_fusion), channel_id=1, source_target_pairs={{0,32},{16,48},{32,0},{48,16},{1,33},{17,49},{33,1},{49,17},{2,34}... | collective-permute-start | bytes 122888 | tf_op jit(solution)/shard_map/ppermute | solution.py:69
  127.7 5.6 %collective-permute-start.16 = (f32[8,1280]{1,0:T(8,128)S(1)}, f32[8,1280]{1,0:T(8,128)S(1)}, u32[]{:S(2)}, u32[]{:S(2)}) collective-permute-start(f32[8,1280]{1,0:T(8,128)S(1)} %select_add_fusion), channel_id=1, source_target_pairs={{0,16},{16,32},{32,48},{48,0},{1,17},{17,33},{33,49},{49,1},{2,18}... | collective-permute-start | bytes 122888 | tf_op jit(solution)/shard_map/ppermute | solution.py:69
  128.2 5.0 %collective-permute-start.17 = (f32[8,1280]{1,0:T(8,128)S(1)}, f32[8,1280]{1,0:T(8,128)S(1)}, u32[]{:S(2)}, u32[]{:S(2)}) collective-permute-start(f32[8,1280]{1,0:T(8,128)S(1)} %select_add_fusion), channel_id=1, source_target_pairs={{0,48},{16,0},{32,16},{48,32},{1,49},{17,1},{33,17},{49,33},{2,50}... | collective-permute-start | bytes 122888 | tf_op jit(solution)/shard_map/ppermute | solution.py:69
  133.3 4.4 %collective-permute-start.18 = (f32[8,1280]{1,0:T(8,128)S(1)}, f32[8,1280]{1,0:T(8,128)S(1)}, u32[]{:S(2)}, u32[]{:S(2)}) collective-permute-start(f32[8,1280]{1,0:T(8,128)S(1)} %add_add_fusion.1), channel_id=1, source_target_pairs={{0,4},{2,6},{4,0},{6,2},{1,5},{3,7},{5,1},{7,3},{8,12},{10,14},{12... | collective-permute-start | bytes 122888 | tf_op jit(solution)/shard_map/ppermute | solution.py:69
  134.4 4.1 %collective-permute-start.19 = (f32[8,1280]{1,0:T(8,128)S(1)}, f32[8,1280]{1,0:T(8,128)S(1)}, u32[]{:S(2)}, u32[]{:S(2)}) collective-permute-start(f32[8,1280]{1,0:T(8,128)S(1)} %add_add_fusion.1), channel_id=1, source_target_pairs={{0,2},{2,4},{4,6},{6,0},{1,3},{3,5},{5,7},{7,1},{8,10},{10,12},{12... | collective-permute-start | bytes 122888 | tf_op jit(solution)/shard_map/ppermute | solution.py:69
  134.9 3.6 %collective-permute-start.20 = (f32[8,1280]{1,0:T(8,128)S(1)}, f32[8,1280]{1,0:T(8,128)S(1)}, u32[]{:S(2)}, u32[]{:S(2)}) collective-permute-start(f32[8,1280]{1,0:T(8,128)S(1)} %add_add_fusion.1), channel_id=1, source_target_pairs={{0,6},{2,0},{4,2},{6,4},{1,7},{3,1},{5,3},{7,5},{8,14},{10,8},{12,... | collective-permute-start | bytes 122888 | tf_op jit(solution)/shard_map/ppermute | solution.py:69
  139.2 11.5 %all-to-all-start.2 = ((f32[8,8,1280]{2,1,0:T(8,128)}), f32[8,8,1280]{2,1,0:T(8,128)S(1)}, u32[]{:S(2)}, u32[]{:S(2)}) async-start(f32[8,8,1280]{2,1,0:T(8,128)} %broadcast_in_dim.15), calls=%async_computation.2 | async-start | bytes 655360 | tf_op jit(solution)/shard_map/all_to_all | solution.py:81
  150.7 5.1 %collective-permute-start.21 = (f32[8,1280]{1,0:T(8,128)S(1)}, f32[8,1280]{1,0:T(8,128)S(1)}, u32[]{:S(2)}, u32[]{:S(2)}) collective-permute-start(f32[8,1280]{1,0:T(8,128)S(1)} %reduce_sum.9), channel_id=1, source_target_pairs={{0,1},{1,0},{2,3},{3,2},{4,5},{5,4},{6,7},{7,6},{8,9},{9,8},{10,11... | collective-permute-start | bytes 122888 | tf_op jit(solution)/shard_map/ppermute | solution.py:83
